TPU v7x, 256 devices: a whole 4x4x8 slice. The times are simulated.
256 devices in a mesh: gx: 16 (over z, y_hi), gy: 8 (over x, core), gz: 2 (over y_lo).
Axes of the slice: x: 4, y: 4 (y_hi: 2, y_lo: 2; y = y_hi * 2 + y_lo), z: 8, core: 2. Of those that a mesh axis runs over, the one named last changes fastest.
Arguments:
- features: bfloat16 [128, 256, 32, 128], P('gx', 'gy', 'gz'), may hold values from 0 to 15
- active: int32 [128, 256, 64], P('gx', 'gy', 'gz'), may hold values from 0 to 1
- weight: bfloat16 [3, 3, 3, 64, 128], replicated, may hold values from -0.15625 to 0.15625
- gain: float32 [128], replicated, may hold values from 0.1 to 1.9
- bias: float32 [128], replicated, may hold values from -1 to 1
- cotangent: bfloat16 [64, 128, 32, 128], P('gx', 'gy', 'gz'), may hold values from -5 to 5
Outputs:
- section_out: bfloat16 [64, 128, 32, 128], P('gx', 'gy', 'gz')
- grad_features: bfloat16 [128, 256, 32, 128], P('gx', 'gy', 'gz')
- grad_weight: float32 [3, 3, 3, 64, 128], replicated
- gain_gradient: float32 [128], replicated
- shift_gradient: float32 [128], replicated
All inputs are finite; a program needn't handle non-finite values.
Results may differ from a plain program's by a relative error of at most 0.0049.
Values may be sent and summed in bfloat16 or wider, within the bound.
No kernel may reach another device: no remote copies, remote signals or barrier semaphores. Data moves between devices by JAX's collectives and lax.ppermute only.
A program may use at most 64 MiB of HBM per device.

v0:
```python
import jax
import jax.numpy as jnp
from jax import lax
from jax.sharding import PartitionSpec as P


def from_behind(value, axis, steps):
    count = lax.axis_size(axis)
    first, last = (max(0, -steps), min(count, count - steps))
    return lax.ppermute(value, axis, [(source, source + steps) for source in range(first, last)])


def extend(block, by, lower):
    rows = block.shape[0]
    face = block[rows - 1 : rows] if by == 1 else block[0:1]
    got = from_behind(face, "gx", by)
    block = (
        jnp.concatenate([got, block], axis=0) if by == 1 else jnp.concatenate([block, got], axis=0)
    )
    cols = block.shape[1]
    face = block[:, cols - 1 : cols] if by == 1 else block[:, 0:1]
    got = from_behind(face, "gy", by)
    block = (
        jnp.concatenate([got, block], axis=1) if by == 1 else jnp.concatenate([block, got], axis=1)
    )
    depth = block.shape[2]
    face = block[:, :, depth - 1 : depth, lower:] if by == 1 else block[:, :, 0:1, lower:]
    got = from_behind(face, "gz", by)
    return (block, got)


def weight_totals(partial_value, count):
    return lax.psum(partial_value, ("gx", "gy", "gz")) / count


def local(features, active, weight, gain, bias, cotangent):
    vx, vy, vzp, width = features.shape
    cin = width // 2
    cout = weight.shape[4]
    mx, my, mz = (vx // 2, vy // 2, vzp)
    pairmask = active.reshape(vx, vy, vzp, 2, 1).astype(jnp.bfloat16)
    xin = (features.reshape(vx, vy, vzp, 2, cin) * pairmask).reshape(vx, vy, vzp, width)
    extended, zplane = extend(xin, 1, cin)
    odd_prev = jnp.concatenate([zplane, extended[:, :, : vzp - 1, cin:]], axis=2)
    pair_w = jnp.concatenate([weight[:, :, 1], weight[:, :, 2]], axis=2)
    preactivation = jnp.zeros((mx, my, mz, cout), jnp.float32)
    for a in range(3):
        for b in range(3):
            pair_in = extended[a : a + 2 * mx : 2, b : b + 2 * my : 2]
            odd_in = odd_prev[a : a + 2 * mx : 2, b : b + 2 * my : 2]
            preactivation = preactivation + jnp.einsum(
                "xyzk,ko->xyzo", pair_in, pair_w[a, b], preferred_element_type=jnp.float32
            )
            preactivation = preactivation + jnp.einsum(
                "xyzk,ko->xyzo", odd_in, weight[a, b, 0], preferred_element_type=jnp.float32
            )
    voxel_mask4 = (
        active.reshape(mx, 2, my, 2, mz, 2).max(axis=(1, 3, 5)).astype(jnp.float32)[..., None]
    )
    count, total = lax.psum(
        (jnp.sum(voxel_mask4), jnp.sum(voxel_mask4 * preactivation, axis=(0, 1, 2))),
        ("gx", "gy", "gz"),
    )
    batch_mean = total / count
    spread = lax.psum(
        jnp.sum(voxel_mask4 * (preactivation - batch_mean) ** 2, axis=(0, 1, 2)), ("gx", "gy", "gz")
    )
    var = spread / count
    inverse_deviation = lax.rsqrt(var + 1e-05)
    standardized_input = (preactivation - batch_mean) * inverse_deviation
    normalized_output = standardized_input * gain + bias
    sig = jax.nn.sigmoid(normalized_output)
    section_out = (voxel_mask4 * normalized_output * sig).astype(jnp.bfloat16)
    silu_slope = (
        voxel_mask4 * cotangent.astype(jnp.float32) * sig * (1.0 + normalized_output * (1.0 - sig))
    )
    sum_slope, sum_prod = lax.psum(
        (
            jnp.sum(silu_slope, axis=(0, 1, 2)),
            jnp.sum(silu_slope * standardized_input, axis=(0, 1, 2)),
        ),
        ("gx", "gy", "gz"),
    )
    shift_gradient = sum_slope / count
    gain_gradient = sum_prod / count
    preactivation_gradient = (
        voxel_mask4
        * inverse_deviation
        * gain
        * (silu_slope - shift_gradient - standardized_input * gain_gradient)
    ).astype(jnp.bfloat16)
    dext, zrim = extend(preactivation_gradient, -1, 0)
    padded = jnp.concatenate([dext, zrim], axis=2)
    taps = (((1, 0),), ((2, 0), (0, 1)))
    rows = []
    for px in range(2):
        cols = []
        for py in range(2):
            accum = jnp.zeros((mx, my, mz, width), jnp.float32)
            odd = jnp.zeros((mx, my, mz, cin), jnp.float32)
            for input_a, sx in taps[px]:
                for input_b, sy in taps[py]:
                    here = padded[sx : sx + mx, sy : sy + my, :mz]
                    after = padded[sx : sx + mx, sy : sy + my, 1 : mz + 1]
                    accum = accum + jnp.einsum(
                        "xyzo,ko->xyzk",
                        here,
                        pair_w[input_a, input_b],
                        preferred_element_type=jnp.float32,
                    )
                    odd = odd + jnp.einsum(
                        "xyzo,ko->xyzk",
                        after,
                        weight[input_a, input_b, 0],
                        preferred_element_type=jnp.float32,
                    )
            accum = accum + jnp.concatenate([jnp.zeros_like(odd), odd], axis=3)
            cols.append(accum)
        rows.append(jnp.stack(cols, axis=2))
    whole = jnp.stack(rows, axis=1).reshape(vx, vy, vzp, 2, cin)
    grad_features = (whole * pairmask).reshape(vx, vy, vzp, width).astype(jnp.bfloat16)
    blocks = []
    for a in range(3):
        for b in range(3):
            pair_in = extended[a : a + 2 * mx : 2, b : b + 2 * my : 2]
            odd_in = odd_prev[a : a + 2 * mx : 2, b : b + 2 * my : 2]
            pair_grad = jnp.einsum(
                "xyzk,xyzo->ko", pair_in, preactivation_gradient, preferred_element_type=jnp.float32
            )
            odd_grad = jnp.einsum(
                "xyzk,xyzo->ko", odd_in, preactivation_gradient, preferred_element_type=jnp.float32
            )
            blocks.append(jnp.stack([odd_grad, pair_grad[:cin], pair_grad[cin:]]))
    grad_weight = weight_totals(jnp.stack(blocks).reshape(3, 3, 3, cin, cout), count)
    return (section_out, grad_features, grad_weight, gain_gradient, shift_gradient)


def solution(mesh):
    in_specs = (
        P("gx", "gy", "gz", None),
        P("gx", "gy", "gz"),
        P(),
        P(),
        P(),
        P("gx", "gy", "gz", None),
    )
    out_specs = (P("gx", "gy", "gz", None), P("gx", "gy", "gz", None), P(), P(), P())
    return jax.shard_map(local, mesh=mesh, in_specs=in_specs, out_specs=out_specs, check_vma=False)
```

profile of v0, /device:TPU:1, one launch (start us, length us, event | category | flops | bytes accessed | tf_op | source)
XLA Modules:
  0.0 586.1 jit_solution(8403148419269660471)
XLA Ops:
  9.4 1.9 reshape.52
  11.3 1.6 slice_multiply_fusion
  13.0 5.7 collective-permute-start
  18.7 6.7 %mul.108 = bf16[8,32,16,2,64]{4,3,2,1,0:T(2,128)(2,1)S(1)} broadcast(bf16[8,32,16,2]{3,2,1,0:T(8,128)(2,1)} %copy-done.3), dimensions={0,1,2,3} | broadcast | bytes 1064960 | tf_op jit(solution)/shard_map/mul | solution.py:42
  25.4 1.8 mul.110
  27.2 1.9 mul.111
  32.4 2.5 reshape.51
  34.9 2.2 copy.18
  37.1 2.7 reduce_max.9
  39.8 8.3 %mul.130 = f32[8,32,16,2,64]{4,3,2,1,0:T(2,128)} broadcast(f32[8,32,16,2]{3,2,1,0:T(8,128)} %copy.18), dimensions={0,1,2,3} | broadcast | bytes 2129920 | tf_op jit(solution)/shard_map/mul | solution.py:121
  48.1 5.4 mul.131
  54.1 4.0 collective-permute-start.1
  59.8 2.3 collective-permute-start.2
  62.8 1.9 collective-permute-done.2
  75.1 80.2 %all-reduce.5 = (f32[128]{0:T(128)S(1)}, f32[]{:T(128)}) all-reduce(f32[128]{0:T(128)S(1)} %get-tuple-element.33, f32[]{:T(128)} %convert_reduce_fusion), channel_id=1, replica_groups=mesh['gx'=16,'gy'=8,'gz'=2] {'gx','gy','gz'}, use_global_device_ids=true, to_apply=%region_2.0 | all-reduce | flops 129 | bytes 1032 | tf_op jit(solution)/shard_map/psum | solution.py:60
  156.2 73.4 %psum.44 = f32[128]{0:T(128)S(1)} all-reduce(f32[128]{0:T(128)S(1)} %multiply_reduce_fusion.1), channel_id=1, replica_groups=mesh['gx'=16,'gy'=8,'gz'=2] {'gx','gy','gz'}, use_global_device_ids=true, to_apply=%region_6.0 | all-reduce | flops 128 | bytes 1024 | tf_op jit(solution)/shard_map/psum | solution.py:65
  230.6 74.3 %all-reduce.4 = (f32[128]{0:T(128)S(1)}, f32[128]{0:T(128)S(1)}) all-reduce(f32[128]{0:T(128)S(1)} %get-tuple-element.6, f32[128]{0:T(128)S(1)} %get-tuple-element.5), channel_id=1, replica_groups=mesh['gx'=16,'gy'=8,'gz'=2] {'gx','gy','gz'}, use_global_device_ids=true, to_apply=%region_10.0 | all-reduce | flops 256 | bytes 2048 | tf_op jit(solution)/shard_map/psum | solution.py:77
  305.6 2.1 multiply_convert_fusion.1
  316.5 5.1 collective-permute-done.3
  321.6 3.7 collective-permute-start.4
  329.4 3.0 collective-permute-done.5
  342.5 1.3 copy-done.2
  345.1 231.4 %all-reduce.8.cloned.1.call-done = f32[3,3,3,64,128]{4,3,2,1,0:T(8,128)} async-done(((f32[3,3,3,64,128]{4,3,2,1,0:T(8,128)}), f32[3,3,3,64,128]{4,3,2,1,0:T(8,128)}) %all-reduce.8.cloned.1.call-update) | async-done | bytes 884752 | tf_op jit(solution)/shard_map/psum | solution.py:33
  576.5 2.8 broadcast_divide_fusion
  (141 shorter events, 45.1 us)
Async XLA Ops:
  7.2 2.2 copy-start.4
  7.2 569.3 %all-reduce.8.cloned.1.call-start = ((), (), s32[]{:S(2)}) async-start(), calls=%async_computation | async-start | bytes 1769472 | tf_op jit(solution)/shard_map/psum | solution.py:33
  9.4 1.9 copy-start.3
  13.0 41.1 %collective-permute-start = (bf16[1,32,16,128]{3,2,1,0:T(8,128)(2,1)S(1)}, bf16[1,32,16,128]{3,2,1,0:T(8,128)(2,1)S(1)}, u32[]{:S(2)}, u32[]{:S(2)}) collective-permute-start(bf16[1,32,16,128]{3,2,1,0:T(8,128)(2,1)S(1)} %slice.257), channel_id=1, source_target_pairs={{0,16},{16,32},{32,48},{48,64},{64,80},{80,96},{96,112},{112,128},... | collective-permute-start | bytes 393224 | tf_op jit(solution)/shard_map/ppermute | solution.py:10
  27.2 1.9 copy-start.11
  31.2 1.2 copy-start.12
  54.1 5.0 collective-permute-start.1
  58.2 1.1 copy-start.5
  59.3 10.7 %copy-start = (bf16[9,33,16,128]{3,2,1,0:T(8,128)(2,1)}, bf16[9,33,16,128]{3,2,1,0:T(8,128)(2,1)S(1)}, u32[]{:S(2)}) copy-start(bf16[9,33,16,128]{3,2,1,0:T(8,128)(2,1)S(1)} %maximum_maximum_fusion) | copy-start | bytes 3649540
  59.8 4.9 collective-permute-start.2
  67.2 2.8 copy-start.7
  70.0 1.0 copy-start.6
  71.0 1.1 copy-start.8
  74.0 156.2 %copy-start.10 = (bf16[4,16,16,128]{3,2,1,0:T(8,128)(2,1)S(1)}, bf16[4,16,16,128]{3,2,1,0:T(8,128)(2,1)}, u32[]{:S(2)}) copy-start(bf16[4,16,16,128]{3,2,1,0:T(8,128)(2,1)} %param.11) | copy-start | bytes 786436
  74.0 156.2 %copy-start.13 = (f32[128]{0:T(128)S(1)}, f32[128]{0:T(128)}, u32[]{:S(2)}) copy-start(f32[128]{0:T(128)} %param.10) | copy-start | bytes 1540
  74.0 156.2 %copy-start.14 = (f32[128]{0:T(128)S(1)}, f32[128]{0:T(128)}, u32[]{:S(2)}) copy-start(f32[128]{0:T(128)} %param.9) | copy-start | bytes 1540
  304.8 3.1 copy-start.1
  305.5 2.7 copy-start.15
  305.6 2.7 copy-start.16
  315.1 6.5 %collective-permute-start.3 = (bf16[1,16,16,128]{3,2,1,0:T(8,128)(2,1)S(1)}, bf16[1,16,16,128]{3,2,1,0:T(8,128)(2,1)S(1)}, u32[]{:S(2)}, u32[]{:S(2)}) collective-permute-start(bf16[1,16,16,128]{3,2,1,0:T(8,128)(2,1)S(1)} %slice.349), channel_id=1, source_target_pairs={{16,0},{32,16},{48,32},{64,48},{80,64},{96,80},{112,96},{128,112},... | collective-permute-start | bytes 196616 | tf_op jit(solution)/shard_map/ppermute | solution.py:10
  321.6 6.0 %collective-permute-start.4 = (bf16[5,1,16,128]{3,2,1,0:T(8,128)(2,1)S(1)}, bf16[5,1,16,128]{3,2,1,0:T(8,128)(2,1)S(1)}, u32[]{:S(2)}, u32[]{:S(2)}) collective-permute-start(bf16[5,1,16,128]{3,2,1,0:T(8,128)(2,1)S(1)} %pad_maximum_fusion.10), channel_id=1, source_target_pairs={{2,0},{4,2},{6,4},{8,6},{10,8},{12,10},{14,12},{3,1},{5,3},{7,5},{... | collective-permute-start | bytes 61448 | tf_op jit(solution)/shard_map/ppermute | solution.py:10
  325.4 0.9 copy-start.9
  327.6 4.8 collective-permute-start.5
  342.3 1.6 copy-start.2
Sparse Core Ops, SparseCore 0:
  326.4 250.0 all-reduce.7
where the time goes:
time: 589 us; the launch traced here: 586 us
  waiting for transfers between devices  243 us (41%)
  blocking collectives  228 us (39%)
  local copies, waits for them, and re-layouts  35 us (6%)
  matrix products  29.9 us (5%)
  starting transfers between devices  18.3 us (3%)
  other arithmetic  17 us (3%)
  between operations  15 us (3%)
    psum x1, waiting for transfers between devices, weight_totals(): return lax.psum(partial_value, ('gx', 'gy', 'gz')) / count  231 us
    psum x1, blocking collectives, local(): lax.psum((jnp.sum(voxel_mask4), jnp.sum(voxel_mask4 * preactivation, axis...  80.2 us
    psum x1, blocking collectives, local(): lax.psum((jnp.sum(silu_slope, axis=(0, 1, 2)), jnp.sum(silu_slope * stand...  74.3 us
    psum x1, blocking collectives, local(): lax.psum(jnp.sum(voxel_mask4 * (preactivation - batch_mean) ** 2, axis=(0...  73.4 us
    ppermute x6, starting transfers between devices, from_behind(): lax.ppermute(value, axis, [(source, source + steps) for source in range(f...  18.2 us
    mul x2, local copies, waits for them, and re-layouts, local(): whole * pairmask  13.7 us
    ppermute x6, waiting for transfers between devices, from_behind(): lax.ppermute(value, axis, [(source, source + steps) for source in range(f...  11.8 us
  transfers between devices with their start and end apart: 7, of which 6 were waited for; matrix products, arithmetic and copies ran while one was open for 8% of the time, Pallas kernels for 0%

commit v1 on v0

--- a/solution.py
+++ b/solution.py
@@ -29,8 +29,31 @@
     return (block, got)
 
 
+ALL = ("gx", "gy", "gz")
+
+
+def gathered(value, axes):
+    count = lax.axis_size(axes)
+    return lax.all_to_all(jnp.broadcast_to(value, (count,) + value.shape), axes, 0, 0)
+
+
+def merged(parts):
+    counts, sums, squares = (parts[:, 0], parts[:, 1], parts[:, 2])
+    count = jnp.sum(counts, axis=0)
+    total = jnp.sum(sums, axis=0)
+    mean = total / jnp.maximum(count, 1.0)
+    apart = sums / jnp.maximum(counts, 1.0) - mean
+    return jnp.stack([count, total, jnp.sum(squares + counts * apart * apart, axis=0)])
+
+
 def weight_totals(partial_value, count):
-    return lax.psum(partial_value, ("gx", "gy", "gz")) / count
+    devices = lax.axis_size(ALL)
+    rows = -(-partial_value.shape[0] // (8 * devices)) * 8
+    padded = jnp.pad(partial_value, ((0, rows * devices - partial_value.shape[0]), (0, 0)))
+    chunks = padded.astype(jnp.bfloat16).reshape(devices, rows, -1)
+    mine = jnp.sum(lax.all_to_all(chunks, ALL, 0, 0).astype(jnp.float32), axis=0) / count
+    whole = gathered(mine.astype(jnp.bfloat16), ALL)
+    return whole.reshape(devices * rows, -1)[: partial_value.shape[0]].astype(jnp.float32)
 
 
 def local(features, active, weight, gain, bias, cotangent):
@@ -57,15 +80,16 @@
     voxel_mask4 = (
         active.reshape(mx, 2, my, 2, mz, 2).max(axis=(1, 3, 5)).astype(jnp.float32)[..., None]
     )
-    count, total = lax.psum(
-        (jnp.sum(voxel_mask4), jnp.sum(voxel_mask4 * preactivation, axis=(0, 1, 2))),
-        ("gx", "gy", "gz"),
-    )
-    batch_mean = total / count
-    spread = lax.psum(
-        jnp.sum(voxel_mask4 * (preactivation - batch_mean) ** 2, axis=(0, 1, 2)), ("gx", "gy", "gz")
-    )
-    var = spread / count
+    mask3 = voxel_mask4[..., 0]
+    own_count = jnp.sum(mask3)
+    own_total = jnp.sum(voxel_mask4 * preactivation, axis=(0, 1, 2))
+    own_mean = own_total / jnp.maximum(own_count, 1.0)
+    own_squares = jnp.sum(voxel_mask4 * (preactivation - own_mean) ** 2, axis=(0, 1, 2))
+    stats = jnp.stack([jnp.full((cout,), own_count), own_total, own_squares])
+    stats = merged(gathered(merged(gathered(stats, ("gy", "gz"))), "gx"))
+    count = stats[0, 0]
+    batch_mean = stats[1] / count
+    var = stats[2] / count
     inverse_deviation = lax.rsqrt(var + 1e-05)
     standardized_input = (preactivation - batch_mean) * inverse_deviation
     normalized_output = standardized_input * gain + bias
@@ -74,13 +98,14 @@
     silu_slope = (
         voxel_mask4 * cotangent.astype(jnp.float32) * sig * (1.0 + normalized_output * (1.0 - sig))
     )
-    sum_slope, sum_prod = lax.psum(
-        (
+    sums = jnp.stack(
+        [
             jnp.sum(silu_slope, axis=(0, 1, 2)),
             jnp.sum(silu_slope * standardized_input, axis=(0, 1, 2)),
-        ),
-        ("gx", "gy", "gz"),
+        ]
     )
+    sums = jnp.sum(gathered(jnp.sum(gathered(sums, ("gy", "gz")), axis=0), "gx"), axis=0)
+    sum_slope, sum_prod = (sums[0], sums[1])
     shift_gradient = sum_slope / count
     gain_gradient = sum_prod / count
     preactivation_gradient = (
@@ -131,7 +156,8 @@
                 "xyzk,xyzo->ko", odd_in, preactivation_gradient, preferred_element_type=jnp.float32
             )
             blocks.append(jnp.stack([odd_grad, pair_grad[:cin], pair_grad[cin:]]))
-    grad_weight = weight_totals(jnp.stack(blocks).reshape(3, 3, 3, cin, cout), count)
+    flat = jnp.stack(blocks).reshape(27 * cin, cout)
+    grad_weight = weight_totals(flat, count).reshape(3, 3, 3, cin, cout)
     return (section_out, grad_features, grad_weight, gain_gradient, shift_gradient)
 
 

time: 589 us -> 207 us (0.35)
  waiting for transfers between devices: 243 us -> 26.7 us
  blocking collectives: 228 us -> 41.6 us
  starting transfers between devices: 18.3 us -> 46.2 us
  between operations: 15 us -> 2.23 us
    psum x1 -> x0, waiting for transfers between devices: 231 us -> none  [weight_totals(): return lax.psum(partial_value, ('gx', 'gy', 'gz')) / count]
    psum x3 -> x0, blocking collectives: 228 us -> none  [the longest x1 80.2 us: local(): lax.psum((jnp.sum(voxel_mask4), jnp.sum(voxel_mask4 * preactivation, axis...]
    all_to_all x0 -> x3, blocking collectives: none -> 41.6 us  [gathered(): lax.all_to_all(jnp.broadcast_to(value, (count,) + value.shape), axes, 0, 0)]
    all_to_all x0 -> x3, starting transfers between devices: none -> 27.6 us  [the longest x2 16.1 us: gathered(): lax.all_to_all(jnp.broadcast_to(value, (count,) + value.shape), axes, 0, 0)]
    all_to_all x0 -> x3, waiting for transfers between devices: none -> 16.8 us  [the longest x2 13.4 us: gathered(): lax.all_to_all(jnp.broadcast_to(value, (count,) + value.shape), axes, 0, 0)]
  transfers between devices with their start and end apart: 7 -> 9, of which waited for: 6 -> 5; matrix products, arithmetic and copies ran while one was open for 8% -> 25% of each run, Pallas kernels for 0% -> 0%
where the time goes in v1:
time: 207 us; the launch traced here: 205 us
  starting transfers between devices  46.2 us (22%)
  blocking collectives  41.6 us (20%)
  local copies, waits for them, and re-layouts  38.5 us (19%)
  matrix products  34 us (16%)
  waiting for transfers between devices  26.7 us (13%)
  other arithmetic  15.5 us (7%)
  between operations  2.23 us (1%)
    all_to_all x3, blocking collectives, gathered(): lax.all_to_all(jnp.broadcast_to(value, (count,) + value.shape), axes, 0, 0)  41.6 us
    ppermute x6, starting transfers between devices, from_behind(): lax.ppermute(value, axis, [(source, source + steps) for source in range(f...  18.6 us
    all_to_all x2, starting transfers between devices, gathered(): lax.all_to_all(jnp.broadcast_to(value, (count,) + value.shape), axes, 0, 0)  16.1 us
    mul x2, local copies, waits for them, and re-layouts, local(): whole * pairmask  13.7 us
    all_to_all x2, waiting for transfers between devices, gathered(): lax.all_to_all(jnp.broadcast_to(value, (count,) + value.shape), axes, 0, 0)  13.4 us
    all_to_all x1, starting transfers between devices, weight_totals(): lax.all_to_all(chunks, ALL, 0, 0).astype(jnp.float32)  11.5 us
    dot_general x9, matrix products, local(): jnp.einsum('xyzo,ko->xyzk', after, weight[input_a, input_b, 0], preferred...  9.98 us
    ppermute x6, waiting for transfers between devices, from_behind(): lax.ppermute(value, axis, [(source, source + steps) for source in range(f...  9.88 us
  transfers between devices with their start and end apart: 9, of which 5 were waited for; matrix products, arithmetic and copies ran while one was open for 25% of the time, Pallas kernels for 0%

profile of v1, /device:TPU:1, one launch (start us, length us, event | category | flops | bytes accessed | tf_op | source)
XLA Modules:
  0.0 204.6 jit_solution(3957296896245936334)
XLA Ops:
  2.8 1.9 reshape.95
  7.1 6.3 %collective-permute-start = (bf16[1,32,16,128]{3,2,1,0:T(8,128)(2,1)}, bf16[1,32,16,128]{3,2,1,0:T(8,128)(2,1)}, u32[]{:S(2)}, u32[]{:S(2)}) collective-permute-start(bf16[1,32,16,128]{3,2,1,0:T(8,128)(2,1)} %slice.306), channel_id=1, source_target_pairs={{0,16},{16,32},{32,48},{48,64},{64,80},{80,96},{96,112},{112,128},... | collective-permute-start | bytes 393224 | tf_op jit(solution)/shard_map/ppermute | solution.py:10
  13.4 4.9 %mul.120 = bf16[8,32,16,2,64]{4,3,2,1,0:T(2,128)(2,1)S(1)} broadcast(bf16[8,32,16,2]{3,2,1,0:T(8,128)(2,1)S(1)} %copy.54), dimensions={0,1,2,3} | broadcast | bytes 1064960 | tf_op jit(solution)/shard_map/mul | solution.py:65
  18.3 1.8 mul.122
  20.1 1.9 mul.123
  24.6 2.1 %reshape.94 = s32[4,2,16,2,16,2]{5,4,3,2,1,0:T(8,128)S(1)} reshape(s32[8,32,32]{2,1,0:T(8,128)} %param.7) | data formatting | bytes 65536 | tf_op jit(solution)/shard_map/reshape | solution.py:81
  31.7 3.9 %collective-permute-start.1 = (bf16[9,1,16,128]{3,2,1,0:T(8,128)(2,1)S(1)}, bf16[9,1,16,128]{3,2,1,0:T(8,128)(2,1)S(1)}, u32[]{:S(2)}, u32[]{:S(2)}) collective-permute-start(bf16[9,1,16,128]{3,2,1,0:T(8,128)(2,1)S(1)} %fusion.121), channel_id=1, source_target_pairs={{0,2},{2,4},{4,6},{6,8},{8,10},{10,12},{12,14},{1,3},{3,5},{5,7},{... | collective-permute-start | bytes 110600 | tf_op jit(solution)/shard_map/ppermute | solution.py:10
  38.7 2.3 %collective-permute-start.2 = (bf16[9,33,1,64]{3,2,1,0:T(2,128)(2,1)S(1)}, bf16[9,33,1,64]{3,2,1,0:T(2,128)(2,1)S(1)}, u32[]{:S(2)}, u32[]{:S(2)}) collective-permute-start(bf16[9,33,1,64]{3,2,1,0:T(2,128)(2,1)S(1)} %slice.392), channel_id=1, source_target_pairs={{0,1},{2,3},{4,5},{6,7},{8,9},{10,11},{12,13},{14,15},{16,17},{18,... | collective-permute-start | bytes 114056 | tf_op jit(solution)/shard_map/ppermute | solution.py:10
  41.6 2.1 %collective-permute-done.2 = bf16[9,33,1,64]{3,2,1,0:T(2,128)(2,1)S(1)} collective-permute-done((bf16[9,33,1,64]{3,2,1,0:T(2,128)(2,1)S(1)}, bf16[9,33,1,64]{3,2,1,0:T(2,128)(2,1)S(1)}, u32[]{:S(2)}, u32[]{:S(2)}) %collective-permute-start.2) | collective-permute-done | bytes 38048 | tf_op jit(solution)/shard_map/ppermute | solution.py:10
  54.3 13.1 %all_to_all.30 = f32[16,3,128]{2,1,0:T(4,128)S(1)} all-to-all(f32[16,3,128]{2,1,0:T(4,128)S(1)} %broadcast_in_dim.10), channel_id=1, replica_groups=mesh['gx'=16,'gy'=8,'gz'=2] {'gy','gz'}, dimensions={0} | all-to-all | bytes 49152 | tf_op jit(solution)/shard_map/all_to_all | solution.py:37
  67.6 18.4 %all_to_all.31 = f32[16,3,128]{2,1,0:T(4,128)S(1)} all-to-all(f32[16,3,128]{2,1,0:T(4,128)S(1)} %broadcast_in_dim.11), channel_id=1, replica_groups=mesh['gx'=16,'gy'=8,'gz'=2] {'gx'}, dimensions={0} | all-to-all | bytes 49152 | tf_op jit(solution)/shard_map/all_to_all | solution.py:37
  86.6 10.0 %all_to_all.32 = f32[16,2,128]{2,1,0:T(2,128)S(1)} all-to-all(f32[16,2,128]{2,1,0:T(2,128)S(1)} %broadcast_in_dim.12), channel_id=1, replica_groups=mesh['gx'=16,'gy'=8,'gz'=2] {'gy','gz'}, dimensions={0} | all-to-all | bytes 32768 | tf_op jit(solution)/shard_map/all_to_all | solution.py:37
  97.2 3.7 %all-to-all-start.3 = ((f32[16,2,128]{2,1,0:T(2,128)}), f32[16,2,128]{2,1,0:T(2,128)S(1)}, u32[]{:S(2)}, u32[]{:S(2)}) async-start(f32[16,2,128]{2,1,0:T(2,128)} %broadcast_in_dim.13), calls=%async_computation.3 | async-start | bytes 32768 | tf_op jit(solution)/shard_map/all_to_all | solution.py:37
  100.9 2.2 %copy.65 = f32[8,32,16,2]{3,2,1,0:T(8,128)} copy(bf16[8,32,16,2]{1,0,3,2:T(8,128)(2,1)S(1)} %bitcast.466) | data formatting | bytes 49152 | tf_op jit(solution)/shard_map/convert_element_type | solution.py:146
  103.1 8.3 %mul.146 = f32[8,32,16,2,64]{4,3,2,1,0:T(2,128)} broadcast(f32[8,32,16,2]{3,2,1,0:T(8,128)} %copy.65), dimensions={0,1,2,3} | broadcast | bytes 2129920 | tf_op jit(solution)/shard_map/mul | solution.py:146
  111.4 5.4 %mul.147 = f32[8,32,16,128]{3,2,1,0:T(8,128)} reshape(f32[8,32,16,2,64]{4,3,2,1,0:T(2,128)} %mul.146) | data formatting | bytes 4194304 | tf_op jit(solution)/shard_map/mul | solution.py:146
  116.9 2.2 %multiply_convert_fusion.1 = (bf16[4,16,16,128]{3,2,1,0:T(8,128)(2,1)S(1)}, bf16[4,16,16,128]{3,2,1,0:T(8,128)(2,1)}) fusion(f32[4,16,16,128]{3,2,1,0:T(8,128)S(1)} %get-tuple-element.40, f32[128]{0:T(128)S(1)} %get-tuple-element.36, f32[128]{0:T(128)S(1)} %get-tuple-element.35, f32[128]{0:T(128)S(1)} %copy-done.16, f32[128]{0:T(128)S(1)} %add_rsqrt_fusion, ...), kind=kLoop, calls=%fused_computation.106 | loop fusion | flops 3145728 | bytes 1317888 | tf_op jit(solution)/shard_map/convert_element_type | solution.py:116
  129.2 5.1 %collective-permute-done.3 = bf16[1,16,16,128]{3,2,1,0:T(8,128)(2,1)S(1)} collective-permute-done((bf16[1,16,16,128]{3,2,1,0:T(8,128)(2,1)S(1)}, bf16[1,16,16,128]{3,2,1,0:T(8,128)(2,1)S(1)}, u32[]{:S(2)}, u32[]{:S(2)}) %collective-permute-start.3) | collective-permute-done | bytes 65568 | tf_op jit(solution)/shard_map/ppermute | solution.py:10
  134.2 3.4 %collective-permute-start.4 = (bf16[5,1,16,128]{3,2,1,0:T(8,128)(2,1)S(1)}, bf16[5,1,16,128]{3,2,1,0:T(8,128)(2,1)S(1)}, u32[]{:S(2)}, u32[]{:S(2)}) collective-permute-start(bf16[5,1,16,128]{3,2,1,0:T(8,128)(2,1)S(1)} %pad_maximum_fusion.10), channel_id=1, source_target_pairs={{2,0},{4,2},{6,4},{8,6},{10,8},{12,10},{14,12},{3,1},{5,3},{7,5},{... | collective-permute-start | bytes 61448 | tf_op jit(solution)/shard_map/ppermute | solution.py:10
  138.5 11.5 %all-to-all-start.4 = ((bf16[256,8,128]{2,1,0:T(8,128)(2,1)}), bf16[256,8,128]{2,1,0:T(8,128)(2,1)S(1)}, u32[]{:S(2)}, u32[]{:S(2)}) async-start(bf16[256,8,128]{2,1,0:T(8,128)(2,1)} %pad_bitcast_fusion), calls=%async_computation.4 | async-start | bytes 1048576 | tf_op jit(solution)/shard_map/all_to_all | solution.py:54
  152.6 2.8 %collective-permute-done.5 = bf16[5,17,1,128]{3,2,1,0:T(2,128)(2,1)S(1)} collective-permute-done((bf16[5,17,1,128]{3,2,1,0:T(2,128)(2,1)S(1)}, bf16[5,17,1,128]{3,2,1,0:T(2,128)(2,1)S(1)}, u32[]{:S(2)}, u32[]{:S(2)}) %collective-permute-start.5) | collective-permute-done | bytes 21792 | tf_op jit(solution)/shard_map/ppermute | solution.py:10
  166.6 3.4 %all-to-all-done.4 = bf16[256,8,128]{2,1,0:T(8,128)(2,1)S(1)} async-done(((bf16[256,8,128]{2,1,0:T(8,128)(2,1)}), bf16[256,8,128]{2,1,0:T(8,128)(2,1)S(1)}, u32[]{:S(2)}, u32[]{:S(2)}) %all-to-all-start.4) | async-done | bytes 524320 | tf_op jit(solution)/shard_map/all_to_all | solution.py:54
  171.1 12.4 %all-to-all-start.5 = ((bf16[256,8,128]{2,1,0:T(8,128)(2,1)}), bf16[256,8,128]{2,1,0:T(8,128)(2,1)}, u32[]{:S(2)}, u32[]{:S(2)}) async-start(bf16[256,8,128]{2,1,0:T(8,128)(2,1)} %broadcast_in_dim.14), calls=%async_computation.5 | async-start | bytes 1048576 | tf_op jit(solution)/shard_map/all_to_all | solution.py:37
  189.2 13.4 %all-to-all-done.5 = bf16[256,8,128]{2,1,0:T(8,128)(2,1)} async-done(((bf16[256,8,128]{2,1,0:T(8,128)(2,1)}), bf16[256,8,128]{2,1,0:T(8,128)(2,1)}, u32[]{:S(2)}, u32[]{:S(2)}) %all-to-all-start.5) | async-done | bytes 524320 | tf_op jit(solution)/shard_map/all_to_all | solution.py:37
  (172 shorter events, 60.0 us)
Async XLA Ops:
  0.6 2.2 %copy-start.3 = (bf16[8,32,16,128]{3,2,1,0:T(8,128)(2,1)S(1)}, bf16[8,32,16,128]{3,2,1,0:T(8,128)(2,1)}, u32[]{:S(2)}) copy-start(bf16[8,32,16,128]{3,2,1,0:T(8,128)(2,1)} %param.6) | copy-start | bytes 3145732
  7.1 23.9 %collective-permute-start = (bf16[1,32,16,128]{3,2,1,0:T(8,128)(2,1)}, bf16[1,32,16,128]{3,2,1,0:T(8,128)(2,1)}, u32[]{:S(2)}, u32[]{:S(2)}) collective-permute-start(bf16[1,32,16,128]{3,2,1,0:T(8,128)(2,1)} %slice.306), channel_id=1, source_target_pairs={{0,16},{16,32},{32,48},{48,64},{64,80},{80,96},{96,112},{112,128},... | collective-permute-start | bytes 393224 | tf_op jit(solution)/shard_map/ppermute | solution.py:10
  20.1 1.9 copy-start.13
  31.7 5.4 %collective-permute-start.1 = (bf16[9,1,16,128]{3,2,1,0:T(8,128)(2,1)S(1)}, bf16[9,1,16,128]{3,2,1,0:T(8,128)(2,1)S(1)}, u32[]{:S(2)}, u32[]{:S(2)}) collective-permute-start(bf16[9,1,16,128]{3,2,1,0:T(8,128)(2,1)S(1)} %fusion.121), channel_id=1, source_target_pairs={{0,2},{2,4},{4,6},{6,8},{8,10},{10,12},{12,14},{1,3},{3,5},{5,7},{... | collective-permute-start | bytes 110600 | tf_op jit(solution)/shard_map/ppermute | solution.py:10
  36.7 1.5 copy-start.4
  38.2 10.8 %copy-start = (bf16[9,33,16,128]{3,2,1,0:T(8,128)(2,1)}, bf16[9,33,16,128]{3,2,1,0:T(8,128)(2,1)S(1)}, u32[]{:S(2)}) copy-start(bf16[9,33,16,128]{3,2,1,0:T(8,128)(2,1)S(1)} %maximum_maximum_fusion) | copy-start | bytes 3649540
  38.7 5.0 %collective-permute-start.2 = (bf16[9,33,1,64]{3,2,1,0:T(2,128)(2,1)S(1)}, bf16[9,33,1,64]{3,2,1,0:T(2,128)(2,1)S(1)}, u32[]{:S(2)}, u32[]{:S(2)}) collective-permute-start(bf16[9,33,1,64]{3,2,1,0:T(2,128)(2,1)S(1)} %slice.392), channel_id=1, source_target_pairs={{0,1},{2,3},{4,5},{6,7},{8,9},{10,11},{12,13},{14,15},{16,17},{18,... | collective-permute-start | bytes 114056 | tf_op jit(solution)/shard_map/ppermute | solution.py:10
  46.2 2.9 %copy-start.6 = (f32[4,16,16,128]{3,2,1,0:T(8,128)S(1)}, f32[4,16,16,128]{3,2,1,0:T(8,128)}, u32[]{:S(2)}) copy-start(f32[4,16,16,128]{3,2,1,0:T(8,128)} %fusion.82) | copy-start | bytes 1572868
  52.9 33.3 %copy-start.12 = (bf16[4,16,16,128]{3,2,1,0:T(8,128)(2,1)S(1)}, bf16[4,16,16,128]{3,2,1,0:T(8,128)(2,1)}, u32[]{:S(2)}) copy-start(bf16[4,16,16,128]{3,2,1,0:T(8,128)(2,1)} %param.11) | copy-start | bytes 786436
  52.9 33.3 %copy-start.15 = (f32[128]{0:T(128)S(1)}, f32[128]{0:T(128)}, u32[]{:S(2)}) copy-start(f32[128]{0:T(128)} %param.10) | copy-start | bytes 1540
  52.9 33.3 %copy-start.16 = (f32[128]{0:T(128)S(1)}, f32[128]{0:T(128)}, u32[]{:S(2)}) copy-start(f32[128]{0:T(128)} %param.9) | copy-start | bytes 1540
  97.2 19.6 %all-to-all-start.3 = ((f32[16,2,128]{2,1,0:T(2,128)}), f32[16,2,128]{2,1,0:T(2,128)S(1)}, u32[]{:S(2)}, u32[]{:S(2)}) async-start(f32[16,2,128]{2,1,0:T(2,128)} %broadcast_in_dim.13), calls=%async_computation.3 | async-start | bytes 32768 | tf_op jit(solution)/shard_map/all_to_all | solution.py:37
  116.9 2.5 %copy-start.1 = (bf16[9,33,16,128]{3,2,1,0:T(8,128)(2,1)S(1)}, bf16[9,33,16,128]{3,2,1,0:T(8,128)(2,1)}, u32[]{:S(2)}) copy-start(bf16[9,33,16,128]{3,2,1,0:T(8,128)(2,1)} %copy-done) | copy-start | bytes 3649540
  116.9 2.8 %copy-start.17 = (f32[128]{0:T(128)}, f32[128]{0:T(128)S(1)}, u32[]{:S(2)}) copy-start(f32[128]{0:T(128)S(1)} %get-tuple-element.35) | copy-start | bytes 1540
  116.9 2.8 %copy-start.18 = (f32[128]{0:T(128)}, f32[128]{0:T(128)S(1)}, u32[]{:S(2)}) copy-start(f32[128]{0:T(128)S(1)} %get-tuple-element.36) | copy-start | bytes 1540
  127.7 6.5 %collective-permute-start.3 = (bf16[1,16,16,128]{3,2,1,0:T(8,128)(2,1)S(1)}, bf16[1,16,16,128]{3,2,1,0:T(8,128)(2,1)S(1)}, u32[]{:S(2)}, u32[]{:S(2)}) collective-permute-start(bf16[1,16,16,128]{3,2,1,0:T(8,128)(2,1)S(1)} %slice.414), channel_id=1, source_target_pairs={{16,0},{32,16},{48,32},{64,48},{80,64},{96,80},{112,96},{128,112},... | collective-permute-start | bytes 196616 | tf_op jit(solution)/shard_map/ppermute | solution.py:10
  134.2 15.8 %collective-permute-start.4 = (bf16[5,1,16,128]{3,2,1,0:T(8,128)(2,1)S(1)}, bf16[5,1,16,128]{3,2,1,0:T(8,128)(2,1)S(1)}, u32[]{:S(2)}, u32[]{:S(2)}) collective-permute-start(bf16[5,1,16,128]{3,2,1,0:T(8,128)(2,1)S(1)} %pad_maximum_fusion.10), channel_id=1, source_target_pairs={{2,0},{4,2},{6,4},{8,6},{10,8},{12,10},{14,12},{3,1},{5,3},{7,5},{... | collective-permute-start | bytes 61448 | tf_op jit(solution)/shard_map/ppermute | solution.py:10
  138.5 31.4 %all-to-all-start.4 = ((bf16[256,8,128]{2,1,0:T(8,128)(2,1)}), bf16[256,8,128]{2,1,0:T(8,128)(2,1)S(1)}, u32[]{:S(2)}, u32[]{:S(2)}) async-start(bf16[256,8,128]{2,1,0:T(8,128)(2,1)} %pad_bitcast_fusion), calls=%async_computation.4 | async-start | bytes 1048576 | tf_op jit(solution)/shard_map/all_to_all | solution.py:54
  150.1 5.3 %collective-permute-start.5 = (bf16[5,17,1,128]{3,2,1,0:T(2,128)(2,1)S(1)}, bf16[5,17,1,128]{3,2,1,0:T(2,128)(2,1)S(1)}, u32[]{:S(2)}, u32[]{:S(2)}) collective-permute-start(bf16[5,17,1,128]{3,2,1,0:T(2,128)(2,1)S(1)} %pad_maximum_fusion.8), channel_id=1, source_target_pairs={{1,0},{3,2},{5,4},{7,6},{9,8},{11,10},{13,12},{15,14},{17,16},{19,... | collective-permute-start | bytes 65288 | tf_op jit(solution)/shard_map/ppermute | solution.py:10
  171.1 12.7 %copy-start.7 = (f32[4,16,16,128]{3,2,1,0:T(8,128)S(1)}, f32[4,16,16,128]{3,2,1,0:T(8,128)}, u32[]{:S(2)}) copy-start(f32[4,16,16,128]{3,2,1,0:T(8,128)} %fusion.145) | copy-start | bytes 1572868
  171.1 12.7 %copy-start.10 = (f32[4,16,16,64]{3,2,1,0:T(8,128)S(1)}, f32[4,16,16,64]{3,2,1,0:T(8,128)}, u32[]{:S(2)}) copy-start(f32[4,16,16,64]{3,2,1,0:T(8,128)} %convolution_add_fusion.2) | copy-start | bytes 786436
  171.1 31.5 %all-to-all-start.5 = ((bf16[256,8,128]{2,1,0:T(8,128)(2,1)}), bf16[256,8,128]{2,1,0:T(8,128)(2,1)}, u32[]{:S(2)}, u32[]{:S(2)}) async-start(bf16[256,8,128]{2,1,0:T(8,128)(2,1)} %broadcast_in_dim.14), calls=%async_computation.5 | async-start | bytes 1048576 | tf_op jit(solution)/shard_map/all_to_all | solution.py:37
  183.8 1.2 copy-start.9
  186.3 1.6 copy-start.2
  (4 other events, 3.9 us)

commit v2 on v0

v2 whole, which is shorter than its diff:
```python
import jax
import jax.numpy as jnp
from jax import lax
from jax.experimental import pallas as pl
from jax.experimental.pallas import tpu as pltpu
from jax.sharding import Mesh, PartitionSpec as P

BF = jnp.bfloat16
F32 = jnp.float32
ALL = ("z", "yh", "x", "c", "yl")
NEAR = ("yh", "x", "c", "yl")
FAR = ("z",)
PARAMS = pltpu.CompilerParams(vmem_limit_bytes=48 * 1024 * 1024)


def call(kernel, outs, args, scratch=(), flops=100_000_000):
    size = sum(a.size * a.dtype.itemsize for a in args) + sum(o.size * o.dtype.itemsize for o in outs)
    return pl.pallas_call(
        kernel,
        out_shape=outs,
        in_specs=[pl.BlockSpec(memory_space=pltpu.VMEM) for _ in args],
        out_specs=[pl.BlockSpec(memory_space=pltpu.VMEM) for _ in outs],
        scratch_shapes=list(scratch),
        compiler_params=PARAMS,
        cost_estimate=pl.CostEstimate(flops=flops, bytes_accessed=size, transcendentals=0),
    )(*args)


def shape(dims, dtype):
    return jax.ShapeDtypeStruct(dims, dtype)


def dot(left, right, dims=((1,), (0,))):
    return lax.dot_general(left, right, (dims, ((), ())), preferred_element_type=F32)


def row_picker(rows, step, offset):
    r = lax.broadcasted_iota(jnp.int32, (rows, rows * step), 0)
    k = lax.broadcasted_iota(jnp.int32, (rows, rows * step), 1)
    return (k == r * step + offset).astype(BF)


def with_edge(value, edge, at, shift):
    groups, depth, lanes = value.shape
    moved = pltpu.roll(value.reshape(groups * depth, lanes), shift % (groups * depth), 0)
    moved = moved.reshape(groups, depth, lanes)
    q = lax.broadcasted_iota(jnp.int32, value.shape, 1)
    return jnp.where(q == at, jnp.broadcast_to(edge[:, None, :], value.shape), moved)


def mask_kernel(feat, active, xin, mask, act, zface):
    nx, _, my, mz, width = xin.shape
    z = active.shape[2]
    sel = (
        lax.broadcasted_iota(jnp.int32, (mz, z), 1) // 2 == lax.broadcasted_iota(jnp.int32, (mz, z), 0)
    ).astype(F32)
    lane = lax.broadcasted_iota(jnp.int32, (z, width), 1) // (width // 2)
    spread = (lax.broadcasted_iota(jnp.int32, (z, width), 0) % 2 == lane).astype(BF)
    pick = row_picker(my, mz, mz - 1)
    count = None
    for x in range(nx):
        a = active[x].astype(F32)
        rep = jnp.broadcast_to(a[:, None, :], (2 * my, mz, z)) * sel[None]
        m = dot(rep.astype(BF).reshape(2 * my * mz, z), spread).astype(BF)
        m = m.reshape(my, 2, mz, width)
        value = feat[x].reshape(my, 2, mz, width) * m
        for py in range(2):
            part = m[:, py]
            mask[x, py] = part
            held = value[:, py]
            xin[x, py] = held
            zface[x, py] = dot(pick, held.reshape(my * mz, width)).astype(BF)
            term = part.astype(F32).reshape(my * mz, width)
            count = term if count is None else count + term
        if x % 2 == 1:
            both = count + pltpu.roll(count, width // 2, 1)
            act[x // 2] = (both > 0.0).astype(F32).astype(BF).reshape(my, mz, width)
            count = None


def tile_of(xin, xh, yh, row, b):
    py = 0 if b == 1 else 1
    my = xin.shape[2]
    base = xh[py, :my] if row == 0 else xin[row - 1, py]
    if b == 0:
        base = jnp.concatenate([yh[row][None], base[: my - 1]], axis=0)
    return base


def edge_of(zh, ch, row, b):
    base = zh[row, 0 if b == 1 else 1]
    if b == 0:
        wide = base.astype(F32)
        wide = jnp.concatenate([ch[row : row + 1].astype(F32), wide[: wide.shape[0] - 1]], axis=0)
        base = wide.astype(BF)
    return base


TAPS = [(a, b) for a in range(3) for b in range(3)]


def forward_kernel(xin, act, xh, yh, zh, ch, weight, pre, stats, wmat):
    mx, my, mz, cout = pre.shape
    width = xin.shape[4]
    half = width // 2
    zero = jnp.zeros((half, cout), BF)
    for i, (a, b) in enumerate(TAPS):
        lo = i * width
        wmat[lo : lo + half, :cout] = weight[a, b, 1]
        wmat[lo + half : lo + width, :cout] = weight[a, b, 2]
        wmat[lo : lo + half, cout:] = zero
        wmat[lo + half : lo + width, cout:] = weight[a, b, 0]
    rows = my * mz
    total = jnp.zeros((1, cout), F32)
    count = jnp.zeros((1, cout), F32)
    w = wmat[...]
    for m in range(mx):
        left = jnp.concatenate(
            [tile_of(xin, xh, yh, 2 * m + a, b).reshape(rows, width) for a, b in TAPS], axis=1
        )
        edge = jnp.concatenate([edge_of(zh, ch, 2 * m + a, b) for a, b in TAPS], axis=1)
        out = dot(left, w)
        rim = dot(edge, w[:, cout:])
        prev = with_edge(out[:, cout:].reshape(my, mz, cout), rim, 0, 1)
        value = out[:, :cout].reshape(my, mz, cout) + prev
        pre[m] = value
        on = act[m].astype(F32)
        total = total + jnp.sum((on * value).reshape(rows, cout), axis=0, keepdims=True)
        count = count + jnp.sum(on.reshape(rows, cout), axis=0, keepdims=True)
    mean = total / jnp.maximum(count, 1.0)
    squares = jnp.zeros((1, cout), F32)
    for m in range(mx):
        apart = pre[m].reshape(rows, cout) - mean
        on = act[m].astype(F32).reshape(rows, cout)
        squares = squares + jnp.sum(on * apart * apart, axis=0, keepdims=True)
    for i in range(stats.shape[0]):
        stats[i, 0:1] = count
        stats[i, 1:2] = total
        stats[i, 2:3] = squares


def slope_kernel(pre, act, cot, par, out, slope, sums):
    mx, my, mz, cout = pre.shape
    rows = my * mz
    mean, rstd, gain, bias = (par[i : i + 1] for i in range(4))
    first = jnp.zeros((1, cout), F32)
    second = jnp.zeros((1, cout), F32)
    for m in range(mx):
        on = act[m].astype(F32).reshape(rows, cout)
        hat = (pre[m].reshape(rows, cout) - mean) * rstd
        normed = hat * gain + bias
        sig = jax.nn.sigmoid(normed)
        out[m] = (on * normed * sig).astype(BF).reshape(my, mz, cout)
        tilt = on * cot[m].astype(F32).reshape(rows, cout) * sig * (1.0 + normed * (1.0 - sig))
        slope[m] = tilt.reshape(my, mz, cout)
        first = first + jnp.sum(tilt, axis=0, keepdims=True)
        second = second + jnp.sum(tilt * hat, axis=0, keepdims=True)
    for i in range(sums.shape[0]):
        sums[i, 0:1] = first
        sums[i, 1:2] = second


def weight_kernel(slope, pre, act, par, xin, xh, yh, zh, ch, dpre, pack, zface, dw):
    mx, my, mz, cout = pre.shape
    width = xin.shape[4]
    half = width // 2
    rows = my * mz
    mean, rstd, gain, shift, tilt = (par[i : i + 1] for i in range(5))
    pick = row_picker(my, mz, 0)
    last = lax.broadcasted_iota(jnp.int32, (my, mz, cout), 1) == mz - 1
    total = None
    rims = []
    for m in range(mx):
        on = act[m].astype(F32).reshape(rows, cout)
        hat = (pre[m].reshape(rows, cout) - mean) * rstd
        grad = on * rstd * gain * (slope[m].reshape(rows, cout) - shift - hat * tilt)
        held = grad.astype(BF)
        dpre[m] = held.reshape(my, mz, cout)
        first = dot(pick, held)
        zface[m] = first.astype(BF)
        if m == 0:
            pack[:my] = held.reshape(my, mz, cout)
            pack[my] = first.astype(BF)
        rims.append(first)
        wide = held.astype(F32)
        after = pltpu.roll(wide, rows - 1, 0).reshape(my, mz, cout)
        after = jnp.where(last, 0.0, after).reshape(rows, cout)
        right = jnp.concatenate([wide.T, after.T], axis=0).astype(BF)
        left = jnp.concatenate(
            [tile_of(xin, xh, yh, 2 * m + a, b).reshape(rows, width) for a, b in TAPS], axis=1
        )
        term = dot(right, left)
        total = term if total is None else total + term
    rim = jnp.concatenate(rims, axis=0).T.astype(BF)
    edge = jnp.concatenate(
        [
            jnp.concatenate([edge_of(zh, ch, 2 * m + a, b) for a, b in TAPS], axis=1)
            for m in range(mx)
        ],
        axis=0,
    )
    low = total[cout:] + dot(rim, edge)
    for i in range(len(TAPS)):
        at = i * width
        own = total[:cout, at : at + width].T
        prev = low[:, at : at + width].T
        dw[3 * half * i : 3 * half * i + half] = prev[half:].astype(BF)
        dw[3 * half * i + half : 3 * half * (i + 1)] = own.astype(BF)
    used = 3 * half * len(TAPS)
    if dw.shape[0] > used:
        dw[used:] = jnp.zeros((dw.shape[0] - used, cout), BF)


def input_kernel(dpre, xh, yh, zh, ch, wmat, mask, out, ext, nxt):
    mx, my, mz, cout = dpre.shape
    width = mask.shape[4]
    rows = my * mz
    for r in range(mx + 1):
        base = dpre[r] if r < mx else xh[:my]
        ext[r, :my] = base
        ext[r, my] = yh[r]
        whole = jnp.concatenate([base, yh[r][None]], axis=0).astype(F32)
        rim = jnp.concatenate([zh[r].astype(F32), ch[r : r + 1].astype(F32)], axis=0)
        nxt[r] = with_edge(whole, rim, mz - 1, -1).astype(BF)
    taps = (((1, 0),), ((2, 0), (0, 1)))
    for m in range(mx):
        for px in range(2):
            for py in range(2):
                left, right = ([], [])
                for a, sx in taps[px]:
                    for b, sy in taps[py]:
                        left.append(ext[m + sx, sy : sy + my].reshape(rows, cout))
                        left.append(nxt[m + sx, sy : sy + my].reshape(rows, cout))
                        at = (a * 3 + b) * width
                        right.append(wmat[at : at + width])
                left = jnp.concatenate(left, axis=1)
                right = jnp.concatenate(right, axis=1)
                value = dot(left, right, ((1,), (1,)))
                x = 2 * m + px
                value = value * mask[x, py].astype(F32).reshape(rows, width)
                out[x, :, py] = value.astype(BF).reshape(my, mz, width)


def moved(value, sizes, by):
    nx, ny, nz = sizes
    pairs = []
    for i in range(nx):
        for j in range(ny):
            for k in range(nz):
                i2, j2, k2 = (i + by[0], j + by[1], k + by[2])
                if 0 <= i2 < nx and 0 <= j2 < ny and 0 <= k2 < nz:
                    pairs.append(((i * ny + j) * nz + k, (i2 * ny + j2) * nz + k2))
    return lax.ppermute(value, ALL, pairs)


def exchanged(value, axes):
    return lax.all_to_all(value, axes, 0, 0)


def spread(value, axes):
    return exchanged(jnp.broadcast_to(value, (lax.axis_size(axes),) + value.shape), axes)


def merged(parts):
    counts, sums, squares = (parts[:, 0], parts[:, 1], parts[:, 2])
    count = jnp.sum(counts, axis=0)
    total = jnp.sum(sums, axis=0)
    mean = total / jnp.maximum(count, 1.0)
    apart = sums / jnp.maximum(counts, 1.0) - mean
    return jnp.stack([count, total, jnp.sum(squares + counts * apart * apart, axis=0)])


def local(sizes, features, active, weight, gain, bias, cotangent):
    vx, vy, mz, width = features.shape
    cin = width // 2
    cout = weight.shape[4]
    mx, my = (vx // 2, vy // 2)
    near = lax.axis_size(NEAR)
    xin, mask, act, zface = call(
        mask_kernel,
        [
            shape((vx, 2, my, mz, width), BF),
            shape((vx, 2, my, mz, width), BF),
            shape((mx, my, mz, width), BF),
            shape((vx, 2, my, width), BF),
        ],
        [features, active],
    )
    pack = jnp.concatenate([xin[vx - 1], zface[vx - 1][:, None]], axis=1)
    xh = moved(pack, sizes, (1, 0, 0))
    yface = jnp.concatenate([xh[1:2, my - 1], xin[:, 1, my - 1]], axis=0)
    zfaces = jnp.concatenate([xh[None, :, my], zface], axis=0)
    corner = zfaces[:, 1, my - 1]
    yh = moved(yface, sizes, (0, 1, 0))
    zh = moved(zfaces, sizes, (0, 0, 1))
    ch = moved(corner, sizes, (0, 1, 1))
    pre, stats, wmat = call(
        forward_kernel,
        [
            shape((mx, my, mz, cout), F32),
            shape((near, 3, cout), F32),
            shape((9 * width, 2 * cout), BF),
        ],
        [xin, act, xh, yh, zh, ch, weight],
        flops=1_200_000_000,
    )
    stats = merged(spread(merged(exchanged(stats, NEAR)), FAR))
    count = stats[0]
    mean = stats[1] / count
    rstd = lax.rsqrt(stats[2] / count + 1e-05)
    par = jnp.stack([mean, rstd, gain, bias])
    section_out, slope, sums = call(
        slope_kernel,
        [
            shape((mx, my, mz, cout), BF),
            shape((mx, my, mz, cout), F32),
            shape((near, 2, cout), F32),
        ],
        [pre, act, cotangent, par],
    )
    sums = jnp.sum(spread(jnp.sum(exchanged(sums, NEAR), axis=0), FAR), axis=0)
    shift_gradient = sums[0] / count
    gain_gradient = sums[1] / count
    par = jnp.stack([mean, rstd, gain, shift_gradient, gain_gradient])
    taps = 27 * cin
    rows = -(-taps // (16 * near)) * 16
    if near * (rows - 8) >= taps and near * (rows - 8) % 16 == 0:
        rows = rows - 8
    dpre, pack, zface, dw = call(
        weight_kernel,
        [
            shape((mx, my, mz, cout), BF),
            shape((my + 1, mz, cout), BF),
            shape((mx, my, cout), BF),
            shape((near * rows, cout), BF),
        ],
        [slope, pre, act, par, xin, xh, yh, zh, ch],
        flops=1_200_000_000,
    )
    xd = moved(pack, sizes, (-1, 0, 0))
    mine = jnp.sum(exchanged(dw.reshape(near, rows, cout), NEAR).astype(F32), axis=0)
    zfaces = jnp.concatenate([zface, xd[my:]], axis=0)
    yd = moved(jnp.concatenate([dpre[:, 0], xd[:1]], axis=0), sizes, (0, -1, 0))
    zd = moved(zfaces, sizes, (0, 0, -1))
    cd = moved(zfaces[:, 0], sizes, (0, -1, -1))
    mine = jnp.sum(spread(mine, FAR), axis=0) / count[0]
    grad_weight = spread(mine.astype(BF), NEAR).reshape(near * rows, cout)[:taps]
    grad_weight = grad_weight.astype(F32).reshape(weight.shape)
    (grad_features,) = call(
        input_kernel,
        [shape((vx, my, 2, mz, width), BF)],
        [dpre, xd, yd, zd, cd, wmat, mask],
        scratch=[pltpu.VMEM((mx + 1, my + 1, mz, cout), BF)] * 2,
        flops=1_200_000_000,
    )
    grad_features = grad_features.reshape(features.shape)
    return (section_out, grad_features, grad_weight, gain_gradient, shift_gradient)


def solution(mesh):
    gx, gy, gz = (mesh.shape[name] for name in ("gx", "gy", "gz"))
    fine = Mesh(mesh.devices.reshape(gx // 2, 2, gy // 2, 2, gz), ALL)
    block = (("z", "yh"), ("x", "c"), "yl")
    in_specs = (P(*block, None), P(*block), P(), P(), P(), P(*block, None))
    out_specs = (P(*block, None), P(*block, None), P(), P(), P())

    def body(*args):
        return local((gx, gy, gz), *args)

    return jax.shard_map(body, mesh=fine, in_specs=in_specs, out_specs=out_specs, check_vma=False)
```

time: 589 us -> 131 us (0.22)
  waiting for transfers between devices: 243 us -> 22.1 us
  blocking collectives: 228 us -> 53.6 us
  matrix products: 29.9 us -> 0 us
  local copies, waits for them, and re-layouts: 35 us -> 5.41 us
  starting transfers between devices: 18.3 us -> 37.5 us
  other arithmetic: 17 us -> 2.04 us
  between operations: 15 us -> 1.04 us
  Pallas kernels: 0 us -> 8.35 us
    psum x1 -> x0, waiting for transfers between devices: 231 us -> none  [weight_totals(): return lax.psum(partial_value, ('gx', 'gy', 'gz')) / count]
    psum x3 -> x0, blocking collectives: 228 us -> none  [the longest x1 80.2 us: local(): lax.psum((jnp.sum(voxel_mask4), jnp.sum(voxel_mask4 * preactivation, axis...]
    all_to_all x0 -> x4, blocking collectives: none -> 53.6 us  [exchanged(): return lax.all_to_all(value, axes, 0, 0)]
    dot_general x54 -> x0, matrix products: 29.9 us -> none  [the longest x9 8.53 us: local(): jnp.einsum('xyzk,ko->xyzo', odd_in, weight[a, b, 0], preferred_element_ty...]
    mul x4 -> x0, local copies, waits for them, and re-layouts: 22.2 us -> none  [the longest x2 13.7 us: local(): whole * pairmask]
    all_to_all x0 -> x3, starting transfers between devices: none -> 16.1 us  [exchanged(): return lax.all_to_all(value, axes, 0, 0)]
    all_to_all x0 -> x3, waiting for transfers between devices: none -> 14.1 us  [exchanged(): return lax.all_to_all(value, axes, 0, 0)]
    pallas_call x0 -> x5, Pallas kernels: none -> 8.35 us  [call(): pl.pallas_call(kernel, out_shape=outs, in_specs=[pl.BlockSpec(memory_spac...]
  transfers between devices with their start and end apart: 7 -> 11, of which waited for: 6 -> 6; matrix products, arithmetic and copies ran while one was open for 8% -> 2% of each run, Pallas kernels for 0% -> 2%
where the time goes in v2:
time: 131 us; the launch traced here: 130 us
  blocking collectives  53.6 us (41%)
  starting transfers between devices  37.5 us (29%)
  waiting for transfers between devices  22.1 us (17%)
  Pallas kernels  8.35 us (6%)
  local copies, waits for them, and re-layouts  5.41 us (4%)
  other arithmetic  2.04 us (2%)
    all_to_all x4, blocking collectives, exchanged(): return lax.all_to_all(value, axes, 0, 0)  53.6 us
    ppermute x8, starting transfers between devices, moved(): return lax.ppermute(value, ALL, pairs)  21.4 us
    all_to_all x3, starting transfers between devices, exchanged(): return lax.all_to_all(value, axes, 0, 0)  16.1 us
    all_to_all x3, waiting for transfers between devices, exchanged(): return lax.all_to_all(value, axes, 0, 0)  14.1 us
    pallas_call x5, Pallas kernels, call(): pl.pallas_call(kernel, out_shape=outs, in_specs=[pl.BlockSpec(memory_spac...  8.35 us
    ppermute x8, waiting for transfers between devices, moved(): return lax.ppermute(value, ALL, pairs)  8.02 us
    unnamed x20, local copies, waits for them, and re-layouts  3.62 us
  transfers between devices with their start and end apart: 11, of which 6 were waited for; matrix products, arithmetic and copies ran while one was open for 2% of the time, Pallas kernels for 2%

profile of v2, /device:TPU:1, one launch (start us, length us, event | category | flops | bytes accessed | tf_op | source)
XLA Modules:
  0.0 130.1 jit_solution(1112543265960511220)
XLA Ops:
  0.6 1.2 copy-done
  2.8 1.8 %shard_map.101 = (bf16[8,2,16,16,128]{4,3,2,1,0:T(8,128)(2,1)S(1)}, bf16[8,2,16,16,128]{4,3,2,1,0:T(8,128)(2,1)S(1)}, bf16[4,16,16,128]{3,2,1,0:T(8,128)(2,1)S(1)}, bf16[8,2,16,128]{3,2,1,0:T(8,128)(2,1)S(1)}) custom-call(bf16[8,32,16,128]{3,2,1,0:T(8,128)(2,1)S(1)} %copy-done, s32[8,32,32]{2,1,0:T(8,128)S(1)} %copy-done.2), custom_call_target="tpu_custom_call" | custom-call | flops 100000000 | bytes 3506176 | tf_op jit(solution)/shard_map/pallas_call | solution.py:18
  4.6 5.8 %collective-permute-start = (bf16[2,17,16,128]{3,2,1,0:T(8,128)(2,1)S(1)}, bf16[2,17,16,128]{3,2,1,0:T(8,128)(2,1)S(1)}, u32[]{:S(2)}, u32[]{:S(2)}) collective-permute-start(bf16[2,17,16,128]{3,2,1,0:T(8,128)(2,1)S(1)} %pad_maximum_fusion.1), channel_id=1, source_target_pairs={{0,16},{1,17},{2,18},{3,19},{4,20},{5,21},{6,22},{7,23},{8,24},{9,... | collective-permute-start | bytes 417800 | tf_op jit(solution)/shard_map/ppermute | solution.py:253
  10.4 2.3 %collective-permute-done.xh = bf16[2,17,16,128]{3,2,1,0:T(8,128)(2,1)S(1)} collective-permute-done((bf16[2,17,16,128]{3,2,1,0:T(8,128)(2,1)S(1)}, bf16[2,17,16,128]{3,2,1,0:T(8,128)(2,1)S(1)}, u32[]{:S(2)}, u32[]{:S(2)}) %collective-permute-start) | collective-permute-done | bytes 139296 | tf_op jit(solution)/shard_map/ppermute | solution.py:253
  12.7 4.6 %collective-permute-start.1 = (bf16[9,16,128]{2,1,0:T(8,128)(2,1)S(1)}, bf16[9,16,128]{2,1,0:T(8,128)(2,1)S(1)}, u32[]{:S(2)}, u32[]{:S(2)}) collective-permute-start(bf16[9,16,128]{2,1,0:T(8,128)(2,1)S(1)} %pad_maximum_fusion.3), channel_id=1, source_target_pairs={{0,2},{1,3},{2,4},{3,5},{4,6},{5,7},{6,8},{7,9},{8,10},{9,11},{10,... | collective-permute-start | bytes 110600 | tf_op jit(solution)/shard_map/ppermute | solution.py:253
  17.3 2.3 %collective-permute-start.2 = (bf16[9,2,16,128]{3,0,2,1:T(8,128)(2,1)S(1)}, bf16[9,2,16,128]{3,0,2,1:T(8,128)(2,1)S(1)}, u32[]{:S(2)}, u32[]{:S(2)}) collective-permute-start(bf16[9,2,16,128]{3,0,2,1:T(8,128)(2,1)S(1)} %pad_maximum_fusion), channel_id=1, source_target_pairs={{0,1},{2,3},{4,5},{6,7},{8,9},{10,11},{12,13},{14,15},{16,17},{18,... | collective-permute-start | bytes 221192 | tf_op jit(solution)/shard_map/ppermute | solution.py:253
  19.7 1.3 collective-permute-start.3
  21.8 1.2 shard_map.102
  23.8 17.3 %all_to_all.35 = f32[32,3,128]{2,1,0:T(4,128)S(1)} all-to-all(f32[32,3,128]{2,1,0:T(4,128)S(1)} %get-tuple-element.23), channel_id=1, replica_groups=mesh['z'=8,'yh'=2,'x'=4,'c'=2,'yl'=2] {'yh','x','c','yl'}, dimensions={0} | all-to-all | bytes 98304 | tf_op jit(solution)/shard_map/all_to_all | solution.py:257
  41.3 15.3 %all_to_all.36 = f32[8,3,128]{2,1,0:T(4,128)S(1)} all-to-all(f32[8,3,128]{2,1,0:T(4,128)S(1)} %broadcast_in_dim.14), channel_id=1, replica_groups=mesh['z'=8,'yh'=2,'x'=4,'c'=2,'yl'=2] {'z'}, dimensions={0} | all-to-all | bytes 24576 | tf_op jit(solution)/shard_map/all_to_all | solution.py:257
  58.3 12.1 %all_to_all.37 = f32[32,2,128]{2,1,0:T(2,128)S(1)} all-to-all(f32[32,2,128]{2,1,0:T(2,128)S(1)} %get-tuple-element.26), channel_id=1, replica_groups=mesh['z'=8,'yh'=2,'x'=4,'c'=2,'yl'=2] {'yh','x','c','yl'}, dimensions={0} | all-to-all | bytes 65536 | tf_op jit(solution)/shard_map/all_to_all | solution.py:257
  70.4 8.9 %all_to_all.38 = f32[8,2,128]{2,1,0:T(2,128)S(1)} all-to-all(f32[8,2,128]{2,1,0:T(2,128)S(1)} %broadcast_in_dim.15), channel_id=1, replica_groups=mesh['z'=8,'yh'=2,'x'=4,'c'=2,'yl'=2] {'z'}, dimensions={0} | all-to-all | bytes 16384 | tf_op jit(solution)/shard_map/all_to_all | solution.py:257
  79.4 2.0 %shard_map.104 = (bf16[4,16,16,128]{3,2,1,0:T(8,128)(2,1)S(1)}, bf16[17,16,128]{2,1,0:T(8,128)(2,1)S(1)}, bf16[4,16,128]{2,1,0:T(8,128)(2,1)S(1)}, bf16[1792,128]{1,0:T(8,128)(2,1)}) custom-call(f32[4,16,16,128]{3,2,1,0:T(8,128)S(1)} %get-tuple-element.25.slope, f32[4,16,16,128]{3,2,1,0:T(8,128)S(1)} %get-tuple-element.22.pre, ...), custom_call_target="tpu_custom_call" | custom-call | flops 1200000000 | bytes 3420928 | tf_op jit(solution)/shard_map/pallas_call | solution.py:18
  81.5 5.4 %all-to-all-start.4 = ((bf16[32,56,128]{2,1,0:T(8,128)(2,1)}), bf16[32,56,128]{2,1,0:T(8,128)(2,1)S(1)}, u32[]{:S(2)}, u32[]{:S(2)}) async-start(bf16[32,56,128]{2,1,0:T(8,128)(2,1)} %bitcast.23), calls=%async_computation.4 | async-start | bytes 917504 | tf_op jit(solution)/shard_map/all_to_all | solution.py:257
  86.9 1.3 collective-permute-start.4
  88.2 9.1 %all-to-all-done.4 = bf16[32,56,128]{2,1,0:T(8,128)(2,1)S(1)} async-done(((bf16[32,56,128]{2,1,0:T(8,128)(2,1)}), bf16[32,56,128]{2,1,0:T(8,128)(2,1)S(1)}, u32[]{:S(2)}, u32[]{:S(2)}) %all-to-all-start.4) | async-done | bytes 458784 | tf_op jit(solution)/shard_map/all_to_all | solution.py:257
  98.1 3.4 %all-to-all-start.5 = ((f32[8,56,128]{2,1,0:T(8,128)}), f32[8,56,128]{2,1,0:T(8,128)S(1)}, u32[]{:S(2)}, u32[]{:S(2)}) async-start(f32[8,56,128]{2,1,0:T(8,128)} %broadcast_in_dim.16), calls=%async_computation.5 | async-start | bytes 458752 | tf_op jit(solution)/shard_map/all_to_all | solution.py:257
  101.6 1.4 %collective-permute-start.7 = (bf16[5,128]{1,0:T(8,128)(2,1)S(1)}, bf16[5,128]{1,0:T(8,128)(2,1)S(1)}, u32[]{:S(2)}, u32[]{:S(2)}) collective-permute-start(bf16[5,128]{1,0:T(8,128)(2,1)S(1)} %fusion.7), channel_id=1, source_target_pairs={{3,0},{5,2},{7,4},{9,6},{11,8},{13,10},{15,12},{19,16},{21,18},{23... | collective-permute-start | bytes 3848 | tf_op jit(solution)/shard_map/ppermute | solution.py:253
  103.0 3.4 %collective-permute-start.5 = (bf16[5,16,128]{2,1,0:T(8,128)(2,1)S(1)}, bf16[5,16,128]{2,1,0:T(8,128)(2,1)S(1)}, u32[]{:S(2)}, u32[]{:S(2)}) collective-permute-start(bf16[5,16,128]{2,1,0:T(8,128)(2,1)S(1)} %pad_maximum_fusion.4), channel_id=1, source_target_pairs={{2,0},{3,1},{4,2},{5,3},{6,4},{7,5},{8,6},{9,7},{10,8},{11,9},{12,... | collective-permute-start | bytes 61448 | tf_op jit(solution)/shard_map/ppermute | solution.py:253
  106.5 4.1 %all-to-all-done.5 = f32[8,56,128]{2,1,0:T(8,128)S(1)} async-done(((f32[8,56,128]{2,1,0:T(8,128)}), f32[8,56,128]{2,1,0:T(8,128)S(1)}, u32[]{:S(2)}, u32[]{:S(2)}) %all-to-all-start.5) | async-done | bytes 229408 | tf_op jit(solution)/shard_map/all_to_all | solution.py:257
  111.5 7.3 %all-to-all-start.6 = ((bf16[32,56,128]{2,1,0:T(8,128)(2,1)}), bf16[32,56,128]{2,1,0:T(8,128)(2,1)S(1)}, u32[]{:S(2)}, u32[]{:S(2)}) async-start(bf16[32,56,128]{2,1,0:T(8,128)(2,1)} %broadcast_in_dim.17), calls=%async_computation.6 | async-start | bytes 917504 | tf_op jit(solution)/shard_map/all_to_all | solution.py:257
  118.9 1.3 collective-permute-start.6
  120.7 5.0 %collective-permute-done.6 = bf16[5,16,128]{2,0,1:T(8,128)(2,1)S(1)} collective-permute-done((bf16[5,16,128]{2,0,1:T(8,128)(2,1)S(1)}, bf16[5,16,128]{2,0,1:T(8,128)(2,1)S(1)}, u32[]{:S(2)}, u32[]{:S(2)}) %collective-permute-start.6) | collective-permute-done | bytes 20512 | tf_op jit(solution)/shard_map/ppermute | solution.py:253
  125.7 2.4 %shard_map.105 = bf16[8,16,2,16,128]{4,3,2,1,0:T(8,128)(2,1)} custom-call(bf16[4,16,16,128]{3,2,1,0:T(8,128)(2,1)S(1)} %get-tuple-element.27.dpre, bf16[17,16,128]{2,1,0:T(8,128)(2,1)S(1)} %copy.70.xh, bf16[5,16,128]{2,1,0:T(8,128)(2,1)S(1)} %collective-permute-done.5.yh, bf16[5,16,128]{2,1,0:T(8,128)(2,1)S(1)} %copy.71.zh, ...), custom_call_target="tpu_custom_call" | custom-call | flops 1200000000 | bytes 3060992 | tf_op jit(solution)/shard_map/pallas_call | solution.py:18
  (76 shorter events, 8.8 us)
Async XLA Ops:
  0.6 1.2 copy-start
  1.9 0.9 copy-start.2
  4.5 17.2 %copy-start.3 = (bf16[8,2,16,16,128]{4,3,2,1,0:T(8,128)(2,1)}, bf16[8,2,16,16,128]{4,3,2,1,0:T(8,128)(2,1)S(1)}, u32[]{:S(2)}) copy-start(bf16[8,2,16,16,128]{4,3,2,1,0:T(8,128)(2,1)S(1)} %get-tuple-element.31.mask) | copy-start | bytes 3145732
  4.6 17.2 %copy-start.5 = (bf16[3,3,3,64,128]{4,3,2,1,0:T(8,128)(2,1)S(1)}, bf16[3,3,3,64,128]{4,3,2,1,0:T(8,128)(2,1)}, u32[]{:S(2)}) copy-start(bf16[3,3,3,64,128]{4,3,2,1,0:T(8,128)(2,1)} %weight.1) | copy-start | bytes 1327108
  4.6 8.1 %collective-permute-start = (bf16[2,17,16,128]{3,2,1,0:T(8,128)(2,1)S(1)}, bf16[2,17,16,128]{3,2,1,0:T(8,128)(2,1)S(1)}, u32[]{:S(2)}, u32[]{:S(2)}) collective-permute-start(bf16[2,17,16,128]{3,2,1,0:T(8,128)(2,1)S(1)} %pad_maximum_fusion.1), channel_id=1, source_target_pairs={{0,16},{1,17},{2,18},{3,19},{4,20},{5,21},{6,22},{7,23},{8,24},{9,... | collective-permute-start | bytes 417800 | tf_op jit(solution)/shard_map/ppermute | solution.py:253
  12.7 9.0 %collective-permute-start.1 = (bf16[9,16,128]{2,1,0:T(8,128)(2,1)S(1)}, bf16[9,16,128]{2,1,0:T(8,128)(2,1)S(1)}, u32[]{:S(2)}, u32[]{:S(2)}) collective-permute-start(bf16[9,16,128]{2,1,0:T(8,128)(2,1)S(1)} %pad_maximum_fusion.3), channel_id=1, source_target_pairs={{0,2},{1,3},{2,4},{3,5},{4,6},{5,7},{6,8},{7,9},{8,10},{9,11},{10,... | collective-permute-start | bytes 110600 | tf_op jit(solution)/shard_map/ppermute | solution.py:253
  17.3 4.4 %collective-permute-start.2 = (bf16[9,2,16,128]{3,0,2,1:T(8,128)(2,1)S(1)}, bf16[9,2,16,128]{3,0,2,1:T(8,128)(2,1)S(1)}, u32[]{:S(2)}, u32[]{:S(2)}) collective-permute-start(bf16[9,2,16,128]{3,0,2,1:T(8,128)(2,1)S(1)} %pad_maximum_fusion), channel_id=1, source_target_pairs={{0,1},{2,3},{4,5},{6,7},{8,9},{10,11},{12,13},{14,15},{16,17},{18,... | collective-permute-start | bytes 221192 | tf_op jit(solution)/shard_map/ppermute | solution.py:253
  19.7 2.1 %collective-permute-start.3 = (bf16[9,128]{1,0:T(8,128)(2,1)S(1)}, bf16[9,128]{1,0:T(8,128)(2,1)S(1)}, u32[]{:S(2)}, u32[]{:S(2)}) collective-permute-start(bf16[9,128]{1,0:T(8,128)(2,1)S(1)} %fusion.5), channel_id=1, source_target_pairs={{0,3},{2,5},{4,7},{6,9},{8,11},{10,13},{12,15},{16,19},{18,21},{20... | collective-permute-start | bytes 6920 | tf_op jit(solution)/shard_map/ppermute | solution.py:253
  23.0 0.8 copy-start.6
  23.8 33.5 %copy-start.1 = (bf16[4,16,16,128]{3,2,1,0:T(8,128)(2,1)S(1)}, bf16[4,16,16,128]{3,2,1,0:T(8,128)(2,1)}, u32[]{:S(2)}) copy-start(bf16[4,16,16,128]{3,2,1,0:T(8,128)(2,1)} %cot.1) | copy-start | bytes 786436
  56.7 0.7 copy-start.8
  56.7 0.7 copy-start.9
  81.5 15.9 %all-to-all-start.4 = ((bf16[32,56,128]{2,1,0:T(8,128)(2,1)}), bf16[32,56,128]{2,1,0:T(8,128)(2,1)S(1)}, u32[]{:S(2)}, u32[]{:S(2)}) async-start(bf16[32,56,128]{2,1,0:T(8,128)(2,1)} %bitcast.23), calls=%async_computation.4 | async-start | bytes 917504 | tf_op jit(solution)/shard_map/all_to_all | solution.py:257
  86.9 14.6 %collective-permute-start.4 = (bf16[17,16,128]{2,0,1:T(8,128)(2,1)S(1)}, bf16[17,16,128]{2,0,1:T(8,128)(2,1)S(1)}, u32[]{:S(2)}, u32[]{:S(2)}) collective-permute-start(bf16[17,16,128]{2,0,1:T(8,128)(2,1)S(1)} %copy.66), channel_id=1, source_target_pairs={{16,0},{17,1},{18,2},{19,3},{20,4},{21,5},{22,6},{23,7},{24,8},{25... | collective-permute-start | bytes 208904 | tf_op jit(solution)/shard_map/ppermute | solution.py:253
  98.1 12.5 %all-to-all-start.5 = ((f32[8,56,128]{2,1,0:T(8,128)}), f32[8,56,128]{2,1,0:T(8,128)S(1)}, u32[]{:S(2)}, u32[]{:S(2)}) async-start(f32[8,56,128]{2,1,0:T(8,128)} %broadcast_in_dim.16), calls=%async_computation.5 | async-start | bytes 458752 | tf_op jit(solution)/shard_map/all_to_all | solution.py:257
  101.5 24.2 %copy-start.4 = (bf16[8,2,16,16,128]{4,3,2,1,0:T(8,128)(2,1)S(1)}, bf16[8,2,16,16,128]{4,3,2,1,0:T(8,128)(2,1)}, u32[]{:S(2)}) copy-start(bf16[8,2,16,16,128]{4,3,2,1,0:T(8,128)(2,1)} %copy-done.3) | copy-start | bytes 3145732
  101.6 24.1 %collective-permute-start.7 = (bf16[5,128]{1,0:T(8,128)(2,1)S(1)}, bf16[5,128]{1,0:T(8,128)(2,1)S(1)}, u32[]{:S(2)}, u32[]{:S(2)}) collective-permute-start(bf16[5,128]{1,0:T(8,128)(2,1)S(1)} %fusion.7), channel_id=1, source_target_pairs={{3,0},{5,2},{7,4},{9,6},{11,8},{13,10},{15,12},{19,16},{21,18},{23... | collective-permute-start | bytes 3848 | tf_op jit(solution)/shard_map/ppermute | solution.py:253
  103.0 22.7 %collective-permute-start.5 = (bf16[5,16,128]{2,1,0:T(8,128)(2,1)S(1)}, bf16[5,16,128]{2,1,0:T(8,128)(2,1)S(1)}, u32[]{:S(2)}, u32[]{:S(2)}) collective-permute-start(bf16[5,16,128]{2,1,0:T(8,128)(2,1)S(1)} %pad_maximum_fusion.4), channel_id=1, source_target_pairs={{2,0},{3,1},{4,2},{5,3},{6,4},{7,5},{8,6},{9,7},{10,8},{11,9},{12,... | collective-permute-start | bytes 61448 | tf_op jit(solution)/shard_map/ppermute | solution.py:253
  111.5 14.2 %copy-start.7 = (bf16[1152,256]{1,0:T(8,128)(2,1)S(1)}, bf16[1152,256]{1,0:T(8,128)(2,1)}, u32[]{:S(2)}) copy-start(bf16[1152,256]{1,0:T(8,128)(2,1)} %copy-done.6) | copy-start | bytes 1769476
  111.5 17.6 %all-to-all-start.6 = ((bf16[32,56,128]{2,1,0:T(8,128)(2,1)}), bf16[32,56,128]{2,1,0:T(8,128)(2,1)S(1)}, u32[]{:S(2)}, u32[]{:S(2)}) async-start(bf16[32,56,128]{2,1,0:T(8,128)(2,1)} %broadcast_in_dim.17), calls=%async_computation.6 | async-start | bytes 917504 | tf_op jit(solution)/shard_map/all_to_all | solution.py:257
  118.9 6.9 %collective-permute-start.6 = (bf16[5,16,128]{2,0,1:T(8,128)(2,1)S(1)}, bf16[5,16,128]{2,0,1:T(8,128)(2,1)S(1)}, u32[]{:S(2)}, u32[]{:S(2)}) collective-permute-start(bf16[5,16,128]{2,0,1:T(8,128)(2,1)S(1)} %pad_maximum_fusion.2), channel_id=1, source_target_pairs={{1,0},{3,2},{5,4},{7,6},{9,8},{11,10},{13,12},{15,14},{17,16},{19,... | collective-permute-start | bytes 61448 | tf_op jit(solution)/shard_map/ppermute | solution.py:253

commit v3 on v2

--- a/solution.py
+++ b/solution.py
@@ -48,22 +48,39 @@
     return jnp.where(q == at, jnp.broadcast_to(edge[:, None, :], value.shape), moved)
 
 
+def masked_row(feat, active):
+    ny, mz, width = feat.shape
+    z = active.shape[1]
+    pair = lax.broadcasted_iota(jnp.int32, (mz, z), 1) // 2
+    sel = (pair == lax.broadcasted_iota(jnp.int32, (mz, z), 0)).astype(F32)
+    lane = lax.broadcasted_iota(jnp.int32, (z, width), 1) // (width // 2)
+    widen = (lax.broadcasted_iota(jnp.int32, (z, width), 0) % 2 == lane).astype(BF)
+    rep = jnp.broadcast_to(active.astype(F32)[:, None, :], (ny, mz, z)) * sel[None]
+    m = dot(rep.astype(BF).reshape(ny * mz, z), widen).astype(BF)
+    m = m.reshape(ny // 2, 2, mz, width)
+    return m, feat.reshape(ny // 2, 2, mz, width) * m
+
+
+def face_kernel(feat, active, pack):
+    _, slabs, mz, width = pack.shape
+    my = slabs - 1
+    last = lax.axis_size("z") * lax.axis_size("yh") - 1
+    here = lax.axis_index("z") * lax.axis_size("yh") + lax.axis_index("yh")
+    keep = jnp.where(here == last, 0.0, 1.0)
+    _, value = masked_row(feat[0], active[0])
+    pick = row_picker(my, mz, mz - 1)
+    for py in range(2):
+        held = (value[:, py].astype(F32) * keep).astype(BF)
+        pack[py, :my] = held
+        pack[py, my] = dot(pick, held.reshape(my * mz, width)).astype(BF)
+
+
 def mask_kernel(feat, active, xin, mask, act, zface):
     nx, _, my, mz, width = xin.shape
-    z = active.shape[2]
-    sel = (
-        lax.broadcasted_iota(jnp.int32, (mz, z), 1) // 2 == lax.broadcasted_iota(jnp.int32, (mz, z), 0)
-    ).astype(F32)
-    lane = lax.broadcasted_iota(jnp.int32, (z, width), 1) // (width // 2)
-    spread = (lax.broadcasted_iota(jnp.int32, (z, width), 0) % 2 == lane).astype(BF)
     pick = row_picker(my, mz, mz - 1)
     count = None
     for x in range(nx):
-        a = active[x].astype(F32)
-        rep = jnp.broadcast_to(a[:, None, :], (2 * my, mz, z)) * sel[None]
-        m = dot(rep.astype(BF).reshape(2 * my * mz, z), spread).astype(BF)
-        m = m.reshape(my, 2, mz, width)
-        value = feat[x].reshape(my, 2, mz, width) * m
+        m, value = masked_row(feat[x], active[x])
         for py in range(2):
             part = m[:, py]
             mask[x, py] = part
@@ -87,11 +104,12 @@
     return base
 
 
-def edge_of(zh, ch, row, b):
-    base = zh[row, 0 if b == 1 else 1]
+def edge_of(zh, row, b):
+    base = zh[2 * row + (0 if b == 1 else 1)]
     if b == 0:
         wide = base.astype(F32)
-        wide = jnp.concatenate([ch[row : row + 1].astype(F32), wide[: wide.shape[0] - 1]], axis=0)
+        first = zh[zh.shape[0] - 1].astype(F32)[row : row + 1]
+        wide = jnp.concatenate([first, wide[: wide.shape[0] - 1]], axis=0)
         base = wide.astype(BF)
     return base
 
@@ -99,7 +117,7 @@
 TAPS = [(a, b) for a in range(3) for b in range(3)]
 
 
-def forward_kernel(xin, act, xh, yh, zh, ch, weight, pre, stats, wmat):
+def forward_kernel(xin, act, xh, yh, zh, weight, pre, stats, wmat):
     mx, my, mz, cout = pre.shape
     width = xin.shape[4]
     half = width // 2
@@ -118,7 +136,7 @@
         left = jnp.concatenate(
             [tile_of(xin, xh, yh, 2 * m + a, b).reshape(rows, width) for a, b in TAPS], axis=1
         )
-        edge = jnp.concatenate([edge_of(zh, ch, 2 * m + a, b) for a, b in TAPS], axis=1)
+        edge = jnp.concatenate([edge_of(zh, 2 * m + a, b) for a, b in TAPS], axis=1)
         out = dot(left, w)
         rim = dot(edge, w[:, cout:])
         prev = with_edge(out[:, cout:].reshape(my, mz, cout), rim, 0, 1)
@@ -160,7 +178,7 @@
         sums[i, 1:2] = second
 
 
-def weight_kernel(slope, pre, act, par, xin, xh, yh, zh, ch, dpre, pack, zface, dw):
+def weight_kernel(slope, pre, act, par, xin, xh, yh, zh, dpre, pack, zface, dw):
     mx, my, mz, cout = pre.shape
     width = xin.shape[4]
     half = width // 2
@@ -179,8 +197,10 @@
         first = dot(pick, held)
         zface[m] = first.astype(BF)
         if m == 0:
-            pack[:my] = held.reshape(my, mz, cout)
-            pack[my] = first.astype(BF)
+            here = lax.axis_index("z") * lax.axis_size("yh") + lax.axis_index("yh")
+            keep = jnp.where(here == 0, 0.0, 1.0)
+            pack[:my] = (held.astype(F32) * keep).astype(BF).reshape(my, mz, cout)
+            pack[my] = (first * keep).astype(BF)
         rims.append(first)
         wide = held.astype(F32)
         after = pltpu.roll(wide, rows - 1, 0).reshape(my, mz, cout)
@@ -194,7 +214,7 @@
     rim = jnp.concatenate(rims, axis=0).T.astype(BF)
     edge = jnp.concatenate(
         [
-            jnp.concatenate([edge_of(zh, ch, 2 * m + a, b) for a, b in TAPS], axis=1)
+            jnp.concatenate([edge_of(zh, 2 * m + a, b) for a, b in TAPS], axis=1)
             for m in range(mx)
         ],
         axis=0,
@@ -211,7 +231,7 @@
         dw[used:] = jnp.zeros((dw.shape[0] - used, cout), BF)
 
 
-def input_kernel(dpre, xh, yh, zh, ch, wmat, mask, out, ext, nxt):
+def input_kernel(dpre, xh, yh, zh, wmat, mask, out, ext, nxt):
     mx, my, mz, cout = dpre.shape
     width = mask.shape[4]
     rows = my * mz
@@ -220,7 +240,7 @@
         ext[r, :my] = base
         ext[r, my] = yh[r]
         whole = jnp.concatenate([base, yh[r][None]], axis=0).astype(F32)
-        rim = jnp.concatenate([zh[r].astype(F32), ch[r : r + 1].astype(F32)], axis=0)
+        rim = jnp.concatenate([zh[r].astype(F32), zh[mx + 1].astype(F32)[r : r + 1]], axis=0)
         nxt[r] = with_edge(whole, rim, mz - 1, -1).astype(BF)
     taps = (((1, 0),), ((2, 0), (0, 1)))
     for m in range(mx):
@@ -241,16 +261,22 @@
                 out[x, :, py] = value.astype(BF).reshape(my, mz, width)
 
 
-def moved(value, sizes, by):
-    nx, ny, nz = sizes
-    pairs = []
-    for i in range(nx):
-        for j in range(ny):
-            for k in range(nz):
-                i2, j2, k2 = (i + by[0], j + by[1], k + by[2])
-                if 0 <= i2 < nx and 0 <= j2 < ny and 0 <= k2 < nz:
-                    pairs.append(((i * ny + j) * nz + k, (i2 * ny + j2) * nz + k2))
-    return lax.ppermute(value, ALL, pairs)
+def moved(value, axes, by):
+    count = lax.axis_size(axes)
+    return lax.ppermute(value, axes, [(i, (i + by) % count) for i in range(count)])
+
+
+GX, GY, GZ = (("z", "yh"), ("x", "c"), ("yl",))
+
+
+def beyond(value, axes, by):
+    end = lax.axis_size(axes) - 1 if by > 0 else 0
+    keep = (lax.axis_index(axes) != end).astype(value.dtype)
+    return moved(value * keep, axes, by)
+
+
+def slab(rows, like):
+    return jnp.pad(rows, ((0, like - rows.shape[0]), (0, 0)))[None]
 
 
 def exchanged(value, axes):
@@ -270,12 +296,25 @@
     return jnp.stack([count, total, jnp.sum(squares + counts * apart * apart, axis=0)])
 
 
-def local(sizes, features, active, weight, gain, bias, cotangent):
+def local(features, active, weight, gain, bias, cotangent):
     vx, vy, mz, width = features.shape
     cin = width // 2
     cout = weight.shape[4]
     mx, my = (vx // 2, vy // 2)
     near = lax.axis_size(NEAR)
+    pack = pl.pallas_call(
+        face_kernel,
+        out_shape=shape((2, my + 1, mz, width), BF),
+        grid=(1,),
+        in_specs=[
+            pl.BlockSpec((1, vy, mz, width), lambda i: (0, 0, 0, 0)),
+            pl.BlockSpec((1, vy, 2 * mz), lambda i: (0, 0, 0)),
+        ],
+        out_specs=pl.BlockSpec((2, my + 1, mz, width), lambda i: (0, 0, 0, 0)),
+        compiler_params=PARAMS,
+        cost_estimate=pl.CostEstimate(flops=10_000_000, bytes_accessed=400_000, transcendentals=0),
+    )(features[vx - 1 :], active[vx - 1 :])
+    xh = moved(pack, GX, 1)
     xin, mask, act, zface = call(
         mask_kernel,
         [
@@ -286,14 +325,12 @@
         ],
         [features, active],
     )
-    pack = jnp.concatenate([xin[vx - 1], zface[vx - 1][:, None]], axis=1)
-    xh = moved(pack, sizes, (1, 0, 0))
     yface = jnp.concatenate([xh[1:2, my - 1], xin[:, 1, my - 1]], axis=0)
     zfaces = jnp.concatenate([xh[None, :, my], zface], axis=0)
-    corner = zfaces[:, 1, my - 1]
-    yh = moved(yface, sizes, (0, 1, 0))
-    zh = moved(zfaces, sizes, (0, 0, 1))
-    ch = moved(corner, sizes, (0, 1, 1))
+    rows = vx + 1
+    yh = beyond(jnp.concatenate([yface, slab(zfaces[:, 1, my - 1], mz)], axis=0), GY, 1)
+    zfaces = jnp.concatenate([zfaces.reshape(2 * rows, my, width), yh[rows:]], axis=0)
+    zh = beyond(zfaces, GZ, 1)
     pre, stats, wmat = call(
         forward_kernel,
         [
@@ -301,7 +338,7 @@
             shape((near, 3, cout), F32),
             shape((9 * width, 2 * cout), BF),
         ],
-        [xin, act, xh, yh, zh, ch, weight],
+        [xin, act, xh, yh, zh, weight],
         flops=1_200_000_000,
     )
     stats = merged(spread(merged(exchanged(stats, NEAR)), FAR))
@@ -334,22 +371,22 @@
             shape((mx, my, cout), BF),
             shape((near * rows, cout), BF),
         ],
-        [slope, pre, act, par, xin, xh, yh, zh, ch],
+        [slope, pre, act, par, xin, xh, yh, zh],
         flops=1_200_000_000,
     )
-    xd = moved(pack, sizes, (-1, 0, 0))
+    xd = moved(pack, GX, -1)
     mine = jnp.sum(exchanged(dw.reshape(near, rows, cout), NEAR).astype(F32), axis=0)
     zfaces = jnp.concatenate([zface, xd[my:]], axis=0)
-    yd = moved(jnp.concatenate([dpre[:, 0], xd[:1]], axis=0), sizes, (0, -1, 0))
-    zd = moved(zfaces, sizes, (0, 0, -1))
-    cd = moved(zfaces[:, 0], sizes, (0, -1, -1))
+    yd = jnp.concatenate([dpre[:, 0], xd[:1], slab(zfaces[:, 0], mz)], axis=0)
+    yd = beyond(yd, GY, -1)
+    zd = beyond(jnp.concatenate([zfaces, yd[mx + 1 :]], axis=0), GZ, -1)
     mine = jnp.sum(spread(mine, FAR), axis=0) / count[0]
     grad_weight = spread(mine.astype(BF), NEAR).reshape(near * rows, cout)[:taps]
     grad_weight = grad_weight.astype(F32).reshape(weight.shape)
     (grad_features,) = call(
         input_kernel,
         [shape((vx, my, 2, mz, width), BF)],
-        [dpre, xd, yd, zd, cd, wmat, mask],
+        [dpre, xd, yd, zd, wmat, mask],
         scratch=[pltpu.VMEM((mx + 1, my + 1, mz, cout), BF)] * 2,
         flops=1_200_000_000,
     )
@@ -363,8 +400,4 @@
     block = (("z", "yh"), ("x", "c"), "yl")
     in_specs = (P(*block, None), P(*block), P(), P(), P(), P(*block, None))
     out_specs = (P(*block, None), P(*block, None), P(), P(), P())
-
-    def body(*args):
-        return local((gx, gy, gz), *args)
-
-    return jax.shard_map(body, mesh=fine, in_specs=in_specs, out_specs=out_specs, check_vma=False)
+    return jax.shard_map(local, mesh=fine, in_specs=in_specs, out_specs=out_specs, check_vma=False)

time: 131 us -> 126 us (0.962)
  starting transfers between devices: 37.5 us -> 29.8 us
  waiting for transfers between devices: 22.1 us -> 29.2 us
  blocking collectives: 53.6 us -> 47.4 us
  local copies, waits for them, and re-layouts: 5.41 us -> 7.16 us
    ppermute x8 -> x6, starting transfers between devices: 21.4 us -> 12.6 us  [moved(): lax.ppermute(value, axes, [(i, (i + by) % count) for i in range(count)])]
    all_to_all x4, blocking collectives: 53.6 us -> 47.4 us  [exchanged(): return lax.all_to_all(value, axes, 0, 0)]
    ppermute x8 -> x6, waiting for transfers between devices: 8.02 us -> 12.4 us  [moved(): lax.ppermute(value, axes, [(i, (i + by) % count) for i in range(count)])]
    all_to_all x3, waiting for transfers between devices: 14.1 us -> 16.8 us  [exchanged(): return lax.all_to_all(value, axes, 0, 0)]
    slice x1 -> x7, local copies, waits for them, and re-layouts: 0.01 us -> 1.66 us  [the longest x1 0.91 us: local(): features[vx - 1:]]
    unnamed x20 -> x24, local copies, waits for them, and re-layouts: 3.62 us -> 3.71 us
  transfers between devices with their start and end apart: 11 -> 9, of which waited for: 6 -> 8; matrix products, arithmetic and copies ran while one was open for 2% -> 1% of each run, Pallas kernels for 2% -> 3%
where the time goes in v3:
time: 126 us; the launch traced here: 125 us
  blocking collectives  47.4 us (38%)
  starting transfers between devices  29.8 us (24%)
  waiting for transfers between devices  29.2 us (23%)
  Pallas kernels  8.65 us (7%)
  local copies, waits for them, and re-layouts  7.16 us (6%)
  other arithmetic  2.02 us (2%)
    all_to_all x4, blocking collectives, exchanged(): return lax.all_to_all(value, axes, 0, 0)  47.4 us
    all_to_all x3, starting transfers between devices, exchanged(): return lax.all_to_all(value, axes, 0, 0)  17.2 us
    all_to_all x3, waiting for transfers between devices, exchanged(): return lax.all_to_all(value, axes, 0, 0)  16.8 us
    ppermute x6, starting transfers between devices, moved(): lax.ppermute(value, axes, [(i, (i + by) % count) for i in range(count)])  12.6 us
    ppermute x6, waiting for transfers between devices, moved(): lax.ppermute(value, axes, [(i, (i + by) % count) for i in range(count)])  12.4 us
    pallas_call x5, Pallas kernels, call(): pl.pallas_call(kernel, out_shape=outs, in_specs=[pl.BlockSpec(memory_spac...  8.33 us
    unnamed x24, local copies, waits for them, and re-layouts  3.71 us
  transfers between devices with their start and end apart: 9, of which 8 were waited for; matrix products, arithmetic and copies ran while one was open for 1% of the time, Pallas kernels for 3%

profile of v3, /device:TPU:1, one launch (start us, length us, event | category | flops | bytes accessed | tf_op | source)
XLA Modules:
  0.0 125.2 jit_solution(11698403072631714501)
XLA Ops:
  2.6 3.8 %collective-permute-start = (bf16[2,17,16,128]{3,2,1,0:T(8,128)(2,1)S(1)}, bf16[2,17,16,128]{3,2,1,0:T(8,128)(2,1)S(1)}, u32[]{:S(2)}, u32[]{:S(2)}) collective-permute-start(bf16[2,17,16,128]{3,2,1,0:T(8,128)(2,1)S(1)} %shard_map.102), channel_id=1, source_target_pairs={{0,16},{16,32},{32,48},{48,64},{64,80},{80,96},{96,112},{112,128},... | collective-permute-start | bytes 417800 | tf_op jit(solution)/shard_map/ppermute | solution.py:266
  6.4 1.2 copy-done
  7.6 1.8 %shard_map.101 = (bf16[8,2,16,16,128]{4,3,2,1,0:T(8,128)(2,1)S(1)}, bf16[8,2,16,16,128]{4,3,2,1,0:T(8,128)(2,1)S(1)}, bf16[4,16,16,128]{3,2,1,0:T(8,128)(2,1)S(1)}, bf16[8,2,16,128]{3,2,1,0:T(8,128)(2,1)S(1)}) custom-call(bf16[8,32,16,128]{3,2,1,0:T(8,128)(2,1)S(1)} %copy-done, s32[8,32,32]{2,1,0:T(8,128)S(1)} %copy-done.2), custom_call_target="tpu_custom_call" | custom-call | flops 100000000 | bytes 3506176 | tf_op jit(solution)/shard_map/pallas_call | solution.py:18
  10.4 4.7 %collective-permute-done.xh = bf16[2,17,16,128]{3,2,1,0:T(8,128)(2,1)S(1)} collective-permute-done((bf16[2,17,16,128]{3,2,1,0:T(8,128)(2,1)S(1)}, bf16[2,17,16,128]{3,2,1,0:T(8,128)(2,1)S(1)}, u32[]{:S(2)}, u32[]{:S(2)}) %collective-permute-start) | collective-permute-done | bytes 139296 | tf_op jit(solution)/shard_map/ppermute | solution.py:266
  15.1 2.3 %collective-permute-start.1 = (bf16[10,16,128]{2,1,0:T(8,128)(2,1)S(1)}, bf16[10,16,128]{2,1,0:T(8,128)(2,1)S(1)}, u32[]{:S(2)}, u32[]{:S(2)}) collective-permute-start(bf16[10,16,128]{2,1,0:T(8,128)(2,1)S(1)} %maximum_multiply_fusion.1), channel_id=1, source_target_pairs={{0,2},{2,4},{4,6},{6,8},{8,10},{10,12},{12,14},{14,0},{1,3},{3,5},... | collective-permute-start | bytes 122888 | tf_op jit(solution)/shard_map/ppermute | solution.py:266
  19.1 2.9 %collective-permute-done.2.zh = bf16[19,16,128]{2,1,0:T(8,128)(2,1)S(1)} collective-permute-done((bf16[19,16,128]{2,1,0:T(8,128)(2,1)S(1)}, bf16[19,16,128]{2,1,0:T(8,128)(2,1)S(1)}, u32[]{:S(2)}, u32[]{:S(2)}) %collective-permute-start.2) | collective-permute-done | bytes 77856 | tf_op jit(solution)/shard_map/ppermute | solution.py:266
  21.9 1.2 shard_map.103
  24.0 14.0 %all_to_all.35 = f32[32,3,128]{2,1,0:T(4,128)S(1)} all-to-all(f32[32,3,128]{2,1,0:T(4,128)S(1)} %get-tuple-element.23), channel_id=1, replica_groups=mesh['z'=8,'yh'=2,'x'=4,'c'=2,'yl'=2] {'yh','x','c','yl'}, dimensions={0} | all-to-all | bytes 98304 | tf_op jit(solution)/shard_map/all_to_all | solution.py:283
  38.2 12.4 %all_to_all.36 = f32[8,3,128]{2,1,0:T(4,128)S(1)} all-to-all(f32[8,3,128]{2,1,0:T(4,128)S(1)} %broadcast_in_dim.21), channel_id=1, replica_groups=mesh['z'=8,'yh'=2,'x'=4,'c'=2,'yl'=2] {'z'}, dimensions={0} | all-to-all | bytes 24576 | tf_op jit(solution)/shard_map/all_to_all | solution.py:283
  52.2 12.1 %all_to_all.37 = f32[32,2,128]{2,1,0:T(2,128)S(1)} all-to-all(f32[32,2,128]{2,1,0:T(2,128)S(1)} %get-tuple-element.26), channel_id=1, replica_groups=mesh['z'=8,'yh'=2,'x'=4,'c'=2,'yl'=2] {'yh','x','c','yl'}, dimensions={0} | all-to-all | bytes 65536 | tf_op jit(solution)/shard_map/all_to_all | solution.py:283
  64.4 8.9 %all_to_all.38 = f32[8,2,128]{2,1,0:T(2,128)S(1)} all-to-all(f32[8,2,128]{2,1,0:T(2,128)S(1)} %broadcast_in_dim.22), channel_id=1, replica_groups=mesh['z'=8,'yh'=2,'x'=4,'c'=2,'yl'=2] {'z'}, dimensions={0} | all-to-all | bytes 16384 | tf_op jit(solution)/shard_map/all_to_all | solution.py:283
  73.4 2.0 %shard_map.105 = (bf16[4,16,16,128]{3,2,1,0:T(8,128)(2,1)S(1)}, bf16[17,16,128]{2,1,0:T(8,128)(2,1)S(1)}, bf16[4,16,128]{2,1,0:T(8,128)(2,1)S(1)}, bf16[1792,128]{1,0:T(8,128)(2,1)}) custom-call(f32[4,16,16,128]{3,2,1,0:T(8,128)S(1)} %get-tuple-element.25.slope, f32[4,16,16,128]{3,2,1,0:T(8,128)S(1)} %get-tuple-element.22.pre, ...), custom_call_target="tpu_custom_call" | custom-call | flops 1200000000 | bytes 3426816 | tf_op jit(solution)/shard_map/pallas_call | solution.py:18
  75.4 5.4 %all-to-all-start.4 = ((bf16[32,56,128]{2,1,0:T(8,128)(2,1)}), bf16[32,56,128]{2,1,0:T(8,128)(2,1)S(1)}, u32[]{:S(2)}, u32[]{:S(2)}) async-start(bf16[32,56,128]{2,1,0:T(8,128)(2,1)} %bitcast.24), calls=%async_computation.4 | async-start | bytes 917504 | tf_op jit(solution)/shard_map/all_to_all | solution.py:283
  80.9 3.0 %collective-permute-start.3 = (bf16[17,16,128]{2,0,1:T(8,128)(2,1)S(1)}, bf16[17,16,128]{2,0,1:T(8,128)(2,1)S(1)}, u32[]{:S(2)}, u32[]{:S(2)}) collective-permute-start(bf16[17,16,128]{2,0,1:T(8,128)(2,1)S(1)} %copy.61), channel_id=1, source_target_pairs={{0,240},{16,0},{32,16},{48,32},{64,48},{80,64},{96,80},{112,96},{1... | collective-permute-start | bytes 208904 | tf_op jit(solution)/shard_map/ppermute | solution.py:266
  84.0 7.3 %all-to-all-done.4 = bf16[32,56,128]{2,1,0:T(8,128)(2,1)S(1)} async-done(((bf16[32,56,128]{2,1,0:T(8,128)(2,1)}), bf16[32,56,128]{2,1,0:T(8,128)(2,1)S(1)}, u32[]{:S(2)}, u32[]{:S(2)}) %all-to-all-start.4) | async-done | bytes 458784 | tf_op jit(solution)/shard_map/all_to_all | solution.py:283
  92.1 3.4 %all-to-all-start.5 = ((f32[8,56,128]{2,1,0:T(8,128)}), f32[8,56,128]{2,1,0:T(8,128)S(1)}, u32[]{:S(2)}, u32[]{:S(2)}) async-start(f32[8,56,128]{2,1,0:T(8,128)} %broadcast_in_dim.24), calls=%async_computation.5 | async-start | bytes 458752 | tf_op jit(solution)/shard_map/all_to_all | solution.py:283
  95.6 1.5 %collective-permute-start.4 = (bf16[6,16,128]{2,1,0:T(8,128)(2,1)S(1)}, bf16[6,16,128]{2,1,0:T(8,128)(2,1)S(1)}, u32[]{:S(2)}, u32[]{:S(2)}) collective-permute-start(bf16[6,16,128]{2,1,0:T(8,128)(2,1)S(1)} %maximum_multiply_fusion.2), channel_id=1, source_target_pairs={{0,14},{2,0},{4,2},{6,4},{8,6},{10,8},{12,10},{14,12},{1,15},{3,1}... | collective-permute-start | bytes 73736 | tf_op jit(solution)/shard_map/ppermute | solution.py:266
  97.1 1.9 %collective-permute-done.4.yh = bf16[6,16,128]{2,1,0:T(8,128)(2,1)S(1)} collective-permute-done((bf16[6,16,128]{2,1,0:T(8,128)(2,1)S(1)}, bf16[6,16,128]{2,1,0:T(8,128)(2,1)S(1)}, u32[]{:S(2)}, u32[]{:S(2)}) %collective-permute-start.4) | collective-permute-done | bytes 24608 | tf_op jit(solution)/shard_map/ppermute | solution.py:266
  99.0 5.6 %all-to-all-done.5 = f32[8,56,128]{2,1,0:T(8,128)S(1)} async-done(((f32[8,56,128]{2,1,0:T(8,128)}), f32[8,56,128]{2,1,0:T(8,128)S(1)}, u32[]{:S(2)}, u32[]{:S(2)}) %all-to-all-start.5) | async-done | bytes 229408 | tf_op jit(solution)/shard_map/all_to_all | solution.py:283
  105.5 8.4 %all-to-all-start.6 = ((bf16[32,56,128]{2,1,0:T(8,128)(2,1)}), bf16[32,56,128]{2,1,0:T(8,128)(2,1)S(1)}, u32[]{:S(2)}, u32[]{:S(2)}) async-start(bf16[32,56,128]{2,1,0:T(8,128)(2,1)} %broadcast_in_dim.25), calls=%async_computation.6 | async-start | bytes 917504 | tf_op jit(solution)/shard_map/all_to_all | solution.py:283
  113.9 1.5 %collective-permute-start.5 = (bf16[6,16,128]{2,1,0:T(8,128)(2,1)S(1)}, bf16[6,16,128]{2,1,0:T(8,128)(2,1)S(1)}, u32[]{:S(2)}, u32[]{:S(2)}) collective-permute-start(bf16[6,16,128]{2,1,0:T(8,128)(2,1)S(1)} %maximum_multiply_fusion.3), channel_id=1, source_target_pairs={{0,1},{1,0},{2,3},{3,2},{4,5},{5,4},{6,7},{7,6},{8,9},{9,8},{10,11... | collective-permute-start | bytes 73736 | tf_op jit(solution)/shard_map/ppermute | solution.py:266
  115.9 2.0 %collective-permute-done.5.zh = bf16[6,16,128]{2,1,0:T(8,128)(2,1)S(1)} collective-permute-done((bf16[6,16,128]{2,1,0:T(8,128)(2,1)S(1)}, bf16[6,16,128]{2,1,0:T(8,128)(2,1)S(1)}, u32[]{:S(2)}, u32[]{:S(2)}) %collective-permute-start.5) | collective-permute-done | bytes 24608 | tf_op jit(solution)/shard_map/ppermute | solution.py:266
  117.9 2.4 %shard_map.106 = bf16[8,16,2,16,128]{4,3,2,1,0:T(8,128)(2,1)} custom-call(bf16[4,16,16,128]{3,2,1,0:T(8,128)(2,1)S(1)} %get-tuple-element.27.dpre, bf16[17,16,128]{2,1,0:T(8,128)(2,1)S(1)} %copy.66.xh, bf16[6,16,128]{2,1,0:T(8,128)(2,1)S(1)} %copy-done.4, bf16[6,16,128]{2,1,0:T(8,128)(2,1)S(1)} %collective-permute-done.5.zh, ...), custom_call_target="tpu_custom_call" | custom-call | flops 1200000000 | bytes 3067904 | tf_op jit(solution)/shard_map/pallas_call | solution.py:18
  120.3 3.9 %all-to-all-done.6 = bf16[32,56,128]{2,1,0:T(8,128)(2,1)S(1)} async-done(((bf16[32,56,128]{2,1,0:T(8,128)(2,1)}), bf16[32,56,128]{2,1,0:T(8,128)(2,1)S(1)}, u32[]{:S(2)}, u32[]{:S(2)}) %all-to-all-start.6) | async-done | bytes 458784 | tf_op jit(solution)/shard_map/all_to_all | solution.py:283
  (82 shorter events, 10.7 us)
Async XLA Ops:
  2.3 4.1 %copy-start.2 = (s32[8,32,32]{2,1,0:T(8,128)S(1)}, s32[8,32,32]{2,1,0:T(8,128)}, u32[]{:S(2)}) copy-start(s32[8,32,32]{2,1,0:T(8,128)} %active.1) | copy-start | bytes 98308
  2.6 12.4 %collective-permute-start = (bf16[2,17,16,128]{3,2,1,0:T(8,128)(2,1)S(1)}, bf16[2,17,16,128]{3,2,1,0:T(8,128)(2,1)S(1)}, u32[]{:S(2)}, u32[]{:S(2)}) collective-permute-start(bf16[2,17,16,128]{3,2,1,0:T(8,128)(2,1)S(1)} %shard_map.102), channel_id=1, source_target_pairs={{0,16},{16,32},{32,48},{48,64},{64,80},{80,96},{96,112},{112,128},... | collective-permute-start | bytes 417800 | tf_op jit(solution)/shard_map/ppermute | solution.py:266
  6.4 1.2 copy-start
  9.3 1.0 copy-start.5
  10.3 11.6 %copy-start.7 = (bf16[3,3,3,64,128]{4,3,2,1,0:T(8,128)(2,1)S(1)}, bf16[3,3,3,64,128]{4,3,2,1,0:T(8,128)(2,1)}, u32[]{:S(2)}) copy-start(bf16[3,3,3,64,128]{4,3,2,1,0:T(8,128)(2,1)} %weight.1) | copy-start | bytes 1327108
  15.1 3.4 %collective-permute-start.1 = (bf16[10,16,128]{2,1,0:T(8,128)(2,1)S(1)}, bf16[10,16,128]{2,1,0:T(8,128)(2,1)S(1)}, u32[]{:S(2)}, u32[]{:S(2)}) collective-permute-start(bf16[10,16,128]{2,1,0:T(8,128)(2,1)S(1)} %maximum_multiply_fusion.1), channel_id=1, source_target_pairs={{0,2},{2,4},{4,6},{6,8},{8,10},{10,12},{12,14},{14,0},{1,3},{3,5},... | collective-permute-start | bytes 122888 | tf_op jit(solution)/shard_map/ppermute | solution.py:266
  18.6 3.3 %collective-permute-start.2 = (bf16[19,16,128]{2,1,0:T(8,128)(2,1)S(1)}, bf16[19,16,128]{2,1,0:T(8,128)(2,1)S(1)}, u32[]{:S(2)}, u32[]{:S(2)}) collective-permute-start(bf16[19,16,128]{2,1,0:T(8,128)(2,1)S(1)} %maximum_multiply_fusion), channel_id=1, source_target_pairs={{0,1},{1,0},{2,3},{3,2},{4,5},{5,4},{6,7},{7,6},{8,9},{9,8},{10,11... | collective-permute-start | bytes 233480 | tf_op jit(solution)/shard_map/ppermute | solution.py:266
  23.2 0.8 copy-start.8
  24.0 27.4 %copy-start.1 = (bf16[4,16,16,128]{3,2,1,0:T(8,128)(2,1)S(1)}, bf16[4,16,16,128]{3,2,1,0:T(8,128)(2,1)}, u32[]{:S(2)}) copy-start(bf16[4,16,16,128]{3,2,1,0:T(8,128)(2,1)} %cot.1) | copy-start | bytes 786436
  50.6 0.7 copy-start.10
  50.7 0.7 copy-start.11
  75.4 15.9 %all-to-all-start.4 = ((bf16[32,56,128]{2,1,0:T(8,128)(2,1)}), bf16[32,56,128]{2,1,0:T(8,128)(2,1)S(1)}, u32[]{:S(2)}, u32[]{:S(2)}) async-start(bf16[32,56,128]{2,1,0:T(8,128)(2,1)} %bitcast.24), calls=%async_computation.4 | async-start | bytes 917504 | tf_op jit(solution)/shard_map/all_to_all | solution.py:283
  80.9 14.6 %collective-permute-start.3 = (bf16[17,16,128]{2,0,1:T(8,128)(2,1)S(1)}, bf16[17,16,128]{2,0,1:T(8,128)(2,1)S(1)}, u32[]{:S(2)}, u32[]{:S(2)}) collective-permute-start(bf16[17,16,128]{2,0,1:T(8,128)(2,1)S(1)} %copy.61), channel_id=1, source_target_pairs={{0,240},{16,0},{32,16},{48,32},{64,48},{80,64},{96,80},{112,96},{1... | collective-permute-start | bytes 208904 | tf_op jit(solution)/shard_map/ppermute | solution.py:266
  92.1 12.5 %all-to-all-start.5 = ((f32[8,56,128]{2,1,0:T(8,128)}), f32[8,56,128]{2,1,0:T(8,128)S(1)}, u32[]{:S(2)}, u32[]{:S(2)}) async-start(f32[8,56,128]{2,1,0:T(8,128)} %broadcast_in_dim.24), calls=%async_computation.5 | async-start | bytes 458752 | tf_op jit(solution)/shard_map/all_to_all | solution.py:283
  95.5 22.4 %copy-start.6 = (bf16[8,2,16,16,128]{4,3,2,1,0:T(8,128)(2,1)S(1)}, bf16[8,2,16,16,128]{4,3,2,1,0:T(8,128)(2,1)}, u32[]{:S(2)}) copy-start(bf16[8,2,16,16,128]{4,3,2,1,0:T(8,128)(2,1)} %copy-done.5) | copy-start | bytes 3145732
  95.6 3.4 %collective-permute-start.4 = (bf16[6,16,128]{2,1,0:T(8,128)(2,1)S(1)}, bf16[6,16,128]{2,1,0:T(8,128)(2,1)S(1)}, u32[]{:S(2)}, u32[]{:S(2)}) collective-permute-start(bf16[6,16,128]{2,1,0:T(8,128)(2,1)S(1)} %maximum_multiply_fusion.2), channel_id=1, source_target_pairs={{0,14},{2,0},{4,2},{6,4},{8,6},{10,8},{12,10},{14,12},{1,15},{3,1}... | collective-permute-start | bytes 73736 | tf_op jit(solution)/shard_map/ppermute | solution.py:266
  99.0 5.7 %copy-start.3 = (bf16[6,16,128]{2,1,0:T(8,128)(2,1)}, bf16[6,16,128]{2,1,0:T(8,128)(2,1)S(1)}, u32[]{:S(2)}) copy-start(bf16[6,16,128]{2,1,0:T(8,128)(2,1)S(1)} %collective-permute-done.4.yh) | copy-start | bytes 73732
  105.5 8.4 %slice-start = ((bf16[6,16,128]{2,1,0:T(8,128)(2,1)}), bf16[1,16,128]{2,1,0:T(8,128)(2,1)S(1)}, s32[]{:S(2)}) async-start(bf16[6,16,128]{2,1,0:T(8,128)(2,1)} %copy-done.3), calls=%async_computation.7 | async-start | bytes 8192 | tf_op jit(solution)/shard_map/slice | solution.py:382
  105.5 12.4 %copy-start.9 = (bf16[1152,256]{1,0:T(8,128)(2,1)S(1)}, bf16[1152,256]{1,0:T(8,128)(2,1)}, u32[]{:S(2)}) copy-start(bf16[1152,256]{1,0:T(8,128)(2,1)} %copy-done.8) | copy-start | bytes 1769476
  105.5 18.6 %all-to-all-start.6 = ((bf16[32,56,128]{2,1,0:T(8,128)(2,1)}), bf16[32,56,128]{2,1,0:T(8,128)(2,1)S(1)}, u32[]{:S(2)}, u32[]{:S(2)}) async-start(bf16[32,56,128]{2,1,0:T(8,128)(2,1)} %broadcast_in_dim.25), calls=%async_computation.6 | async-start | bytes 917504 | tf_op jit(solution)/shard_map/all_to_all | solution.py:283
  113.9 4.0 %collective-permute-start.5 = (bf16[6,16,128]{2,1,0:T(8,128)(2,1)S(1)}, bf16[6,16,128]{2,1,0:T(8,128)(2,1)S(1)}, u32[]{:S(2)}, u32[]{:S(2)}) collective-permute-start(bf16[6,16,128]{2,1,0:T(8,128)(2,1)S(1)} %maximum_multiply_fusion.3), channel_id=1, source_target_pairs={{0,1},{1,0},{2,3},{3,2},{4,5},{5,4},{6,7},{7,6},{8,9},{9,8},{10,11... | collective-permute-start | bytes 73736 | tf_op jit(solution)/shard_map/ppermute | solution.py:266
  115.9 2.0 %copy-start.4 = (bf16[6,16,128]{2,1,0:T(8,128)(2,1)S(1)}, bf16[6,16,128]{2,1,0:T(8,128)(2,1)}, u32[]{:S(2)}) copy-start(bf16[6,16,128]{2,1,0:T(8,128)(2,1)} %copy-done.3) | copy-start | bytes 73732

commit v4 on v3

--- a/solution.py
+++ b/solution.py
@@ -157,12 +157,90 @@
         stats[i, 2:3] = squares
 
 
-def slope_kernel(pre, act, cot, par, out, slope, sums):
+def split(value, parts):
+    out = []
+    for _ in range(parts):
+        out.append(value.astype(BF).astype(F32))
+        value = value - out[-1]
+    return out
+
+
+def rounded(value):
+    high, low = split(value, 2)
+    return high + low
+
+
+def outer(column, rows):
+    return lax.dot_general(
+        column, rows, (((0,), (0,)), ((), ())), precision=lax.Precision.HIGHEST, preferred_element_type=F32
+    )
+
+
+def write_chunk(ref, i, body, column, common):
+    left, right = common
+    line = lax.broadcasted_iota(jnp.int32, left.shape, 0)
+    for at, part in enumerate(split(column, 3)):
+        left = jnp.where(line == at, part, left)
+    ref[i] = jnp.concatenate([body, jnp.concatenate([left, right], axis=1)], axis=0).astype(BF)
+
+
+def common_rows(first, second, alpha, beta, high):
+    zero = jnp.zeros_like(first)
+    rows = split(first, 3) + split(second, 3) + split(alpha, 3) + split(beta, 2) + split(high, 2)
+    return (
+        jnp.concatenate([zero] * 3 + rows[:5], axis=0),
+        jnp.concatenate(rows[5:], axis=0),
+    )
+
+
+def read_chunks(ref):
+    devices, depth, _ = ref.shape
+    rows = depth - 8
+    cout = ref.shape[2] // 2
+    slopes = hats = None
+    firsts = seconds = None
+    columns, vectors, betas = ([], [], None)
+    for j in range(devices):
+        value = ref[j].astype(F32)
+        left, right = (value[rows:, :cout], value[rows:, cout:])
+        part = value[:rows, cout:]
+        beta = right[4:5] + right[5:6]
+        term = value[:rows, :cout] + part * beta
+        first = left[3:4] + left[4:5] + left[5:6]
+        second = left[6:7] + left[7:8] + right[0:1]
+        alpha = right[1:2] + right[2:3] + right[3:4]
+        columns.append(left[0:1] + left[1:2] + left[2:3])
+        vectors.append(jnp.concatenate([alpha, right[6:7] + right[7:8]], axis=1))
+        if j == 0:
+            slopes, hats, firsts, seconds, betas = (term, part, first, second, beta)
+        else:
+            slopes, hats = (slopes + term, hats + part)
+            firsts, seconds, betas = (firsts + first, seconds + second, betas + beta)
+    columns = jnp.concatenate(columns, axis=0)
+    vectors = jnp.concatenate(vectors, axis=0)
+    both = outer(columns, vectors)[:rows]
+    slopes = slopes + both[:, :cout]
+    hats = hats + both[:, cout:]
+    column = jnp.sum(columns, axis=0, keepdims=True)
+    middle = jnp.sum(vectors, axis=0, keepdims=True) / devices
+    return slopes, hats, column, firsts, seconds, middle[:, :cout], betas / devices, middle[:, cout:]
+
+
+def eight(row):
+    return jnp.broadcast_to(row, (8, row.shape[1]))
+
+
+def lone(row):
+    return jnp.where(lax.broadcasted_iota(jnp.int32, (8, row.shape[1]), 0) == 0, eight(row), 0.0)
+
+
+def slope_kernel(pre, act, cot, par, xin, xh, yh, zh, out, slope, big, acc):
     mx, my, mz, cout = pre.shape
+    width = xin.shape[4]
+    half = width // 2
     rows = my * mz
     mean, rstd, gain, bias = (par[i : i + 1] for i in range(4))
-    first = jnp.zeros((1, cout), F32)
-    second = jnp.zeros((1, cout), F32)
+    first, second, count, high, square = (jnp.zeros((1, cout), F32) for _ in range(5))
     for m in range(mx):
         on = act[m].astype(F32).reshape(rows, cout)
         hat = (pre[m].reshape(rows, cout) - mean) * rstd
@@ -173,62 +251,117 @@
         slope[m] = tilt.reshape(my, mz, cout)
         first = first + jnp.sum(tilt, axis=0, keepdims=True)
         second = second + jnp.sum(tilt * hat, axis=0, keepdims=True)
-    for i in range(sums.shape[0]):
-        sums[i, 0:1] = first
-        sums[i, 1:2] = second
-
-
-def weight_kernel(slope, pre, act, par, xin, xh, yh, zh, dpre, pack, zface, dw):
-    mx, my, mz, cout = pre.shape
-    width = xin.shape[4]
-    half = width // 2
-    rows = my * mz
-    mean, rstd, gain, shift, tilt = (par[i : i + 1] for i in range(5))
+        count = count + jnp.sum(on, axis=0, keepdims=True)
+        high = high + jnp.sum(on * hat, axis=0, keepdims=True)
+        square = square + jnp.sum(on * hat * hat, axis=0, keepdims=True)
+    some = jnp.maximum(count, 1.0)
+    alpha = first / some
+    high = rounded(high / some)
+    beta = (second - high * first) / jnp.maximum(square - count * high * high, 0.01 * some)
+    beta = rounded(beta)
     pick = row_picker(my, mz, 0)
     last = lax.broadcasted_iota(jnp.int32, (my, mz, cout), 1) == mz - 1
     total = None
-    rims = []
+    rims = [[], [], []]
+    for m in range(mx):
+        on = act[m].astype(F32).reshape(rows, cout)
+        hat = on * ((pre[m].reshape(rows, cout) - mean) * rstd - high)
+        rest = slope[m].reshape(rows, cout) - on * alpha - hat * beta
+        here, after = ([], [])
+        for i, part in enumerate((rest, hat, on)):
+            held = part.astype(BF)
+            keep = 8 if i == 2 else cout
+            rims[i].append(dot(pick, held))
+            wide = held.astype(F32)
+            nxt = pltpu.roll(wide, rows - 1, 0).reshape(my, mz, cout)
+            nxt = jnp.where(last, 0.0, nxt).reshape(rows, cout)
+            here.append(wide.T[:keep])
+            after.append(nxt.T[:keep])
+        right = jnp.concatenate(here + after, axis=0).astype(BF)
+        left = jnp.concatenate(
+            [tile_of(xin, xh, yh, 2 * m + a, b).reshape(rows, width) for a, b in TAPS], axis=1
+        )
+        term = dot(right, left)
+        total = term if total is None else total + term
+    rim = [jnp.concatenate(parts, axis=0).T for parts in rims]
+    rim = jnp.concatenate([rim[0], rim[1], rim[2][:8]], axis=0).astype(BF)
+    edge = jnp.concatenate(
+        [
+            jnp.concatenate([edge_of(zh, 2 * m + a, b) for a, b in TAPS], axis=1)
+            for m in range(mx)
+        ],
+        axis=0,
+    )
+    size = 2 * cout + 8
+    own = total[:size]
+    low = total[size:] + dot(rim, edge)
+    taps = 3 * len(TAPS)
+    for i in range(len(TAPS)):
+        at = i * width
+        to = 3 * half * i
+        acc[to : to + half] = low[: 2 * cout, at : at + width].T[half:]
+        acc[to + half : to + 3 * half] = own[: 2 * cout, at : at + width].T
+    if acc.shape[0] > half * taps:
+        acc[half * taps :] = jnp.zeros((acc.shape[0] - half * taps, 2 * cout), F32)
+    common = common_rows(first, second, alpha, beta, high)
+    lane = lax.broadcasted_iota(jnp.int32, (8, width), 1)
+    near, depth, _ = big.shape
+    depth = depth - 8
+    for n in range(near):
+        column = jnp.zeros((8, width), F32)
+        for tap in range(taps):
+            start = half * tap - depth * n
+            lo, hi = (max(start, 0), min(start + half, depth))
+            if lo < hi:
+                at = tap // 3 * width
+                row = (low if tap % 3 == 0 else own)[2 * cout :, at : at + width]
+                shift = (start - (0 if tap % 3 == 1 else half)) % width
+                if shift:
+                    row = pltpu.roll(row, shift, 1)
+                column = jnp.where((lane >= lo) & (lane < hi), row, column)
+        write_chunk(big, n, acc[depth * n : depth * (n + 1)], column, common)
+
+
+def near_kernel(parts, out):
+    slopes, hats, column, first, second, alpha, beta, high = read_chunks(parts)
+    rows = slopes.shape[0]
+    cout = slopes.shape[1]
+    beta, high = (rounded(beta), rounded(high))
+    both = outer(lone(column), lone(jnp.concatenate([alpha, high], axis=1)))[:rows]
+    hats = hats - both[:, cout:]
+    slopes = slopes - both[:, :cout] - hats * beta
+    common = common_rows(first, second, alpha, beta, high)
+    body = jnp.concatenate([slopes, hats], axis=1)
+    for i in range(out.shape[0]):
+        write_chunk(out, i, body, eight(column), common)
+
+
+def far_kernel(parts, par, slope, pre, act, dw, grads, dpre, pack, zface):
+    mx, my, mz, cout = pre.shape
+    rows = my * mz
+    mean, rstd, gain, _, count = (par[i : i + 1] for i in range(5))
+    slopes, hats, column, first, second, _, _, _ = read_chunks(parts)
+    shift, tilt = (first / count, second / count)
+    grads[0:1] = shift
+    grads[1:2] = tilt
+    pick = row_picker(my, mz, 0)
     for m in range(mx):
         on = act[m].astype(F32).reshape(rows, cout)
         hat = (pre[m].reshape(rows, cout) - mean) * rstd
         grad = on * rstd * gain * (slope[m].reshape(rows, cout) - shift - hat * tilt)
         held = grad.astype(BF)
         dpre[m] = held.reshape(my, mz, cout)
-        first = dot(pick, held)
-        zface[m] = first.astype(BF)
+        edge = dot(pick, held)
+        zface[m] = edge.astype(BF)
         if m == 0:
             here = lax.axis_index("z") * lax.axis_size("yh") + lax.axis_index("yh")
             keep = jnp.where(here == 0, 0.0, 1.0)
             pack[:my] = (held.astype(F32) * keep).astype(BF).reshape(my, mz, cout)
-            pack[my] = (first * keep).astype(BF)
-        rims.append(first)
-        wide = held.astype(F32)
-        after = pltpu.roll(wide, rows - 1, 0).reshape(my, mz, cout)
-        after = jnp.where(last, 0.0, after).reshape(rows, cout)
-        right = jnp.concatenate([wide.T, after.T], axis=0).astype(BF)
-        left = jnp.concatenate(
-            [tile_of(xin, xh, yh, 2 * m + a, b).reshape(rows, width) for a, b in TAPS], axis=1
-        )
-        term = dot(right, left)
-        total = term if total is None else total + term
-    rim = jnp.concatenate(rims, axis=0).T.astype(BF)
-    edge = jnp.concatenate(
-        [
-            jnp.concatenate([edge_of(zh, 2 * m + a, b) for a, b in TAPS], axis=1)
-            for m in range(mx)
-        ],
-        axis=0,
-    )
-    low = total[cout:] + dot(rim, edge)
-    for i in range(len(TAPS)):
-        at = i * width
-        own = total[:cout, at : at + width].T
-        prev = low[:, at : at + width].T
-        dw[3 * half * i : 3 * half * i + half] = prev[half:].astype(BF)
-        dw[3 * half * i + half : 3 * half * (i + 1)] = own.astype(BF)
-    used = 3 * half * len(TAPS)
-    if dw.shape[0] > used:
-        dw[used:] = jnp.zeros((dw.shape[0] - used, cout), BF)
+            pack[my] = (edge * keep).astype(BF)
+    value = slopes - outer(lone(column), lone(shift))[: slopes.shape[0]] - hats * tilt
+    value = (value * (rstd * gain / count)).astype(BF)
+    for i in range(dw.shape[0]):
+        dw[i] = value
 
 
 def input_kernel(dpre, xh, yh, zh, wmat, mask, out, ext, nxt):
@@ -345,43 +478,40 @@
     count = stats[0]
     mean = stats[1] / count
     rstd = lax.rsqrt(stats[2] / count + 1e-05)
-    par = jnp.stack([mean, rstd, gain, bias])
-    section_out, slope, sums = call(
+    par = jnp.stack([mean, rstd, gain, bias, count])
+    taps = 27 * cin
+    rows = -(-taps // (8 * near)) * 8
+    section_out, slope, big = call(
         slope_kernel,
         [
             shape((mx, my, mz, cout), BF),
             shape((mx, my, mz, cout), F32),
-            shape((near, 2, cout), F32),
+            shape((near, rows + 8, 2 * cout), BF),
         ],
-        [pre, act, cotangent, par],
-    )
-    sums = jnp.sum(spread(jnp.sum(exchanged(sums, NEAR), axis=0), FAR), axis=0)
-    shift_gradient = sums[0] / count
-    gain_gradient = sums[1] / count
-    par = jnp.stack([mean, rstd, gain, shift_gradient, gain_gradient])
-    taps = 27 * cin
-    rows = -(-taps // (16 * near)) * 16
-    if near * (rows - 8) >= taps and near * (rows - 8) % 16 == 0:
-        rows = rows - 8
-    dpre, pack, zface, dw = call(
-        weight_kernel,
+        [pre, act, cotangent, par, xin, xh, yh, zh],
+        scratch=[pltpu.VMEM((near * rows, 2 * cout), F32)],
+        flops=2_400_000_000,
+    )
+    far = lax.axis_size(FAR)
+    (big,) = call(near_kernel, [shape((far, rows + 8, 2 * cout), BF)], [exchanged(big, NEAR)])
+    dw, grads, dpre, pack, zface = call(
+        far_kernel,
         [
+            shape((near, rows, cout), BF),
+            shape((2, cout), F32),
             shape((mx, my, mz, cout), BF),
             shape((my + 1, mz, cout), BF),
             shape((mx, my, cout), BF),
-            shape((near * rows, cout), BF),
         ],
-        [slope, pre, act, par, xin, xh, yh, zh],
-        flops=1_200_000_000,
-    )
+        [exchanged(big, FAR), par, slope, pre, act],
+    )
+    shift_gradient, gain_gradient = (grads[0], grads[1])
     xd = moved(pack, GX, -1)
-    mine = jnp.sum(exchanged(dw.reshape(near, rows, cout), NEAR).astype(F32), axis=0)
     zfaces = jnp.concatenate([zface, xd[my:]], axis=0)
     yd = jnp.concatenate([dpre[:, 0], xd[:1], slab(zfaces[:, 0], mz)], axis=0)
     yd = beyond(yd, GY, -1)
     zd = beyond(jnp.concatenate([zfaces, yd[mx + 1 :]], axis=0), GZ, -1)
-    mine = jnp.sum(spread(mine, FAR), axis=0) / count[0]
-    grad_weight = spread(mine.astype(BF), NEAR).reshape(near * rows, cout)[:taps]
+    grad_weight = exchanged(dw, NEAR).reshape(near * rows, cout)[:taps]
     grad_weight = grad_weight.astype(F32).reshape(weight.shape)
     (grad_features,) = call(
         input_kernel,

time: 126 us -> 118 us (0.937)
  starting transfers between devices: 29.8 us -> 20 us
  Pallas kernels: 8.65 us -> 11.6 us
    all_to_all x3 -> x2, starting transfers between devices: 17.2 us -> 8.05 us  [exchanged(): return lax.all_to_all(value, axes, 0, 0)]
    ppermute x6, waiting for transfers between devices: 12.4 us -> 15.4 us  [moved(): lax.ppermute(value, axes, [(i, (i + by) % count) for i in range(count)])]
    pallas_call x5 -> x6, Pallas kernels: 8.33 us -> 11.3 us  [call(): pl.pallas_call(kernel, out_shape=outs, in_specs=[pl.BlockSpec(memory_spac...]
    all_to_all x3 -> x2, waiting for transfers between devices: 16.8 us -> 13.9 us  [exchanged(): return lax.all_to_all(value, axes, 0, 0)]
    broadcast_in_dim x4 -> x1, local copies, waits for them, and re-layouts: 1.55 us -> 0.01 us  [spread(): jnp.broadcast_to(value, (lax.axis_size(axes),) + value.shape)]
    all_to_all x4 -> x3, blocking collectives: 47.4 us -> 48.5 us  [exchanged(): return lax.all_to_all(value, axes, 0, 0)]
    unnamed x24 -> x20, local copies, waits for them, and re-layouts: 3.71 us -> 3.7 us
  transfers between devices with their start and end apart: 9 -> 8, of which waited for: 8 -> 7; matrix products, arithmetic and copies ran while one was open for 1% -> 1% of each run, Pallas kernels for 3% -> 4%
where the time goes in v4:
time: 118 us
  blocking collectives  48.5 us (41%)
  waiting for transfers between devices  29.3 us (25%)
  starting transfers between devices  20 us (17%)
  Pallas kernels  11.6 us (10%)
  local copies, waits for them, and re-layouts  6.12 us (5%)
  other arithmetic  1.28 us (1%)
    all_to_all x3, blocking collectives, exchanged(): return lax.all_to_all(value, axes, 0, 0)  48.5 us
    ppermute x6, waiting for transfers between devices, moved(): lax.ppermute(value, axes, [(i, (i + by) % count) for i in range(count)])  15.4 us
    all_to_all x2, waiting for transfers between devices, exchanged(): return lax.all_to_all(value, axes, 0, 0)  13.9 us
    ppermute x6, starting transfers between devices, moved(): lax.ppermute(value, axes, [(i, (i + by) % count) for i in range(count)])  12 us
    pallas_call x6, Pallas kernels, call(): pl.pallas_call(kernel, out_shape=outs, in_specs=[pl.BlockSpec(memory_spac...  11.3 us
    all_to_all x2, starting transfers between devices, exchanged(): return lax.all_to_all(value, axes, 0, 0)  8.05 us
    unnamed x20, local copies, waits for them, and re-layouts  3.7 us
  transfers between devices with their start and end apart: 8, of which 7 were waited for; matrix products, arithmetic and copies ran while one was open for 1% of the time, Pallas kernels for 4%

profile of v4, /device:TPU:1, one launch (start us, length us, event | category | flops | bytes accessed | tf_op | source)
XLA Modules:
  0.0 117.8 jit_solution(8672134635752254434)
XLA Ops:
  2.6 3.8 %collective-permute-start = (bf16[2,17,16,128]{3,2,1,0:T(8,128)(2,1)S(1)}, bf16[2,17,16,128]{3,2,1,0:T(8,128)(2,1)S(1)}, u32[]{:S(2)}, u32[]{:S(2)}) collective-permute-start(bf16[2,17,16,128]{3,2,1,0:T(8,128)(2,1)S(1)} %shard_map.102), channel_id=1, source_target_pairs={{0,16},{16,32},{32,48},{48,64},{64,80},{80,96},{96,112},{112,128},... | collective-permute-start | bytes 417800 | tf_op jit(solution)/shard_map/ppermute | solution.py:399
  6.4 1.2 %copy-done = bf16[8,32,16,128]{3,2,1,0:T(8,128)(2,1)S(1)} copy-done((bf16[8,32,16,128]{3,2,1,0:T(8,128)(2,1)S(1)}, bf16[8,32,16,128]{3,2,1,0:T(8,128)(2,1)}, u32[]{:S(2)}) %copy-start) | copy-done | bytes 1048600
  7.6 1.8 %shard_map.101 = (bf16[8,2,16,16,128]{4,3,2,1,0:T(8,128)(2,1)S(1)}, bf16[8,2,16,16,128]{4,3,2,1,0:T(8,128)(2,1)S(1)}, bf16[4,16,16,128]{3,2,1,0:T(8,128)(2,1)S(1)}, bf16[8,2,16,128]{3,2,1,0:T(8,128)(2,1)S(1)}) custom-call(bf16[8,32,16,128]{3,2,1,0:T(8,128)(2,1)S(1)} %copy-done, s32[8,32,32]{2,1,0:T(8,128)S(1)} %copy-done.1), custom_call_target="tpu_custom_call" | custom-call | flops 100000000 | bytes 3506176 | tf_op jit(solution)/shard_map/pallas_call | solution.py:18
  10.4 4.7 %collective-permute-done.xh = bf16[2,17,16,128]{3,2,1,0:T(8,128)(2,1)S(1)} collective-permute-done((bf16[2,17,16,128]{3,2,1,0:T(8,128)(2,1)S(1)}, bf16[2,17,16,128]{3,2,1,0:T(8,128)(2,1)S(1)}, u32[]{:S(2)}, u32[]{:S(2)}) %collective-permute-start) | collective-permute-done | bytes 139296 | tf_op jit(solution)/shard_map/ppermute | solution.py:399
  15.1 2.3 %collective-permute-start.1 = (bf16[10,16,128]{2,1,0:T(8,128)(2,1)S(1)}, bf16[10,16,128]{2,1,0:T(8,128)(2,1)S(1)}, u32[]{:S(2)}, u32[]{:S(2)}) collective-permute-start(bf16[10,16,128]{2,1,0:T(8,128)(2,1)S(1)} %maximum_multiply_fusion.1), channel_id=1, source_target_pairs={{0,2},{2,4},{4,6},{6,8},{8,10},{10,12},{12,14},{14,0},{1,3},{3,5},... | collective-permute-start | bytes 122888 | tf_op jit(solution)/shard_map/ppermute | solution.py:399
  17.5 1.0 collective-permute-done.1.yh
  19.1 2.9 %collective-permute-done.2.zh = bf16[19,16,128]{2,1,0:T(8,128)(2,1)S(1)} collective-permute-done((bf16[19,16,128]{2,1,0:T(8,128)(2,1)S(1)}, bf16[19,16,128]{2,1,0:T(8,128)(2,1)S(1)}, u32[]{:S(2)}, u32[]{:S(2)}) %collective-permute-start.2) | collective-permute-done | bytes 77856 | tf_op jit(solution)/shard_map/ppermute | solution.py:399
  21.9 1.2 %shard_map.103 = (f32[4,16,16,128]{3,2,1,0:T(8,128)S(1)}, f32[32,3,128]{2,1,0:T(4,128)S(1)}, bf16[1152,256]{1,0:T(8,128)(2,1)S(1)}) custom-call(bf16[8,2,16,16,128]{4,3,2,1,0:T(8,128)(2,1)S(1)} %get-tuple-element.20.xin, bf16[4,16,16,128]{3,2,1,0:T(8,128)(2,1)S(1)} %get-tuple-element.21.act, bf16[2,17,16,128]{3,2,1,0:T(8,128)(2,1)S(1)} %collective-permute-done.xh, ...), custom_call_target="tpu_custom_call" | custom-call | flops 1200000000 | bytes 3174400 | tf_op jit(solution)/shard_map/pallas_call | solution.py:18
  24.0 14.0 %all_to_all.25 = f32[32,3,128]{2,1,0:T(4,128)S(1)} all-to-all(f32[32,3,128]{2,1,0:T(4,128)S(1)} %get-tuple-element.24), channel_id=1, replica_groups=mesh['z'=8,'yh'=2,'x'=4,'c'=2,'yl'=2] {'yh','x','c','yl'}, dimensions={0} | all-to-all | bytes 98304 | tf_op jit(solution)/shard_map/all_to_all | solution.py:416
  38.2 12.4 %all_to_all.26 = f32[8,3,128]{2,1,0:T(4,128)S(1)} all-to-all(f32[8,3,128]{2,1,0:T(4,128)S(1)} %broadcast_in_dim.12), channel_id=1, replica_groups=mesh['z'=8,'yh'=2,'x'=4,'c'=2,'yl'=2] {'z'}, dimensions={0} | all-to-all | bytes 24576 | tf_op jit(solution)/shard_map/all_to_all | solution.py:416
  51.3 3.4 %shard_map.104 = (bf16[4,16,16,128]{3,2,1,0:T(8,128)(2,1)}, f32[4,16,16,128]{3,2,1,0:T(8,128)S(1)}, bf16[32,64,256]{2,1,0:T(8,128)(2,1)S(1)}) custom-call(f32[4,16,16,128]{3,2,1,0:T(8,128)S(1)} %get-tuple-element.23.pre, bf16[4,16,16,128]{3,2,1,0:T(8,128)(2,1)S(1)} %get-tuple-element.21.act, bf16[4,16,16,128]{3,2,1,0:T(8,128)(2,1)S(1)} %copy-done.5, ...), custom_call_target="tpu_custom_call" | custom-call | flops 2400000000 | bytes 4192768 | tf_op jit(solution)/shard_map/pallas_call | solution.py:18
  54.7 22.1 %all_to_all.27.parts = bf16[32,64,256]{2,1,0:T(8,128)(2,1)S(1)} all-to-all(bf16[32,64,256]{2,1,0:T(8,128)(2,1)S(1)} %get-tuple-element.26), channel_id=1, replica_groups=mesh['z'=8,'yh'=2,'x'=4,'c'=2,'yl'=2] {'yh','x','c','yl'}, dimensions={0} | all-to-all | bytes 2097152 | tf_op jit(solution)/shard_map/all_to_all | solution.py:416
  76.9 1.3 %shard_map.105 = bf16[8,64,256]{2,1,0:T(8,128)(2,1)} custom-call(bf16[32,64,256]{2,1,0:T(8,128)(2,1)S(1)} %all_to_all.27.parts), custom_call_target="tpu_custom_call" | custom-call | flops 100000000 | bytes 1310720 | tf_op jit(solution)/shard_map/pallas_call | solution.py:18
  78.1 3.4 %all-to-all-start.3 = ((bf16[8,64,256]{2,1,0:T(8,128)(2,1)}), bf16[8,64,256]{2,1,0:T(8,128)(2,1)S(1)}, u32[]{:S(2)}, u32[]{:S(2)}) async-start(bf16[8,64,256]{2,1,0:T(8,128)(2,1)} %shard_map.105), calls=%async_computation.3 | async-start | bytes 524288 | tf_op jit(solution)/shard_map/all_to_all | solution.py:416
  81.6 10.1 %all-to-all-done.3.parts = bf16[8,64,256]{2,1,0:T(8,128)(2,1)S(1)} async-done(((bf16[8,64,256]{2,1,0:T(8,128)(2,1)}), bf16[8,64,256]{2,1,0:T(8,128)(2,1)S(1)}, u32[]{:S(2)}, u32[]{:S(2)}) %all-to-all-start.3) | async-done | bytes 262176 | tf_op jit(solution)/shard_map/all_to_all | solution.py:416
  91.6 1.2 %shard_map.106 = (bf16[32,56,128]{2,1,0:T(8,128)(2,1)}, f32[2,128]{1,0:T(2,128)S(1)}, bf16[4,16,16,128]{3,2,1,0:T(8,128)(2,1)S(1)}, bf16[17,16,128]{2,1,0:T(8,128)(2,1)S(1)}, bf16[4,16,128]{2,1,0:T(8,128)(2,1)S(1)}) custom-call(bf16[8,64,256]{2,1,0:T(8,128)(2,1)S(1)} %all-to-all-done.3.parts, f32[5,128]{1,0:T(8,128)S(1)} %stack.30.par, ...), custom_call_target="tpu_custom_call" | custom-call | flops 100000000 | bytes 2383360 | tf_op jit(solution)/shard_map/pallas_call | solution.py:18
  93.0 4.9 %collective-permute-done.3 = bf16[17,16,128]{2,0,1:T(8,128)(2,1)S(1)} collective-permute-done((bf16[17,16,128]{2,0,1:T(8,128)(2,1)S(1)}, bf16[17,16,128]{2,0,1:T(8,128)(2,1)S(1)}, u32[]{:S(2)}, u32[]{:S(2)}) %collective-permute-start.3) | collective-permute-done | bytes 69664 | tf_op jit(solution)/shard_map/ppermute | solution.py:399
  98.0 3.8 %collective-permute-start.4 = (bf16[6,16,128]{2,1,0:T(8,128)(2,1)S(1)}, bf16[6,16,128]{2,1,0:T(8,128)(2,1)S(1)}, u32[]{:S(2)}, u32[]{:S(2)}) collective-permute-start(bf16[6,16,128]{2,1,0:T(8,128)(2,1)S(1)} %maximum_multiply_fusion.2), channel_id=1, source_target_pairs={{0,14},{2,0},{4,2},{6,4},{8,6},{10,8},{12,10},{14,12},{1,15},{3,1}... | collective-permute-start | bytes 73736 | tf_op jit(solution)/shard_map/ppermute | solution.py:399
  101.9 4.6 %all-to-all-start.4 = ((bf16[32,56,128]{2,1,0:T(8,128)(2,1)}), bf16[32,56,128]{2,1,0:T(8,128)(2,1)S(1)}, u32[]{:S(2)}, u32[]{:S(2)}) async-start(bf16[32,56,128]{2,1,0:T(8,128)(2,1)} %get-tuple-element.33), calls=%async_computation.4 | async-start | bytes 917504 | tf_op jit(solution)/shard_map/all_to_all | solution.py:416
  106.5 1.5 %collective-permute-start.5 = (bf16[6,16,128]{2,1,0:T(8,128)(2,1)S(1)}, bf16[6,16,128]{2,1,0:T(8,128)(2,1)S(1)}, u32[]{:S(2)}, u32[]{:S(2)}) collective-permute-start(bf16[6,16,128]{2,1,0:T(8,128)(2,1)S(1)} %maximum_multiply_fusion.3), channel_id=1, source_target_pairs={{0,1},{1,0},{2,3},{3,2},{4,5},{5,4},{6,7},{7,6},{8,9},{9,8},{10,11... | collective-permute-start | bytes 73736 | tf_op jit(solution)/shard_map/ppermute | solution.py:399
  108.5 1.9 %collective-permute-done.5.zh = bf16[6,16,128]{2,1,0:T(8,128)(2,1)S(1)} collective-permute-done((bf16[6,16,128]{2,1,0:T(8,128)(2,1)S(1)}, bf16[6,16,128]{2,1,0:T(8,128)(2,1)S(1)}, u32[]{:S(2)}, u32[]{:S(2)}) %collective-permute-start.5) | collective-permute-done | bytes 24608 | tf_op jit(solution)/shard_map/ppermute | solution.py:399
  110.5 2.4 %shard_map.107 = bf16[8,16,2,16,128]{4,3,2,1,0:T(8,128)(2,1)} custom-call(bf16[4,16,16,128]{3,2,1,0:T(8,128)(2,1)S(1)} %get-tuple-element.28.dpre, bf16[17,16,128]{2,1,0:T(8,128)(2,1)S(1)} %copy.65.xh, bf16[6,16,128]{2,1,0:T(8,128)(2,1)S(1)} %collective-permute-done.4.yh, bf16[6,16,128]{2,1,0:T(8,128)(2,1)S(1)} %collective-permute-done.5.zh, ...), custom_call_target="tpu_custom_call" | custom-call | flops 1200000000 | bytes 3067904 | tf_op jit(solution)/shard_map/pallas_call | solution.py:18
  112.9 3.8 %all-to-all-done.4 = bf16[32,56,128]{2,1,0:T(8,128)(2,1)S(1)} async-done(((bf16[32,56,128]{2,1,0:T(8,128)(2,1)}), bf16[32,56,128]{2,1,0:T(8,128)(2,1)S(1)}, u32[]{:S(2)}, u32[]{:S(2)}) %all-to-all-start.4) | async-done | bytes 458784 | tf_op jit(solution)/shard_map/all_to_all | solution.py:416
  116.8 1.0 convert.1
  (65 shorter events, 6.1 us)
Async XLA Ops:
  2.3 4.1 %copy-start.1 = (s32[8,32,32]{2,1,0:T(8,128)S(1)}, s32[8,32,32]{2,1,0:T(8,128)}, u32[]{:S(2)}) copy-start(s32[8,32,32]{2,1,0:T(8,128)} %active.1) | copy-start | bytes 98308
  2.6 12.4 %collective-permute-start = (bf16[2,17,16,128]{3,2,1,0:T(8,128)(2,1)S(1)}, bf16[2,17,16,128]{3,2,1,0:T(8,128)(2,1)S(1)}, u32[]{:S(2)}, u32[]{:S(2)}) collective-permute-start(bf16[2,17,16,128]{3,2,1,0:T(8,128)(2,1)S(1)} %shard_map.102), channel_id=1, source_target_pairs={{0,16},{16,32},{32,48},{48,64},{64,80},{80,96},{96,112},{112,128},... | collective-permute-start | bytes 417800 | tf_op jit(solution)/shard_map/ppermute | solution.py:399
  6.4 1.2 %copy-start = (bf16[8,32,16,128]{3,2,1,0:T(8,128)(2,1)S(1)}, bf16[8,32,16,128]{3,2,1,0:T(8,128)(2,1)}, u32[]{:S(2)}) copy-start(bf16[8,32,16,128]{3,2,1,0:T(8,128)(2,1)} %feat.1) | copy-start | bytes 3145732
  9.3 1.0 copy-start.2
  10.3 11.6 %copy-start.4 = (bf16[3,3,3,64,128]{4,3,2,1,0:T(8,128)(2,1)S(1)}, bf16[3,3,3,64,128]{4,3,2,1,0:T(8,128)(2,1)}, u32[]{:S(2)}) copy-start(bf16[3,3,3,64,128]{4,3,2,1,0:T(8,128)(2,1)} %weight.1) | copy-start | bytes 1327108
  15.1 3.4 %collective-permute-start.1 = (bf16[10,16,128]{2,1,0:T(8,128)(2,1)S(1)}, bf16[10,16,128]{2,1,0:T(8,128)(2,1)S(1)}, u32[]{:S(2)}, u32[]{:S(2)}) collective-permute-start(bf16[10,16,128]{2,1,0:T(8,128)(2,1)S(1)} %maximum_multiply_fusion.1), channel_id=1, source_target_pairs={{0,2},{2,4},{4,6},{6,8},{8,10},{10,12},{12,14},{14,0},{1,3},{3,5},... | collective-permute-start | bytes 122888 | tf_op jit(solution)/shard_map/ppermute | solution.py:399
  18.6 3.3 %collective-permute-start.2 = (bf16[19,16,128]{2,1,0:T(8,128)(2,1)S(1)}, bf16[19,16,128]{2,1,0:T(8,128)(2,1)S(1)}, u32[]{:S(2)}, u32[]{:S(2)}) collective-permute-start(bf16[19,16,128]{2,1,0:T(8,128)(2,1)S(1)} %maximum_multiply_fusion), channel_id=1, source_target_pairs={{0,1},{1,0},{2,3},{3,2},{4,5},{5,4},{6,7},{7,6},{8,9},{9,8},{10,11... | collective-permute-start | bytes 233480 | tf_op jit(solution)/shard_map/ppermute | solution.py:399
  23.2 0.8 copy-start.6
  24.0 27.4 %copy-start.5 = (bf16[4,16,16,128]{3,2,1,0:T(8,128)(2,1)S(1)}, bf16[4,16,16,128]{3,2,1,0:T(8,128)(2,1)}, u32[]{:S(2)}) copy-start(bf16[4,16,16,128]{3,2,1,0:T(8,128)(2,1)} %cot.1) | copy-start | bytes 786436
  50.6 0.7 copy-start.8
  50.6 0.7 copy-start.9
  78.1 13.5 %all-to-all-start.3 = ((bf16[8,64,256]{2,1,0:T(8,128)(2,1)}), bf16[8,64,256]{2,1,0:T(8,128)(2,1)S(1)}, u32[]{:S(2)}, u32[]{:S(2)}) async-start(bf16[8,64,256]{2,1,0:T(8,128)(2,1)} %shard_map.105), calls=%async_computation.3 | async-start | bytes 524288 | tf_op jit(solution)/shard_map/all_to_all | solution.py:416
  91.6 18.9 %copy-start.7 = (bf16[1152,256]{1,0:T(8,128)(2,1)S(1)}, bf16[1152,256]{1,0:T(8,128)(2,1)}, u32[]{:S(2)}) copy-start(bf16[1152,256]{1,0:T(8,128)(2,1)} %copy-done.6) | copy-start | bytes 1769476
  92.9 17.6 %copy-start.3 = (bf16[8,2,16,16,128]{4,3,2,1,0:T(8,128)(2,1)S(1)}, bf16[8,2,16,16,128]{4,3,2,1,0:T(8,128)(2,1)}, u32[]{:S(2)}) copy-start(bf16[8,2,16,16,128]{4,3,2,1,0:T(8,128)(2,1)} %copy-done.2) | copy-start | bytes 3145732
  92.9 5.0 %collective-permute-start.3 = (bf16[17,16,128]{2,0,1:T(8,128)(2,1)S(1)}, bf16[17,16,128]{2,0,1:T(8,128)(2,1)S(1)}, u32[]{:S(2)}, u32[]{:S(2)}) collective-permute-start(bf16[17,16,128]{2,0,1:T(8,128)(2,1)S(1)} %copy.60), channel_id=1, source_target_pairs={{0,240},{16,0},{32,16},{48,32},{64,48},{80,64},{96,80},{112,96},{1... | collective-permute-start | bytes 208904 | tf_op jit(solution)/shard_map/ppermute | solution.py:399
  98.0 8.5 %collective-permute-start.4 = (bf16[6,16,128]{2,1,0:T(8,128)(2,1)S(1)}, bf16[6,16,128]{2,1,0:T(8,128)(2,1)S(1)}, u32[]{:S(2)}, u32[]{:S(2)}) collective-permute-start(bf16[6,16,128]{2,1,0:T(8,128)(2,1)S(1)} %maximum_multiply_fusion.2), channel_id=1, source_target_pairs={{0,14},{2,0},{4,2},{6,4},{8,6},{10,8},{12,10},{14,12},{1,15},{3,1}... | collective-permute-start | bytes 73736 | tf_op jit(solution)/shard_map/ppermute | solution.py:399
  101.9 14.9 %all-to-all-start.4 = ((bf16[32,56,128]{2,1,0:T(8,128)(2,1)}), bf16[32,56,128]{2,1,0:T(8,128)(2,1)S(1)}, u32[]{:S(2)}, u32[]{:S(2)}) async-start(bf16[32,56,128]{2,1,0:T(8,128)(2,1)} %get-tuple-element.33), calls=%async_computation.4 | async-start | bytes 917504 | tf_op jit(solution)/shard_map/all_to_all | solution.py:416
  106.5 3.9 %collective-permute-start.5 = (bf16[6,16,128]{2,1,0:T(8,128)(2,1)S(1)}, bf16[6,16,128]{2,1,0:T(8,128)(2,1)S(1)}, u32[]{:S(2)}, u32[]{:S(2)}) collective-permute-start(bf16[6,16,128]{2,1,0:T(8,128)(2,1)S(1)} %maximum_multiply_fusion.3), channel_id=1, source_target_pairs={{0,1},{1,0},{2,3},{3,2},{4,5},{5,4},{6,7},{7,6},{8,9},{9,8},{10,11... | collective-permute-start | bytes 73736 | tf_op jit(solution)/shard_map/ppermute | solution.py:399

commit v5 on v4

--- a/solution.py
+++ b/solution.py
@@ -8,9 +8,12 @@
 BF = jnp.bfloat16
 F32 = jnp.float32
 ALL = ("z", "yh", "x", "c", "yl")
-NEAR = ("yh", "x", "c", "yl")
+NEAR = ("c", "yh", "x", "yl")
+PLANE = ("yh", "x", "yl")
+GX, GY, GZ = (("z", "yh"), ("x", "c"), ("yl",))
 FAR = ("z",)
-PARAMS = pltpu.CompilerParams(vmem_limit_bytes=48 * 1024 * 1024)
+PARAMS = pltpu.CompilerParams(vmem_limit_bytes=24 * 1024 * 1024)
+WIDE = pltpu.CompilerParams(vmem_limit_bytes=60 * 1024 * 1024)
 
 
 def call(kernel, outs, args, scratch=(), flops=100_000_000):
@@ -40,6 +43,10 @@
     return (k == r * step + offset).astype(BF)
 
 
+def rows_at(value, depth):
+    return jnp.concatenate([value[i, depth : depth + 1] for i in range(value.shape[0])], axis=0)
+
+
 def with_edge(value, edge, at, shift):
     groups, depth, lanes = value.shape
     moved = pltpu.roll(value.reshape(groups * depth, lanes), shift % (groups * depth), 0)
@@ -48,42 +55,67 @@
     return jnp.where(q == at, jnp.broadcast_to(edge[:, None, :], value.shape), moved)
 
 
-def masked_row(feat, active):
-    ny, mz, width = feat.shape
-    z = active.shape[1]
+def mask_row(active, mz, width):
+    ny, z = active.shape
     pair = lax.broadcasted_iota(jnp.int32, (mz, z), 1) // 2
     sel = (pair == lax.broadcasted_iota(jnp.int32, (mz, z), 0)).astype(F32)
     lane = lax.broadcasted_iota(jnp.int32, (z, width), 1) // (width // 2)
     widen = (lax.broadcasted_iota(jnp.int32, (z, width), 0) % 2 == lane).astype(BF)
     rep = jnp.broadcast_to(active.astype(F32)[:, None, :], (ny, mz, z)) * sel[None]
     m = dot(rep.astype(BF).reshape(ny * mz, z), widen).astype(BF)
-    m = m.reshape(ny // 2, 2, mz, width)
-    return m, feat.reshape(ny // 2, 2, mz, width) * m
-
-
-def face_kernel(feat, active, pack):
+    return m.reshape(ny // 2, 2, mz, width)
+
+
+def ring_index(axes):
+    index = 0
+    for name in axes:
+        index = index * lax.axis_size(name) + lax.axis_index(name)
+    return index
+
+
+def ring_size(axes):
+    size = 1
+    for name in axes:
+        size = size * lax.axis_size(name)
+    return size
+
+
+def unless(condition):
+    return jnp.where(condition, 0.0, 1.0)
+
+
+def face_kernel(feat, active, pack, row, cells, sems):
     _, slabs, mz, width = pack.shape
     my = slabs - 1
-    last = lax.axis_size("z") * lax.axis_size("yh") - 1
-    here = lax.axis_index("z") * lax.axis_size("yh") + lax.axis_index("yh")
-    keep = jnp.where(here == last, 0.0, 1.0)
-    _, value = masked_row(feat[0], active[0])
+    copies = [
+        pltpu.make_async_copy(feat.at[feat.shape[0] - 1], row, sems.at[0]),
+        pltpu.make_async_copy(active.at[active.shape[0] - 1], cells, sems.at[1]),
+    ]
+    for copy in copies:
+        copy.start()
+    keep = unless(ring_index(GX) == ring_size(GX) - 1)
     pick = row_picker(my, mz, mz - 1)
+    for copy in copies:
+        copy.wait()
+    m = mask_row(cells[...], mz, width)
+    value = row[...].reshape(m.shape) * m
     for py in range(2):
         held = (value[:, py].astype(F32) * keep).astype(BF)
         pack[py, :my] = held
         pack[py, my] = dot(pick, held.reshape(my * mz, width)).astype(BF)
 
 
-def mask_kernel(feat, active, xin, mask, act, zface):
+def mask_kernel(feat, active, gain, bias, xin, act, zface, norm):
     nx, _, my, mz, width = xin.shape
     pick = row_picker(my, mz, mz - 1)
+    norm[0:1] = gain[...]
+    norm[1:2] = bias[...]
     count = None
     for x in range(nx):
-        m, value = masked_row(feat[x], active[x])
+        m = mask_row(active[x], mz, width)
+        value = feat[x].reshape(m.shape) * m
         for py in range(2):
             part = m[:, py]
-            mask[x, py] = part
             held = value[:, py]
             xin[x, py] = held
             zface[x, py] = dot(pick, held.reshape(my * mz, width)).astype(BF)
@@ -117,10 +149,9 @@
 TAPS = [(a, b) for a in range(3) for b in range(3)]
 
 
-def forward_kernel(xin, act, xh, yh, zh, weight, pre, stats, wmat):
-    mx, my, mz, cout = pre.shape
-    width = xin.shape[4]
-    half = width // 2
+def build_matrix(weight, wmat):
+    half, cout = weight.shape[3:]
+    width = 2 * half
     zero = jnp.zeros((half, cout), BF)
     for i, (a, b) in enumerate(TAPS):
         lo = i * width
@@ -128,6 +159,55 @@
         wmat[lo + half : lo + width, :cout] = weight[a, b, 2]
         wmat[lo : lo + half, cout:] = zero
         wmat[lo + half : lo + width, cout:] = weight[a, b, 0]
+
+
+OFF = 1e30
+
+
+def standardized(value, mean, rstd):
+    active = value < 0.1 * OFF
+    return jnp.where(active, 1.0, 0.0), jnp.where(active, value - mean, 0.0) * rstd
+
+
+def slope_of(normed, sig, cot):
+    return cot * sig * (1.0 + normed * (1.0 - sig))
+
+
+def rim_parts(value, on, cot):
+    high, low = split(value, 2)
+    return [part.astype(BF) for part in (jnp.where(on > 0.0, high, OFF), low, cot)]
+
+
+def merge_kernel(parts, xd, yface, zface, out, yplane):
+    mx = yface.shape[1]
+    my = zface.shape[2]
+    counts, sums, squares = (
+        jnp.concatenate([parts[j, i : i + 1] for j in range(parts.shape[0])], axis=0) for i in range(3)
+    )
+    count = jnp.sum(counts, axis=0, keepdims=True)
+    total = jnp.sum(sums, axis=0, keepdims=True)
+    mean = total / jnp.maximum(count, 1.0)
+    apart = sums / jnp.maximum(counts, 1.0) - mean
+    square = jnp.sum(squares + counts * apart * apart, axis=0, keepdims=True)
+    for i in range(out.shape[0]):
+        out[i, 0:1] = count
+        out[i, 1:2] = total
+        out[i, 2:3] = square
+    depth = yplane.shape[2]
+    yplane[:, :mx] = yface[...]
+    yplane[:, mx] = xd[:, 0]
+    for i in range(3):
+        rows = [zface[i, m].astype(F32)[0:1] for m in range(mx)] + [xd[i, my].astype(F32)[0:1]]
+        rows.append(jnp.zeros((depth - mx - 1, yplane.shape[3]), F32))
+        yplane[i, mx + 1] = jnp.concatenate(rows, axis=0).astype(BF)
+
+
+def forward_kernel(
+    xin, act, xh, yh, zh, weight, cot, pre, stats, xface, yface, zface, wmat
+):
+    mx, my, mz, cout = pre.shape
+    width = xin.shape[4]
+    build_matrix(weight, wmat)
     rows = my * mz
     total = jnp.zeros((1, cout), F32)
     count = jnp.zeros((1, cout), F32)
@@ -141,16 +221,26 @@
         rim = dot(edge, w[:, cout:])
         prev = with_edge(out[:, cout:].reshape(my, mz, cout), rim, 0, 1)
         value = out[:, :cout].reshape(my, mz, cout) + prev
-        pre[m] = value
         on = act[m].astype(F32)
+        pre[m] = jnp.where(on > 0.0, value, OFF)
+        planes = (value, on, cot[m].astype(F32))
+        side = rim_parts(*[rows_at(part, 0) for part in planes])
+        line = rim_parts(*[part[0] for part in planes])
+        whole = rim_parts(*planes) if m == 0 else None
+        for i in range(3):
+            yface[i, m] = line[i]
+            zface[i, m] = side[i]
+            if m == 0:
+                xface[i, :my] = whole[i]
+                xface[i, my] = side[i]
         total = total + jnp.sum((on * value).reshape(rows, cout), axis=0, keepdims=True)
         count = count + jnp.sum(on.reshape(rows, cout), axis=0, keepdims=True)
     mean = total / jnp.maximum(count, 1.0)
     squares = jnp.zeros((1, cout), F32)
     for m in range(mx):
-        apart = pre[m].reshape(rows, cout) - mean
         on = act[m].astype(F32).reshape(rows, cout)
-        squares = squares + jnp.sum(on * apart * apart, axis=0, keepdims=True)
+        apart = jnp.where(on > 0.0, pre[m].reshape(rows, cout) - mean, 0.0)
+        squares = squares + jnp.sum(apart * apart, axis=0, keepdims=True)
     for i in range(stats.shape[0]):
         stats[i, 0:1] = count
         stats[i, 1:2] = total
@@ -234,20 +324,24 @@
     return jnp.where(lax.broadcasted_iota(jnp.int32, (8, row.shape[1]), 0) == 0, eight(row), 0.0)
 
 
-def slope_kernel(pre, act, cot, par, xin, xh, yh, zh, out, slope, big, acc):
+def slope_kernel(
+    pre, cot, par, xin, xh, yh, zh, xd, yd, zface, out, big, zplane, slope, acc
+):
     mx, my, mz, cout = pre.shape
     width = xin.shape[4]
     half = width // 2
     rows = my * mz
     mean, rstd, gain, bias = (par[i : i + 1] for i in range(4))
     first, second, count, high, square = (jnp.zeros((1, cout), F32) for _ in range(5))
+    zplane[:, :mx] = zface[...]
+    zplane[:, mx] = xd[:, my]
+    zplane[:, mx + 1] = yd[:, mx + 1]
     for m in range(mx):
-        on = act[m].astype(F32).reshape(rows, cout)
-        hat = (pre[m].reshape(rows, cout) - mean) * rstd
+        on, hat = standardized(pre[m].reshape(rows, cout), mean, rstd)
         normed = hat * gain + bias
         sig = jax.nn.sigmoid(normed)
         out[m] = (on * normed * sig).astype(BF).reshape(my, mz, cout)
-        tilt = on * cot[m].astype(F32).reshape(rows, cout) * sig * (1.0 + normed * (1.0 - sig))
+        tilt = slope_of(normed, sig, on * cot[m].astype(F32).reshape(rows, cout))
         slope[m] = tilt.reshape(my, mz, cout)
         first = first + jnp.sum(tilt, axis=0, keepdims=True)
         second = second + jnp.sum(tilt * hat, axis=0, keepdims=True)
@@ -259,20 +353,19 @@
     high = rounded(high / some)
     beta = (second - high * first) / jnp.maximum(square - count * high * high, 0.01 * some)
     beta = rounded(beta)
-    pick = row_picker(my, mz, 0)
     last = lax.broadcasted_iota(jnp.int32, (my, mz, cout), 1) == mz - 1
     total = None
     rims = [[], [], []]
     for m in range(mx):
-        on = act[m].astype(F32).reshape(rows, cout)
-        hat = on * ((pre[m].reshape(rows, cout) - mean) * rstd - high)
+        on, hat = standardized(pre[m].reshape(rows, cout), mean, rstd)
+        hat = on * (hat - high)
         rest = slope[m].reshape(rows, cout) - on * alpha - hat * beta
         here, after = ([], [])
         for i, part in enumerate((rest, hat, on)):
             held = part.astype(BF)
             keep = 8 if i == 2 else cout
-            rims[i].append(dot(pick, held))
             wide = held.astype(F32)
+            rims[i].append(rows_at(wide.reshape(my, mz, cout), 0))
             nxt = pltpu.roll(wide, rows - 1, 0).reshape(my, mz, cout)
             nxt = jnp.where(last, 0.0, nxt).reshape(rows, cout)
             here.append(wide.T[:keep])
@@ -336,48 +429,63 @@
         write_chunk(out, i, body, eight(column), common)
 
 
-def far_kernel(parts, par, slope, pre, act, dw, grads, dpre, pack, zface):
-    mx, my, mz, cout = pre.shape
-    rows = my * mz
-    mean, rstd, gain, _, count = (par[i : i + 1] for i in range(5))
+def far_kernel(parts, par, dw, shift_out, tilt_out, both):
+    _, rstd, gain, _, count = (par[i : i + 1] for i in range(5))
     slopes, hats, column, first, second, _, _, _ = read_chunks(parts)
     shift, tilt = (first / count, second / count)
-    grads[0:1] = shift
-    grads[1:2] = tilt
-    pick = row_picker(my, mz, 0)
-    for m in range(mx):
-        on = act[m].astype(F32).reshape(rows, cout)
-        hat = (pre[m].reshape(rows, cout) - mean) * rstd
-        grad = on * rstd * gain * (slope[m].reshape(rows, cout) - shift - hat * tilt)
-        held = grad.astype(BF)
-        dpre[m] = held.reshape(my, mz, cout)
-        edge = dot(pick, held)
-        zface[m] = edge.astype(BF)
-        if m == 0:
-            here = lax.axis_index("z") * lax.axis_size("yh") + lax.axis_index("yh")
-            keep = jnp.where(here == 0, 0.0, 1.0)
-            pack[:my] = (held.astype(F32) * keep).astype(BF).reshape(my, mz, cout)
-            pack[my] = (edge * keep).astype(BF)
+    shift_out[...] = shift
+    tilt_out[...] = tilt
+    both[0:1] = shift
+    both[1:2] = tilt
     value = slopes - outer(lone(column), lone(shift))[: slopes.shape[0]] - hats * tilt
     value = (value * (rstd * gain / count)).astype(BF)
     for i in range(dw.shape[0]):
         dw[i] = value
 
 
-def input_kernel(dpre, xh, yh, zh, wmat, mask, out, ext, nxt):
-    mx, my, mz, cout = dpre.shape
-    width = mask.shape[4]
+def input_kernel(pre, cot, par, grads, xd, yd, zd, active, weight, out, ext, nxt, wmat):
+    mx, my, mz, cout = pre.shape
+    width = out.shape[4]
     rows = my * mz
+    mean, rstd, gain, bias = (par[i : i + 1] for i in range(4))
+    shift, tilt = (grads[i : i + 1] for i in range(2))
+    scale = rstd * gain
+    inside = [
+        unless(ring_index(axes) == ring_size(axes) - 1) for axes in (GX, GY, GZ)
+    ]
+
+    def gradient(value, cot, keep):
+        on, hat = standardized(value, mean, rstd)
+        normed = hat * gain + bias
+        slope = slope_of(normed, jax.nn.sigmoid(normed), cot)
+        return (on * keep * scale * (slope - shift - hat * tilt)).astype(BF)
+
+    def rim(parts, keep):
+        high, low, cot = (part.astype(F32) for part in parts)
+        return gradient(high + low, cot, keep)
+
+    build_matrix(weight, wmat)
     for r in range(mx + 1):
-        base = dpre[r] if r < mx else xh[:my]
+        keep = 1.0 if r < mx else inside[0]
+        if r < mx:
+            own = cot[r].astype(F32).reshape(rows, cout)
+            base = gradient(pre[r].reshape(rows, cout), own, keep).reshape(my, mz, cout)
+        else:
+            flat = [xd[i, :my].reshape(rows, cout) for i in range(3)]
+            base = rim(flat, keep).reshape(my, mz, cout)
+        row = rim([yd[i, r] for i in range(3)], keep * inside[1])
         ext[r, :my] = base
-        ext[r, my] = yh[r]
-        whole = jnp.concatenate([base, yh[r][None]], axis=0).astype(F32)
-        rim = jnp.concatenate([zh[r].astype(F32), zh[mx + 1].astype(F32)[r : r + 1]], axis=0)
-        nxt[r] = with_edge(whole, rim, mz - 1, -1).astype(BF)
+        ext[r, my] = row
+        whole = jnp.concatenate([base, row[None]], axis=0).astype(F32)
+        side = rim([zd[i, r] for i in range(3)], keep * inside[2]).astype(F32)
+        last = [zd[i, mx + 1].astype(F32)[r : r + 1] for i in range(3)]
+        last = rim(last, keep * inside[1] * inside[2]).astype(F32)
+        nxt[r] = with_edge(whole, jnp.concatenate([side, last], axis=0), mz - 1, -1).astype(BF)
     taps = (((1, 0),), ((2, 0), (0, 1)))
     for m in range(mx):
         for px in range(2):
+            x = 2 * m + px
+            mask = mask_row(active[x], mz, width)
             for py in range(2):
                 left, right = ([], [])
                 for a, sx in taps[px]:
@@ -389,17 +497,13 @@
                 left = jnp.concatenate(left, axis=1)
                 right = jnp.concatenate(right, axis=1)
                 value = dot(left, right, ((1,), (1,)))
-                x = 2 * m + px
-                value = value * mask[x, py].astype(F32).reshape(rows, width)
+                value = value * mask[:, py].astype(F32).reshape(rows, width)
                 out[x, :, py] = value.astype(BF).reshape(my, mz, width)
 
 
 def moved(value, axes, by):
     count = lax.axis_size(axes)
     return lax.ppermute(value, axes, [(i, (i + by) % count) for i in range(count)])
-
-
-GX, GY, GZ = (("z", "yh"), ("x", "c"), ("yl",))
 
 
 def beyond(value, axes, by):
@@ -414,10 +518,6 @@
 
 def exchanged(value, axes):
     return lax.all_to_all(value, axes, 0, 0)
-
-
-def spread(value, axes):
-    return exchanged(jnp.broadcast_to(value, (lax.axis_size(axes),) + value.shape), axes)
 
 
 def merged(parts):
@@ -438,25 +538,26 @@
     pack = pl.pallas_call(
         face_kernel,
         out_shape=shape((2, my + 1, mz, width), BF),
-        grid=(1,),
-        in_specs=[
-            pl.BlockSpec((1, vy, mz, width), lambda i: (0, 0, 0, 0)),
-            pl.BlockSpec((1, vy, 2 * mz), lambda i: (0, 0, 0)),
+        in_specs=[pl.BlockSpec(memory_space=pltpu.HBM)] * 2,
+        out_specs=pl.BlockSpec(memory_space=pltpu.VMEM),
+        scratch_shapes=[
+            pltpu.VMEM((vy, mz, width), BF),
+            pltpu.VMEM((vy, 2 * mz), jnp.int32),
+            pltpu.SemaphoreType.DMA((2,)),
         ],
-        out_specs=pl.BlockSpec((2, my + 1, mz, width), lambda i: (0, 0, 0, 0)),
-        compiler_params=PARAMS,
+        compiler_params=WIDE,
         cost_estimate=pl.CostEstimate(flops=10_000_000, bytes_accessed=400_000, transcendentals=0),
-    )(features[vx - 1 :], active[vx - 1 :])
+    )(features, active)
     xh = moved(pack, GX, 1)
-    xin, mask, act, zface = call(
+    xin, act, zface, norm = call(
         mask_kernel,
         [
             shape((vx, 2, my, mz, width), BF),
-            shape((vx, 2, my, mz, width), BF),
             shape((mx, my, mz, width), BF),
             shape((vx, 2, my, width), BF),
+            shape((2, cout), F32),
         ],
-        [features, active],
+        [features, active, gain[None], bias[None]],
     )
     yface = jnp.concatenate([xh[1:2, my - 1], xin[:, 1, my - 1]], axis=0)
     zfaces = jnp.concatenate([xh[None, :, my], zface], axis=0)
@@ -464,62 +565,76 @@
     yh = beyond(jnp.concatenate([yface, slab(zfaces[:, 1, my - 1], mz)], axis=0), GY, 1)
     zfaces = jnp.concatenate([zfaces.reshape(2 * rows, my, width), yh[rows:]], axis=0)
     zh = beyond(zfaces, GZ, 1)
-    pre, stats, wmat = call(
+    pre, stats, xface, yface, zface = call(
         forward_kernel,
         [
             shape((mx, my, mz, cout), F32),
             shape((near, 3, cout), F32),
-            shape((9 * width, 2 * cout), BF),
+            shape((3, my + 1, mz, cout), BF),
+            shape((3, mx, mz, cout), BF),
+            shape((3, mx, my, cout), BF),
         ],
-        [xin, act, xh, yh, zh, weight],
+        [xin, act, xh, yh, zh, weight, cotangent],
+        scratch=[pltpu.VMEM((9 * width, 2 * cout), BF)],
         flops=1_200_000_000,
     )
-    stats = merged(spread(merged(exchanged(stats, NEAR)), FAR))
+    xd = moved(xface, GX, -1)
+    stats, yplane = call(
+        merge_kernel,
+        [shape((lax.axis_size(FAR), 3, cout), F32), shape((3, mx + 2, mz, cout), BF)],
+        [exchanged(stats, NEAR), xd, yface, zface],
+    )
+    yd = moved(yplane, GY, -1)
+    stats = merged(exchanged(stats, FAR))
     count = stats[0]
     mean = stats[1] / count
     rstd = lax.rsqrt(stats[2] / count + 1e-05)
-    par = jnp.stack([mean, rstd, gain, bias, count])
+    par = jnp.stack([mean, rstd, norm[0], norm[1], count])
     taps = 27 * cin
     rows = -(-taps // (8 * near)) * 8
-    section_out, slope, big = call(
+    section_out, big, zplane = call(
         slope_kernel,
         [
             shape((mx, my, mz, cout), BF),
-            shape((mx, my, mz, cout), F32),
             shape((near, rows + 8, 2 * cout), BF),
+            shape((3, mx + 2, my, cout), BF),
         ],
-        [pre, act, cotangent, par, xin, xh, yh, zh],
-        scratch=[pltpu.VMEM((near * rows, 2 * cout), F32)],
+        [pre, cotangent, par, xin, xh, yh, zh, xd, yd, zface],
+        scratch=[pltpu.VMEM(pre.shape, F32), pltpu.VMEM((near * rows, 2 * cout), F32)],
         flops=2_400_000_000,
     )
+    zd = moved(zplane, GZ, -1)
     far = lax.axis_size(FAR)
     (big,) = call(near_kernel, [shape((far, rows + 8, 2 * cout), BF)], [exchanged(big, NEAR)])
-    dw, grads, dpre, pack, zface = call(
+    plane = lax.axis_size(PLANE)
+    dw, shift, tilt, grads = call(
         far_kernel,
         [
-            shape((near, rows, cout), BF),
+            shape((plane, rows, cout), BF),
+            shape((1, cout), F32),
+            shape((1, cout), F32),
             shape((2, cout), F32),
-            shape((mx, my, mz, cout), BF),
-            shape((my + 1, mz, cout), BF),
-            shape((mx, my, cout), BF),
         ],
-        [exchanged(big, FAR), par, slope, pre, act],
-    )
-    shift_gradient, gain_gradient = (grads[0], grads[1])
-    xd = moved(pack, GX, -1)
-    zfaces = jnp.concatenate([zface, xd[my:]], axis=0)
-    yd = jnp.concatenate([dpre[:, 0], xd[:1], slab(zfaces[:, 0], mz)], axis=0)
-    yd = beyond(yd, GY, -1)
-    zd = beyond(jnp.concatenate([zfaces, yd[mx + 1 :]], axis=0), GZ, -1)
-    grad_weight = exchanged(dw, NEAR).reshape(near * rows, cout)[:taps]
-    grad_weight = grad_weight.astype(F32).reshape(weight.shape)
+        [exchanged(big, FAR), par],
+    )
+    shift_gradient, gain_gradient = (shift.reshape(cout), tilt.reshape(cout))
     (grad_features,) = call(
         input_kernel,
         [shape((vx, my, 2, mz, width), BF)],
-        [dpre, xd, yd, zd, wmat, mask],
-        scratch=[pltpu.VMEM((mx + 1, my + 1, mz, cout), BF)] * 2,
-        flops=1_200_000_000,
-    )
+        [pre, cotangent, par, grads, xd, yd, zd, active, weight],
+        scratch=[
+            pltpu.VMEM((mx + 1, my + 1, mz, cout), BF),
+            pltpu.VMEM((mx + 1, my + 1, mz, cout), BF),
+            pltpu.VMEM((9 * width, 2 * cout), BF),
+        ],
+        flops=2_400_000_000,
+    )
+    mine, grad_features = lax.optimization_barrier((exchanged(dw, PLANE), grad_features))
+    other = moved(mine, "c", 1)
+    low = lax.axis_index("c") == 0
+    grad_weight = jnp.stack([jnp.where(low, mine, other), jnp.where(low, other, mine)])
+    grad_weight = grad_weight.reshape(near * rows, cout)[:taps]
+    grad_weight = grad_weight.astype(F32).reshape(weight.shape)
     grad_features = grad_features.reshape(features.shape)
     return (section_out, grad_features, grad_weight, gain_gradient, shift_gradient)
 

time: 118 us -> 113 us (0.958)
  blocking collectives: 48.5 us -> 38.6 us
  local copies, waits for them, and re-layouts: 6.12 us -> 0.81 us
  waiting for transfers between devices: 29.3 us -> 33.8 us
  starting transfers between devices: 20 us -> 22.8 us
  Pallas kernels: 11.6 us -> 14.3 us
    all_to_all x3 -> x2, blocking collectives: 48.5 us -> 38.6 us  [exchanged(): return lax.all_to_all(value, axes, 0, 0)]
    all_to_all x2 -> x3, waiting for transfers between devices: 13.9 us -> 22.4 us  [exchanged(): return lax.all_to_all(value, axes, 0, 0)]
    ppermute x6 -> x7, waiting for transfers between devices: 15.4 us -> 11.4 us  [moved(): lax.ppermute(value, axes, [(i, (i + by) % count) for i in range(count)])]
    unnamed x20 -> x12, local copies, waits for them, and re-layouts: 3.7 us -> 0.68 us
    all_to_all x2 -> x3, starting transfers between devices: 8.05 us -> 10.7 us  [exchanged(): return lax.all_to_all(value, axes, 0, 0)]
    pallas_call x1, Pallas kernels: 0.32 us -> 2.01 us  [local(): pl.pallas_call(face_kernel, out_shape=shape((2, my + 1, mz, width), BF),...]
    slice x7 -> x1, local copies, waits for them, and re-layouts: 1.69 us -> 0.03 us  [local(): grad_weight = grad_weight.reshape(near * rows, cout)[:taps]]
    pallas_call x6 -> x7, Pallas kernels: 11.3 us -> 12.3 us  [call(): pl.pallas_call(kernel, out_shape=outs, in_specs=[pl.BlockSpec(memory_spac...]
  transfers between devices with their start and end apart: 8 -> 10, of which waited for: 7 -> 7; matrix products, arithmetic and copies ran while one was open for 1% -> 0% of each run, Pallas kernels for 4% -> 5%
where the time goes in v5:
time: 113 us; the launch traced here: 112 us
  blocking collectives  38.6 us (34%)
  waiting for transfers between devices  33.8 us (30%)
  starting transfers between devices  22.8 us (20%)
  Pallas kernels  14.3 us (13%)
  other arithmetic  1.26 us (1%)
    all_to_all x2, blocking collectives, exchanged(): return lax.all_to_all(value, axes, 0, 0)  38.6 us
    all_to_all x3, waiting for transfers between devices, exchanged(): return lax.all_to_all(value, axes, 0, 0)  22.4 us
    pallas_call x7, Pallas kernels, call(): pl.pallas_call(kernel, out_shape=outs, in_specs=[pl.BlockSpec(memory_spac...  12.3 us
    ppermute x7, starting transfers between devices, moved(): lax.ppermute(value, axes, [(i, (i + by) % count) for i in range(count)])  12.1 us
    ppermute x7, waiting for transfers between devices, moved(): lax.ppermute(value, axes, [(i, (i + by) % count) for i in range(count)])  11.4 us
    all_to_all x3, starting transfers between devices, exchanged(): return lax.all_to_all(value, axes, 0, 0)  10.7 us
  transfers between devices with their start and end apart: 10, of which 7 were waited for; matrix products, arithmetic and copies ran while one was open for 0% of the time, Pallas kernels for 5%

profile of v5, /device:TPU:1, one launch (start us, length us, event | category | flops | bytes accessed | tf_op | source)
XLA Modules:
  0.0 112.3 jit_solution(17023304156205450036)
XLA Ops:
  0.7 2.0 %shard_map.102 = bf16[2,17,16,128]{3,2,1,0:T(8,128)(2,1)} custom-call(bf16[8,32,16,128]{3,2,1,0:T(8,128)(2,1)} %feat.3, s32[8,32,32]{2,1,0:T(8,128)} %active.5), custom_call_target="tpu_custom_call" | custom-call | flops 10000000 | bytes 400000 | tf_op jit(solution)/shard_map/pallas_call | solution.py:538
  2.7 3.8 %collective-permute-start = (bf16[2,17,16,128]{3,2,1,0:T(8,128)(2,1)}, bf16[2,17,16,128]{3,2,1,0:T(8,128)(2,1)S(1)}, u32[]{:S(2)}, u32[]{:S(2)}) collective-permute-start(bf16[2,17,16,128]{3,2,1,0:T(8,128)(2,1)} %shard_map.102), channel_id=1, source_target_pairs={{0,16},{16,32},{32,48},{48,64},{64,80},{80,96},{96,112},{112,128},... | collective-permute-start | bytes 417800 | tf_op jit(solution)/shard_map/ppermute | solution.py:506
  7.2 1.8 %shard_map.101 = (bf16[8,2,16,16,128]{4,3,2,1,0:T(8,128)(2,1)S(1)}, bf16[4,16,16,128]{3,2,1,0:T(8,128)(2,1)S(1)}, bf16[8,2,16,128]{3,2,1,0:T(8,128)(2,1)S(1)}, f32[2,128]{1,0:T(2,128)S(1)}) custom-call(bf16[8,32,16,128]{3,2,1,0:T(8,128)(2,1)S(1)} %copy-done, s32[8,32,32]{2,1,0:T(8,128)S(1)} %copy-done.1, f32[1,128]{1,0:T(1,128)S(1)} %bitcast.39, ...), custom_call_target="tpu_custom_call" | custom-call | flops 100000000 | bytes 2459648 | tf_op jit(solution)/shard_map/pallas_call | solution.py:21
  9.0 6.4 %collective-permute-done.xh = bf16[2,17,16,128]{3,2,1,0:T(8,128)(2,1)S(1)} collective-permute-done((bf16[2,17,16,128]{3,2,1,0:T(8,128)(2,1)}, bf16[2,17,16,128]{3,2,1,0:T(8,128)(2,1)S(1)}, u32[]{:S(2)}, u32[]{:S(2)}) %collective-permute-start) | collective-permute-done | bytes 139296 | tf_op jit(solution)/shard_map/ppermute | solution.py:506
  15.5 2.3 %collective-permute-start.1 = (bf16[10,16,128]{2,1,0:T(8,128)(2,1)S(1)}, bf16[10,16,128]{2,1,0:T(8,128)(2,1)S(1)}, u32[]{:S(2)}, u32[]{:S(2)}) collective-permute-start(bf16[10,16,128]{2,1,0:T(8,128)(2,1)S(1)} %maximum_multiply_fusion.1), channel_id=1, source_target_pairs={{0,2},{2,4},{4,6},{6,8},{8,10},{10,12},{12,14},{14,0},{1,3},{3,5},... | collective-permute-start | bytes 122888 | tf_op jit(solution)/shard_map/ppermute | solution.py:506
  17.9 1.0 collective-permute-done.1.yh
  19.4 2.9 %collective-permute-done.2.zh = bf16[19,16,128]{2,1,0:T(8,128)(2,1)S(1)} collective-permute-done((bf16[19,16,128]{2,1,0:T(8,128)(2,1)S(1)}, bf16[19,16,128]{2,1,0:T(8,128)(2,1)S(1)}, u32[]{:S(2)}, u32[]{:S(2)}) %collective-permute-start.2) | collective-permute-done | bytes 77856 | tf_op jit(solution)/shard_map/ppermute | solution.py:506
  22.3 1.3 %shard_map.103 = (f32[4,16,16,128]{3,2,1,0:T(8,128)S(1)}, f32[32,3,128]{2,1,0:T(4,128)S(1)}, bf16[3,17,16,128]{3,2,1,0:T(8,128)(2,1)S(1)}, bf16[3,4,16,128]{3,2,...) custom-call(bf16[8,2,16,16,128]{4,3,2,1,0:T(8,128)(2,1)S(1)} %get-tuple-element.25.xin, ...), custom_call_target="tpu_custom_call" | custom-call | flops 1200000000 | bytes 3153920 | tf_op jit(solution)/shard_map/pallas_call | solution.py:21
  23.6 3.0 %collective-permute-start.3 = (bf16[3,17,16,128]{3,2,1,0:T(8,128)(2,1)S(1)}, bf16[3,17,16,128]{3,2,1,0:T(8,128)(2,1)S(1)}, u32[]{:S(2)}, u32[]{:S(2)}) collective-permute-start(bf16[3,17,16,128]{3,2,1,0:T(8,128)(2,1)S(1)} %get-tuple-element.30), channel_id=1, source_target_pairs={{0,240},{16,0},{32,16},{48,32},{64,48},{80,64},{96,80},{112,96},{1... | collective-permute-start | bytes 626696 | tf_op jit(solution)/shard_map/ppermute | solution.py:506
  26.6 16.1 %all_to_all.25.parts = f32[32,3,128]{2,1,0:T(4,128)S(1)} all-to-all(f32[32,3,128]{2,1,0:T(4,128)S(1)} %get-tuple-element.29), channel_id=1, replica_groups=mesh['z'=8,'yh'=2,'x'=4,'c'=2,'yl'=2] {'c','yh','x','yl'}, dimensions={0} | all-to-all | bytes 98304 | tf_op jit(solution)/shard_map/all_to_all | solution.py:520
  43.4 3.5 %all-to-all-start.1 = ((f32[8,3,128]{2,1,0:T(4,128)}), f32[8,3,128]{2,1,0:T(4,128)S(1)}, u32[]{:S(2)}, u32[]{:S(2)}) async-start(f32[8,3,128]{2,1,0:T(4,128)} %get-tuple-element.33), calls=%async_computation.1 | async-start | bytes 32768 | tf_op jit(solution)/shard_map/all_to_all | solution.py:520
  47.7 5.9 %all-to-all-done.1 = f32[8,3,128]{2,1,0:T(4,128)S(1)} async-done(((f32[8,3,128]{2,1,0:T(4,128)}), f32[8,3,128]{2,1,0:T(4,128)S(1)}, u32[]{:S(2)}, u32[]{:S(2)}) %all-to-all-start.1) | async-done | bytes 12320 | tf_op jit(solution)/shard_map/all_to_all | solution.py:520
  53.7 3.2 %shard_map.105 = (bf16[4,16,16,128]{3,2,1,0:T(8,128)(2,1)}, bf16[32,64,256]{2,1,0:T(8,128)(2,1)S(1)}, bf16[3,6,16,128]{3,2,1,0:T(8,128)(2,1)S(1)}) custom-call(f32[4,16,16,128]{3,2,1,0:T(8,128)S(1)} %get-tuple-element.28.pre, bf16[4,16,16,128]{3,2,1,0:T(8,128)(2,1)S(1)} %copy-done.5, f32[5,128]{1,0:T(8,128)S(1)} %pad_maximum_fusion.2.par, ...), custom_call_target="tpu_custom_call" | custom-call | flops 2400000000 | bytes 3811840 | tf_op jit(solution)/shard_map/pallas_call | solution.py:21
  56.9 22.5 %all_to_all.26.parts = bf16[32,64,256]{2,1,0:T(8,128)(2,1)S(1)} all-to-all(bf16[32,64,256]{2,1,0:T(8,128)(2,1)S(1)} %get-tuple-element.37), channel_id=1, replica_groups=mesh['z'=8,'yh'=2,'x'=4,'c'=2,'yl'=2] {'c','yh','x','yl'}, dimensions={0} | all-to-all | bytes 2097152 | tf_op jit(solution)/shard_map/all_to_all | solution.py:520
  79.4 1.3 %shard_map.106 = bf16[8,64,256]{2,1,0:T(8,128)(2,1)} custom-call(bf16[32,64,256]{2,1,0:T(8,128)(2,1)S(1)} %all_to_all.26.parts), custom_call_target="tpu_custom_call" | custom-call | flops 100000000 | bytes 1310720 | tf_op jit(solution)/shard_map/pallas_call | solution.py:21
  80.7 3.4 %all-to-all-start.3 = ((bf16[8,64,256]{2,1,0:T(8,128)(2,1)}), bf16[8,64,256]{2,1,0:T(8,128)(2,1)S(1)}, u32[]{:S(2)}, u32[]{:S(2)}) async-start(bf16[8,64,256]{2,1,0:T(8,128)(2,1)} %shard_map.106), calls=%async_computation.3 | async-start | bytes 524288 | tf_op jit(solution)/shard_map/all_to_all | solution.py:520
  84.2 12.2 %all-to-all-done.3.parts = bf16[8,64,256]{2,1,0:T(8,128)(2,1)S(1)} async-done(((bf16[8,64,256]{2,1,0:T(8,128)(2,1)}), bf16[8,64,256]{2,1,0:T(8,128)(2,1)S(1)}, u32[]{:S(2)}, u32[]{:S(2)}) %all-to-all-start.3) | async-done | bytes 262176 | tf_op jit(solution)/shard_map/all_to_all | solution.py:520
  96.4 1.1 shard_map.107
  97.4 3.7 %all-to-all-start.4 = ((bf16[16,56,128]{2,1,0:T(8,128)(2,1)}), bf16[16,56,128]{2,1,0:T(8,128)(2,1)S(1)}, u32[]{:S(2)}, u32[]{:S(2)}) async-start(bf16[16,56,128]{2,1,0:T(8,128)(2,1)} %get-tuple-element.38), calls=%async_computation.4 | async-start | bytes 458752 | tf_op jit(solution)/shard_map/all_to_all | solution.py:520
  101.2 3.0 %shard_map.108 = bf16[8,16,2,16,128]{4,3,2,1,0:T(8,128)(2,1)} custom-call(f32[4,16,16,128]{3,2,1,0:T(8,128)S(1)} %get-tuple-element.28.pre, bf16[4,16,16,128]{3,2,1,0:T(8,128)(2,1)S(1)} %copy-done.5, f32[5,128]{1,0:T(8,128)S(1)} %pad_maximum_fusion.2.par, f32[2,128]{1,0:T(2,128)S(1)} %get-tuple-element.39.grads, ...), custom_call_target="tpu_custom_call" | custom-call | flops 2400000000 | bytes 2670080 | tf_op jit(solution)/shard_map/pallas_call | solution.py:21
  104.1 4.4 %all-to-all-done.4 = bf16[16,56,128]{2,1,0:T(8,128)(2,1)S(1)} async-done(((bf16[16,56,128]{2,1,0:T(8,128)(2,1)}), bf16[16,56,128]{2,1,0:T(8,128)(2,1)S(1)}, u32[]{:S(2)}, u32[]{:S(2)}) %all-to-all-start.4) | async-done | bytes 229408 | tf_op jit(solution)/shard_map/all_to_all | solution.py:520
  108.5 1.6 %collective-permute-start.6 = (bf16[16,56,128]{2,1,0:T(8,128)(2,1)S(1)}, bf16[16,56,128]{2,1,0:T(8,128)(2,1)S(1)}, u32[]{:S(2)}, u32[]{:S(2)}) collective-permute-start(bf16[16,56,128]{2,1,0:T(8,128)(2,1)S(1)} %all-to-all-done.4), channel_id=1, source_target_pairs={{0,2},{2,0},{1,3},{3,1},{4,6},{6,4},{5,7},{7,5},{8,10},{10,8},{9,1... | collective-permute-start | bytes 688136 | tf_op jit(solution)/shard_map/ppermute | solution.py:506
  110.1 1.1 collective-permute-done.6
  111.3 1.0 convert.1
  (41 shorter events, 3.1 us)
Async XLA Ops:
  0.6 5.9 %copy-start.1 = (s32[8,32,32]{2,1,0:T(8,128)S(1)}, s32[8,32,32]{2,1,0:T(8,128)}, u32[]{:S(2)}) copy-start(s32[8,32,32]{2,1,0:T(8,128)} %active.5) | copy-start | bytes 98308
  0.6 5.9 %copy-start = (bf16[8,32,16,128]{3,2,1,0:T(8,128)(2,1)S(1)}, bf16[8,32,16,128]{3,2,1,0:T(8,128)(2,1)}, u32[]{:S(2)}) copy-start(bf16[8,32,16,128]{3,2,1,0:T(8,128)(2,1)} %feat.3) | copy-start | bytes 3145732
  2.7 12.7 %collective-permute-start = (bf16[2,17,16,128]{3,2,1,0:T(8,128)(2,1)}, bf16[2,17,16,128]{3,2,1,0:T(8,128)(2,1)S(1)}, u32[]{:S(2)}, u32[]{:S(2)}) collective-permute-start(bf16[2,17,16,128]{3,2,1,0:T(8,128)(2,1)} %shard_map.102), channel_id=1, source_target_pairs={{0,16},{16,32},{32,48},{48,64},{64,80},{80,96},{96,112},{112,128},... | collective-permute-start | bytes 417800 | tf_op jit(solution)/shard_map/ppermute | solution.py:506
  6.5 0.7 copy-start.2
  6.5 0.7 copy-start.3
  9.0 13.3 %copy-start.4 = (bf16[3,3,3,64,128]{4,3,2,1,0:T(8,128)(2,1)S(1)}, bf16[3,3,3,64,128]{4,3,2,1,0:T(8,128)(2,1)}, u32[]{:S(2)}) copy-start(bf16[3,3,3,64,128]{4,3,2,1,0:T(8,128)(2,1)} %weight.3) | copy-start | bytes 1327108
  15.5 6.8 %copy-start.5 = (bf16[4,16,16,128]{3,2,1,0:T(8,128)(2,1)S(1)}, bf16[4,16,16,128]{3,2,1,0:T(8,128)(2,1)}, u32[]{:S(2)}) copy-start(bf16[4,16,16,128]{3,2,1,0:T(8,128)(2,1)} %cot.5) | copy-start | bytes 786436
  15.5 3.4 %collective-permute-start.1 = (bf16[10,16,128]{2,1,0:T(8,128)(2,1)S(1)}, bf16[10,16,128]{2,1,0:T(8,128)(2,1)S(1)}, u32[]{:S(2)}, u32[]{:S(2)}) collective-permute-start(bf16[10,16,128]{2,1,0:T(8,128)(2,1)S(1)} %maximum_multiply_fusion.1), channel_id=1, source_target_pairs={{0,2},{2,4},{4,6},{6,8},{8,10},{10,12},{12,14},{14,0},{1,3},{3,5},... | collective-permute-start | bytes 122888 | tf_op jit(solution)/shard_map/ppermute | solution.py:506
  18.9 3.3 %collective-permute-start.2 = (bf16[19,16,128]{2,1,0:T(8,128)(2,1)S(1)}, bf16[19,16,128]{2,1,0:T(8,128)(2,1)S(1)}, u32[]{:S(2)}, u32[]{:S(2)}) collective-permute-start(bf16[19,16,128]{2,1,0:T(8,128)(2,1)S(1)} %maximum_multiply_fusion), channel_id=1, source_target_pairs={{0,1},{1,0},{2,3},{3,2},{4,5},{5,4},{6,7},{7,6},{8,9},{9,8},{10,11... | collective-permute-start | bytes 233480 | tf_op jit(solution)/shard_map/ppermute | solution.py:506
  23.6 19.1 %collective-permute-start.3 = (bf16[3,17,16,128]{3,2,1,0:T(8,128)(2,1)S(1)}, bf16[3,17,16,128]{3,2,1,0:T(8,128)(2,1)S(1)}, u32[]{:S(2)}, u32[]{:S(2)}) collective-permute-start(bf16[3,17,16,128]{3,2,1,0:T(8,128)(2,1)S(1)} %get-tuple-element.30), channel_id=1, source_target_pairs={{0,240},{16,0},{32,16},{48,32},{64,48},{80,64},{96,80},{112,96},{1... | collective-permute-start | bytes 626696 | tf_op jit(solution)/shard_map/ppermute | solution.py:506
  43.4 10.2 %all-to-all-start.1 = ((f32[8,3,128]{2,1,0:T(4,128)}), f32[8,3,128]{2,1,0:T(4,128)S(1)}, u32[]{:S(2)}, u32[]{:S(2)}) async-start(f32[8,3,128]{2,1,0:T(4,128)} %get-tuple-element.33), calls=%async_computation.1 | async-start | bytes 32768 | tf_op jit(solution)/shard_map/all_to_all | solution.py:520
  46.9 6.7 %collective-permute-start.4 = (bf16[3,6,16,128]{3,2,1,0:T(8,128)(2,1)S(1)}, bf16[3,6,16,128]{3,2,1,0:T(8,128)(2,1)S(1)}, u32[]{:S(2)}, u32[]{:S(2)}) collective-permute-start(bf16[3,6,16,128]{3,2,1,0:T(8,128)(2,1)S(1)} %get-tuple-element.35), channel_id=1, source_target_pairs={{0,14},{2,0},{4,2},{6,4},{8,6},{10,8},{12,10},{14,12},{1,15},{3,1}... | collective-permute-start | bytes 221192 | tf_op jit(solution)/shard_map/ppermute | solution.py:506
  80.7 15.7 %all-to-all-start.3 = ((bf16[8,64,256]{2,1,0:T(8,128)(2,1)}), bf16[8,64,256]{2,1,0:T(8,128)(2,1)S(1)}, u32[]{:S(2)}, u32[]{:S(2)}) async-start(bf16[8,64,256]{2,1,0:T(8,128)(2,1)} %shard_map.106), calls=%async_computation.3 | async-start | bytes 524288 | tf_op jit(solution)/shard_map/all_to_all | solution.py:520
  84.1 17.1 %collective-permute-start.5 = (bf16[3,6,16,128]{3,2,1,0:T(8,128)(2,1)S(1)}, bf16[3,6,16,128]{3,2,1,0:T(8,128)(2,1)S(1)}, u32[]{:S(2)}, u32[]{:S(2)}) collective-permute-start(bf16[3,6,16,128]{3,2,1,0:T(8,128)(2,1)S(1)} %get-tuple-element.40), channel_id=1, source_target_pairs={{0,1},{1,0},{2,3},{3,2},{4,5},{5,4},{6,7},{7,6},{8,9},{9,8},{10,11... | collective-permute-start | bytes 221192 | tf_op jit(solution)/shard_map/ppermute | solution.py:506
  97.4 11.1 %all-to-all-start.4 = ((bf16[16,56,128]{2,1,0:T(8,128)(2,1)}), bf16[16,56,128]{2,1,0:T(8,128)(2,1)S(1)}, u32[]{:S(2)}, u32[]{:S(2)}) async-start(bf16[16,56,128]{2,1,0:T(8,128)(2,1)} %get-tuple-element.38), calls=%async_computation.4 | async-start | bytes 458752 | tf_op jit(solution)/shard_map/all_to_all | solution.py:520
  108.5 2.7 %collective-permute-start.6 = (bf16[16,56,128]{2,1,0:T(8,128)(2,1)S(1)}, bf16[16,56,128]{2,1,0:T(8,128)(2,1)S(1)}, u32[]{:S(2)}, u32[]{:S(2)}) collective-permute-start(bf16[16,56,128]{2,1,0:T(8,128)(2,1)S(1)} %all-to-all-done.4), channel_id=1, source_target_pairs={{0,2},{2,0},{1,3},{3,1},{4,6},{6,4},{5,7},{7,5},{8,10},{10,8},{9,1... | collective-permute-start | bytes 688136 | tf_op jit(solution)/shard_map/ppermute | solution.py:506

commit v6 on v5

--- a/solution.py
+++ b/solution.py
@@ -324,18 +324,11 @@
     return jnp.where(lax.broadcasted_iota(jnp.int32, (8, row.shape[1]), 0) == 0, eight(row), 0.0)
 
 
-def slope_kernel(
-    pre, cot, par, xin, xh, yh, zh, xd, yd, zface, out, big, zplane, slope, acc
-):
+def slope_kernel(pre, cot, par, out, slope, sums):
     mx, my, mz, cout = pre.shape
-    width = xin.shape[4]
-    half = width // 2
     rows = my * mz
     mean, rstd, gain, bias = (par[i : i + 1] for i in range(4))
     first, second, count, high, square = (jnp.zeros((1, cout), F32) for _ in range(5))
-    zplane[:, :mx] = zface[...]
-    zplane[:, mx] = xd[:, my]
-    zplane[:, mx + 1] = yd[:, mx + 1]
     for m in range(mx):
         on, hat = standardized(pre[m].reshape(rows, cout), mean, rstd)
         normed = hat * gain + bias
@@ -346,8 +339,24 @@
         first = first + jnp.sum(tilt, axis=0, keepdims=True)
         second = second + jnp.sum(tilt * hat, axis=0, keepdims=True)
         count = count + jnp.sum(on, axis=0, keepdims=True)
-        high = high + jnp.sum(on * hat, axis=0, keepdims=True)
-        square = square + jnp.sum(on * hat * hat, axis=0, keepdims=True)
+        high = high + jnp.sum(hat, axis=0, keepdims=True)
+        square = square + jnp.sum(hat * hat, axis=0, keepdims=True)
+    sums[...] = jnp.concatenate([first, second, count, high, square] + [jnp.zeros((3, cout), F32)], axis=0)
+
+
+def product_kernel(
+    pre, slope, sums, others, par, xin, xh, yh, zh, xd, yd, zface, keep, send, zplane, acc, big
+):
+    mx, my, mz, cout = pre.shape
+    width = xin.shape[4]
+    half = width // 2
+    rows = my * mz
+    mean, rstd = (par[i : i + 1] for i in range(2))
+    zplane[:, :mx] = zface[...]
+    zplane[:, mx] = xd[:, my]
+    zplane[:, mx + 1] = yd[:, mx + 1]
+    both = sums[...] + others[...]
+    first, second, count, high, square = (both[i : i + 1] for i in range(5))
     some = jnp.maximum(count, 1.0)
     alpha = first / some
     high = rounded(high / some)
@@ -363,13 +372,13 @@
         here, after = ([], [])
         for i, part in enumerate((rest, hat, on)):
             held = part.astype(BF)
-            keep = 8 if i == 2 else cout
+            lines = 8 if i == 2 else cout
             wide = held.astype(F32)
             rims[i].append(rows_at(wide.reshape(my, mz, cout), 0))
             nxt = pltpu.roll(wide, rows - 1, 0).reshape(my, mz, cout)
             nxt = jnp.where(last, 0.0, nxt).reshape(rows, cout)
-            here.append(wide.T[:keep])
-            after.append(nxt.T[:keep])
+            here.append(wide.T[:lines])
+            after.append(nxt.T[:lines])
         right = jnp.concatenate(here + after, axis=0).astype(BF)
         left = jnp.concatenate(
             [tile_of(xin, xh, yh, 2 * m + a, b).reshape(rows, width) for a, b in TAPS], axis=1
@@ -398,9 +407,9 @@
         acc[half * taps :] = jnp.zeros((acc.shape[0] - half * taps, 2 * cout), F32)
     common = common_rows(first, second, alpha, beta, high)
     lane = lax.broadcasted_iota(jnp.int32, (8, width), 1)
-    near, depth, _ = big.shape
+    _, plane, depth, _ = big.shape
     depth = depth - 8
-    for n in range(near):
+    for n in range(2 * plane):
         column = jnp.zeros((8, width), F32)
         for tap in range(taps):
             start = half * tap - depth * n
@@ -412,7 +421,21 @@
                 if shift:
                     row = pltpu.roll(row, shift, 1)
                 column = jnp.where((lane >= lo) & (lane < hi), row, column)
-        write_chunk(big, n, acc[depth * n : depth * (n + 1)], column, common)
+        write_chunk(big.at[n // plane], n % plane, acc[depth * n : depth * (n + 1)], column, common)
+    core = lax.axis_index("c")
+    keep[...] = big[core]
+    send[...] = big[1 - core]
+
+
+def pair_kernel(mine, other, out):
+    _, depth, width = mine.shape
+    rows = depth - 8
+    cout = width // 2
+    for i in range(mine.shape[0]):
+        value = mine[i].astype(F32)
+        both = value + other[i].astype(F32)
+        column = both[rows : rows + 1, :cout] + both[rows + 1 : rows + 2, :cout] + both[rows + 2 : rows + 3, :cout]
+        write_chunk(out, i, both[:rows], eight(column), (value[rows:, :cout], value[rows:, cout:]))
 
 
 def near_kernel(parts, out):
@@ -592,21 +615,24 @@
     par = jnp.stack([mean, rstd, norm[0], norm[1], count])
     taps = 27 * cin
     rows = -(-taps // (8 * near)) * 8
-    section_out, big, zplane = call(
+    section_out, slope, sums = call(
         slope_kernel,
-        [
-            shape((mx, my, mz, cout), BF),
-            shape((near, rows + 8, 2 * cout), BF),
-            shape((3, mx + 2, my, cout), BF),
-        ],
-        [pre, cotangent, par, xin, xh, yh, zh, xd, yd, zface],
-        scratch=[pltpu.VMEM(pre.shape, F32), pltpu.VMEM((near * rows, 2 * cout), F32)],
+        [shape((mx, my, mz, cout), BF), shape((mx, my, mz, cout), F32), shape((8, cout), F32)],
+        [pre, cotangent, par],
+    )
+    plane = lax.axis_size(PLANE)
+    chunks = (plane, rows + 8, 2 * cout)
+    big, send, zplane = call(
+        product_kernel,
+        [shape(chunks, BF), shape(chunks, BF), shape((3, mx + 2, my, cout), BF)],
+        [pre, slope, sums, moved(sums, "c", 1), par, xin, xh, yh, zh, xd, yd, zface],
+        scratch=[pltpu.VMEM((near * rows, 2 * cout), F32), pltpu.VMEM((2,) + chunks, BF)],
         flops=2_400_000_000,
     )
+    (big,) = call(pair_kernel, [shape(chunks, BF)], [big, moved(send, "c", 1)])
     zd = moved(zplane, GZ, -1)
     far = lax.axis_size(FAR)
-    (big,) = call(near_kernel, [shape((far, rows + 8, 2 * cout), BF)], [exchanged(big, NEAR)])
-    plane = lax.axis_size(PLANE)
+    (big,) = call(near_kernel, [shape((far, rows + 8, 2 * cout), BF)], [exchanged(big, PLANE)])
     dw, shift, tilt, grads = call(
         far_kernel,
         [

time: 113 us -> 108 us (0.956)
  blocking collectives: 38.6 us -> 29.7 us
  starting transfers between devices: 22.8 us -> 28 us
    all_to_all x2, blocking collectives: 38.6 us -> 29.7 us  [exchanged(): return lax.all_to_all(value, axes, 0, 0)]
    ppermute x7 -> x9, starting transfers between devices: 12.1 us -> 17.3 us  [moved(): lax.ppermute(value, axes, [(i, (i + by) % count) for i in range(count)])]
    all_to_all x3, waiting for transfers between devices: 22.4 us -> 19.2 us  [exchanged(): return lax.all_to_all(value, axes, 0, 0)]
    ppermute x7 -> x9, waiting for transfers between devices: 11.4 us -> 13.8 us  [moved(): lax.ppermute(value, axes, [(i, (i + by) % count) for i in range(count)])]
    pallas_call x7 -> x9, Pallas kernels: 12.3 us -> 12.4 us  [call(): pl.pallas_call(kernel, out_shape=outs, in_specs=[pl.BlockSpec(memory_spac...]
  transfers between devices with their start and end apart: 10 -> 12, of which waited for: 7 -> 9; matrix products, arithmetic and copies ran while one was open for 0% -> 0% of each run, Pallas kernels for 5% -> 6%
where the time goes in v6:
time: 108 us
  waiting for transfers between devices  33 us (31%)
  blocking collectives  29.7 us (28%)
  starting transfers between devices  28 us (26%)
  Pallas kernels  14.4 us (13%)
  other arithmetic  1.26 us (1%)
    all_to_all x2, blocking collectives, exchanged(): return lax.all_to_all(value, axes, 0, 0)  29.7 us
    all_to_all x3, waiting for transfers between devices, exchanged(): return lax.all_to_all(value, axes, 0, 0)  19.2 us
    ppermute x9, starting transfers between devices, moved(): lax.ppermute(value, axes, [(i, (i + by) % count) for i in range(count)])  17.3 us
    ppermute x9, waiting for transfers between devices, moved(): lax.ppermute(value, axes, [(i, (i + by) % count) for i in range(count)])  13.8 us
    pallas_call x9, Pallas kernels, call(): pl.pallas_call(kernel, out_shape=outs, in_specs=[pl.BlockSpec(memory_spac...  12.4 us
    all_to_all x3, starting transfers between devices, exchanged(): return lax.all_to_all(value, axes, 0, 0)  10.7 us
  transfers between devices with their start and end apart: 12, of which 9 were waited for; matrix products, arithmetic and copies ran while one was open for 0% of the time, Pallas kernels for 6%

profile of v6, /device:TPU:1, one launch (start us, length us, event | category | flops | bytes accessed | tf_op | source)
XLA Modules:
  0.0 108.0 jit_solution(8135825110226959830)
XLA Ops:
  0.7 2.0 %shard_map.102 = bf16[2,17,16,128]{3,2,1,0:T(8,128)(2,1)} custom-call(bf16[8,32,16,128]{3,2,1,0:T(8,128)(2,1)} %feat.3, s32[8,32,32]{2,1,0:T(8,128)} %active.5), custom_call_target="tpu_custom_call" | custom-call | flops 10000000 | bytes 400000 | tf_op jit(solution)/shard_map/pallas_call | solution.py:561
  2.7 3.8 %collective-permute-start = (bf16[2,17,16,128]{3,2,1,0:T(8,128)(2,1)}, bf16[2,17,16,128]{3,2,1,0:T(8,128)(2,1)S(1)}, u32[]{:S(2)}, u32[]{:S(2)}) collective-permute-start(bf16[2,17,16,128]{3,2,1,0:T(8,128)(2,1)} %shard_map.102), channel_id=1, source_target_pairs={{0,16},{16,32},{32,48},{48,64},{64,80},{80,96},{96,112},{112,128},... | collective-permute-start | bytes 417800 | tf_op jit(solution)/shard_map/ppermute | solution.py:529
  7.2 1.8 %shard_map.101 = (bf16[8,2,16,16,128]{4,3,2,1,0:T(8,128)(2,1)S(1)}, bf16[4,16,16,128]{3,2,1,0:T(8,128)(2,1)S(1)}, bf16[8,2,16,128]{3,2,1,0:T(8,128)(2,1)S(1)}, f32[2,128]{1,0:T(2,128)S(1)}) custom-call(bf16[8,32,16,128]{3,2,1,0:T(8,128)(2,1)S(1)} %copy-done, s32[8,32,32]{2,1,0:T(8,128)S(1)} %copy-done.1, f32[1,128]{1,0:T(1,128)S(1)} %bitcast.39, ...), custom_call_target="tpu_custom_call" | custom-call | flops 100000000 | bytes 2459648 | tf_op jit(solution)/shard_map/pallas_call | solution.py:21
  9.0 6.4 %collective-permute-done.xh = bf16[2,17,16,128]{3,2,1,0:T(8,128)(2,1)S(1)} collective-permute-done((bf16[2,17,16,128]{3,2,1,0:T(8,128)(2,1)}, bf16[2,17,16,128]{3,2,1,0:T(8,128)(2,1)S(1)}, u32[]{:S(2)}, u32[]{:S(2)}) %collective-permute-start) | collective-permute-done | bytes 139296 | tf_op jit(solution)/shard_map/ppermute | solution.py:529
  15.5 2.3 %collective-permute-start.1 = (bf16[10,16,128]{2,1,0:T(8,128)(2,1)S(1)}, bf16[10,16,128]{2,1,0:T(8,128)(2,1)S(1)}, u32[]{:S(2)}, u32[]{:S(2)}) collective-permute-start(bf16[10,16,128]{2,1,0:T(8,128)(2,1)S(1)} %maximum_multiply_fusion.1), channel_id=1, source_target_pairs={{0,2},{2,4},{4,6},{6,8},{8,10},{10,12},{12,14},{14,0},{1,3},{3,5},... | collective-permute-start | bytes 122888 | tf_op jit(solution)/shard_map/ppermute | solution.py:529
  19.4 2.9 %collective-permute-done.2.zh = bf16[19,16,128]{2,1,0:T(8,128)(2,1)S(1)} collective-permute-done((bf16[19,16,128]{2,1,0:T(8,128)(2,1)S(1)}, bf16[19,16,128]{2,1,0:T(8,128)(2,1)S(1)}, u32[]{:S(2)}, u32[]{:S(2)}) %collective-permute-start.2) | collective-permute-done | bytes 77856 | tf_op jit(solution)/shard_map/ppermute | solution.py:529
  22.3 1.3 %shard_map.103 = (f32[4,16,16,128]{3,2,1,0:T(8,128)S(1)}, f32[32,3,128]{2,1,0:T(4,128)S(1)}, bf16[3,17,16,128]{3,2,1,0:T(8,128)(2,1)S(1)}, bf16[3,4,16,128]{3,2,...) custom-call(bf16[8,2,16,16,128]{4,3,2,1,0:T(8,128)(2,1)S(1)} %get-tuple-element.28.xin, ...), custom_call_target="tpu_custom_call" | custom-call | flops 1200000000 | bytes 3153920 | tf_op jit(solution)/shard_map/pallas_call | solution.py:21
  23.6 3.0 %collective-permute-start.3 = (bf16[3,17,16,128]{3,2,1,0:T(8,128)(2,1)S(1)}, bf16[3,17,16,128]{3,2,1,0:T(8,128)(2,1)S(1)}, u32[]{:S(2)}, u32[]{:S(2)}) collective-permute-start(bf16[3,17,16,128]{3,2,1,0:T(8,128)(2,1)S(1)} %get-tuple-element.33), channel_id=1, source_target_pairs={{0,240},{16,0},{32,16},{48,32},{64,48},{80,64},{96,80},{112,96},{1... | collective-permute-start | bytes 626696 | tf_op jit(solution)/shard_map/ppermute | solution.py:529
  26.6 16.1 %all_to_all.25.parts = f32[32,3,128]{2,1,0:T(4,128)S(1)} all-to-all(f32[32,3,128]{2,1,0:T(4,128)S(1)} %get-tuple-element.32), channel_id=1, replica_groups=mesh['z'=8,'yh'=2,'x'=4,'c'=2,'yl'=2] {'c','yh','x','yl'}, dimensions={0} | all-to-all | bytes 98304 | tf_op jit(solution)/shard_map/all_to_all | solution.py:543
  43.4 3.5 %all-to-all-start.1 = ((f32[8,3,128]{2,1,0:T(4,128)}), f32[8,3,128]{2,1,0:T(4,128)S(1)}, u32[]{:S(2)}, u32[]{:S(2)}) async-start(f32[8,3,128]{2,1,0:T(4,128)} %get-tuple-element.36), calls=%async_computation.1 | async-start | bytes 32768 | tf_op jit(solution)/shard_map/all_to_all | solution.py:543
  47.7 5.9 %all-to-all-done.1 = f32[8,3,128]{2,1,0:T(4,128)S(1)} async-done(((f32[8,3,128]{2,1,0:T(4,128)}), f32[8,3,128]{2,1,0:T(4,128)S(1)}, u32[]{:S(2)}, u32[]{:S(2)}) %all-to-all-start.1) | async-done | bytes 12320 | tf_op jit(solution)/shard_map/all_to_all | solution.py:543
  54.7 1.9 %collective-permute-start.4 = (f32[8,128]{1,0:T(8,128)S(1)}, f32[8,128]{1,0:T(8,128)S(1)}, u32[]{:S(2)}, u32[]{:S(2)}) collective-permute-start(f32[8,128]{1,0:T(8,128)S(1)} %get-tuple-element.40.sums), channel_id=1, source_target_pairs={{0,2},{2,0},{1,3},{3,1},{4,6},{6,4},{5,7},{7,5},{8,10},{10,8},{9,1... | collective-permute-start | bytes 12296 | tf_op jit(solution)/shard_map/ppermute | solution.py:529
  57.4 2.3 %shard_map.106 = (bf16[16,64,256]{2,1,0:T(8,128)(2,1)S(1)}, bf16[16,64,256]{2,1,0:T(8,128)(2,1)S(1)}, bf16[3,6,16,128]{3,2,1,0:T(8,128)(2,1)S(1)}) custom-call(f32[4,16,16,128]{3,2,1,0:T(8,128)S(1)} %get-tuple-element.31.pre, f32[4,16,16,128]{3,2,1,0:T(8,128)S(1)} %get-tuple-element.39.slope, f32[8,128]{1,0:T(8,128)S(1)} %get-tuple-element.40.sums, ...), custom_call_target="tpu_custom_call" | custom-call | flops 2400000000 | bytes 3820032 | tf_op jit(solution)/shard_map/pallas_call | solution.py:21
  60.1 1.6 %collective-permute-done.6.other = bf16[16,64,256]{2,1,0:T(8,128)(2,1)S(1)} collective-permute-done((bf16[16,64,256]{2,1,0:T(8,128)(2,1)S(1)}, bf16[16,64,256]{2,1,0:T(8,128)(2,1)S(1)}, u32[]{:S(2)}, u32[]{:S(2)}) %collective-permute-start.6) | collective-permute-done | bytes 524320 | tf_op jit(solution)/shard_map/ppermute | solution.py:529
  61.9 13.6 %all_to_all.26.parts = bf16[16,64,256]{2,1,0:T(8,128)(2,1)S(1)} all-to-all(bf16[16,64,256]{2,1,0:T(8,128)(2,1)S(1)} %shard_map.107), channel_id=1, replica_groups=mesh['z'=8,'yh'=2,'x'=4,'c'=2,'yl'=2] {'yh','x','yl'}, dimensions={0} | all-to-all | bytes 1048576 | tf_op jit(solution)/shard_map/all_to_all | solution.py:543
  75.5 1.2 %shard_map.108 = bf16[8,64,256]{2,1,0:T(8,128)(2,1)} custom-call(bf16[16,64,256]{2,1,0:T(8,128)(2,1)S(1)} %all_to_all.26.parts), custom_call_target="tpu_custom_call" | custom-call | flops 100000000 | bytes 786432 | tf_op jit(solution)/shard_map/pallas_call | solution.py:21
  76.6 3.4 %all-to-all-start.3 = ((bf16[8,64,256]{2,1,0:T(8,128)(2,1)}), bf16[8,64,256]{2,1,0:T(8,128)(2,1)S(1)}, u32[]{:S(2)}, u32[]{:S(2)}) async-start(bf16[8,64,256]{2,1,0:T(8,128)(2,1)} %shard_map.108), calls=%async_computation.3 | async-start | bytes 524288 | tf_op jit(solution)/shard_map/all_to_all | solution.py:543
  80.4 9.3 %all-to-all-done.3.parts = bf16[8,64,256]{2,1,0:T(8,128)(2,1)S(1)} async-done(((bf16[8,64,256]{2,1,0:T(8,128)(2,1)}), bf16[8,64,256]{2,1,0:T(8,128)(2,1)S(1)}, u32[]{:S(2)}, u32[]{:S(2)}) %all-to-all-start.3) | async-done | bytes 262176 | tf_op jit(solution)/shard_map/all_to_all | solution.py:543
  89.7 1.1 shard_map.109
  90.8 3.7 %all-to-all-start.4 = ((bf16[16,56,128]{2,1,0:T(8,128)(2,1)}), bf16[16,56,128]{2,1,0:T(8,128)(2,1)S(1)}, u32[]{:S(2)}, u32[]{:S(2)}) async-start(bf16[16,56,128]{2,1,0:T(8,128)(2,1)} %get-tuple-element.44), calls=%async_computation.4 | async-start | bytes 458752 | tf_op jit(solution)/shard_map/all_to_all | solution.py:543
  94.5 3.0 %shard_map.110 = bf16[8,16,2,16,128]{4,3,2,1,0:T(8,128)(2,1)} custom-call(f32[4,16,16,128]{3,2,1,0:T(8,128)S(1)} %get-tuple-element.31.pre, bf16[4,16,16,128]{3,2,1,0:T(8,128)(2,1)S(1)} %copy-done.2, f32[5,128]{1,0:T(8,128)S(1)} %pad_maximum_fusion.2.par, f32[2,128]{1,0:T(2,128)S(1)} %get-tuple-element.45.grads, ...), custom_call_target="tpu_custom_call" | custom-call | flops 2400000000 | bytes 2670080 | tf_op jit(solution)/shard_map/pallas_call | solution.py:21
  97.5 4.0 %all-to-all-done.4 = bf16[16,56,128]{2,1,0:T(8,128)(2,1)S(1)} async-done(((bf16[16,56,128]{2,1,0:T(8,128)(2,1)}), bf16[16,56,128]{2,1,0:T(8,128)(2,1)S(1)}, u32[]{:S(2)}, u32[]{:S(2)}) %all-to-all-start.4) | async-done | bytes 229408 | tf_op jit(solution)/shard_map/all_to_all | solution.py:543
  101.5 4.3 %collective-permute-start.8 = (bf16[16,56,128]{2,1,0:T(8,128)(2,1)S(1)}, bf16[16,56,128]{2,1,0:T(8,128)(2,1)S(1)}, u32[]{:S(2)}, u32[]{:S(2)}) collective-permute-start(bf16[16,56,128]{2,1,0:T(8,128)(2,1)S(1)} %all-to-all-done.4), channel_id=1, source_target_pairs={{0,2},{2,0},{1,3},{3,1},{4,6},{6,4},{5,7},{7,5},{8,10},{10,8},{9,1... | collective-permute-start | bytes 688136 | tf_op jit(solution)/shard_map/ppermute | solution.py:529
  105.7 1.1 %collective-permute-done.8 = bf16[16,56,128]{2,1,0:T(8,128)(2,1)S(1)} collective-permute-done((bf16[16,56,128]{2,1,0:T(8,128)(2,1)S(1)}, bf16[16,56,128]{2,1,0:T(8,128)(2,1)S(1)}, u32[]{:S(2)}, u32[]{:S(2)}) %collective-permute-start.8) | collective-permute-done | bytes 229408 | tf_op jit(solution)/shard_map/ppermute | solution.py:529
  (47 shorter events, 7.7 us)
Async XLA Ops:
  0.6 5.9 %copy-start.1 = (s32[8,32,32]{2,1,0:T(8,128)S(1)}, s32[8,32,32]{2,1,0:T(8,128)}, u32[]{:S(2)}) copy-start(s32[8,32,32]{2,1,0:T(8,128)} %active.5) | copy-start | bytes 98308
  0.6 5.9 %copy-start = (bf16[8,32,16,128]{3,2,1,0:T(8,128)(2,1)S(1)}, bf16[8,32,16,128]{3,2,1,0:T(8,128)(2,1)}, u32[]{:S(2)}) copy-start(bf16[8,32,16,128]{3,2,1,0:T(8,128)(2,1)} %feat.3) | copy-start | bytes 3145732
  2.7 12.7 %collective-permute-start = (bf16[2,17,16,128]{3,2,1,0:T(8,128)(2,1)}, bf16[2,17,16,128]{3,2,1,0:T(8,128)(2,1)S(1)}, u32[]{:S(2)}, u32[]{:S(2)}) collective-permute-start(bf16[2,17,16,128]{3,2,1,0:T(8,128)(2,1)} %shard_map.102), channel_id=1, source_target_pairs={{0,16},{16,32},{32,48},{48,64},{64,80},{80,96},{96,112},{112,128},... | collective-permute-start | bytes 417800 | tf_op jit(solution)/shard_map/ppermute | solution.py:529
  6.5 0.7 copy-start.3
  6.5 0.7 copy-start.4
  9.0 13.3 %copy-start.5 = (bf16[3,3,3,64,128]{4,3,2,1,0:T(8,128)(2,1)S(1)}, bf16[3,3,3,64,128]{4,3,2,1,0:T(8,128)(2,1)}, u32[]{:S(2)}) copy-start(bf16[3,3,3,64,128]{4,3,2,1,0:T(8,128)(2,1)} %weight.3) | copy-start | bytes 1327108
  15.5 6.8 %copy-start.2 = (bf16[4,16,16,128]{3,2,1,0:T(8,128)(2,1)S(1)}, bf16[4,16,16,128]{3,2,1,0:T(8,128)(2,1)}, u32[]{:S(2)}) copy-start(bf16[4,16,16,128]{3,2,1,0:T(8,128)(2,1)} %cot.5) | copy-start | bytes 786436
  15.5 3.4 %collective-permute-start.1 = (bf16[10,16,128]{2,1,0:T(8,128)(2,1)S(1)}, bf16[10,16,128]{2,1,0:T(8,128)(2,1)S(1)}, u32[]{:S(2)}, u32[]{:S(2)}) collective-permute-start(bf16[10,16,128]{2,1,0:T(8,128)(2,1)S(1)} %maximum_multiply_fusion.1), channel_id=1, source_target_pairs={{0,2},{2,4},{4,6},{6,8},{8,10},{10,12},{12,14},{14,0},{1,3},{3,5},... | collective-permute-start | bytes 122888 | tf_op jit(solution)/shard_map/ppermute | solution.py:529
  18.9 3.3 %collective-permute-start.2 = (bf16[19,16,128]{2,1,0:T(8,128)(2,1)S(1)}, bf16[19,16,128]{2,1,0:T(8,128)(2,1)S(1)}, u32[]{:S(2)}, u32[]{:S(2)}) collective-permute-start(bf16[19,16,128]{2,1,0:T(8,128)(2,1)S(1)} %maximum_multiply_fusion), channel_id=1, source_target_pairs={{0,1},{1,0},{2,3},{3,2},{4,5},{5,4},{6,7},{7,6},{8,9},{9,8},{10,11... | collective-permute-start | bytes 233480 | tf_op jit(solution)/shard_map/ppermute | solution.py:529
  23.6 19.1 %collective-permute-start.3 = (bf16[3,17,16,128]{3,2,1,0:T(8,128)(2,1)S(1)}, bf16[3,17,16,128]{3,2,1,0:T(8,128)(2,1)S(1)}, u32[]{:S(2)}, u32[]{:S(2)}) collective-permute-start(bf16[3,17,16,128]{3,2,1,0:T(8,128)(2,1)S(1)} %get-tuple-element.33), channel_id=1, source_target_pairs={{0,240},{16,0},{32,16},{48,32},{64,48},{80,64},{96,80},{112,96},{1... | collective-permute-start | bytes 626696 | tf_op jit(solution)/shard_map/ppermute | solution.py:529
  43.4 10.2 %all-to-all-start.1 = ((f32[8,3,128]{2,1,0:T(4,128)}), f32[8,3,128]{2,1,0:T(4,128)S(1)}, u32[]{:S(2)}, u32[]{:S(2)}) async-start(f32[8,3,128]{2,1,0:T(4,128)} %get-tuple-element.36), calls=%async_computation.1 | async-start | bytes 32768 | tf_op jit(solution)/shard_map/all_to_all | solution.py:543
  46.9 10.5 %collective-permute-start.5 = (bf16[3,6,16,128]{3,2,1,0:T(8,128)(2,1)S(1)}, bf16[3,6,16,128]{3,2,1,0:T(8,128)(2,1)S(1)}, u32[]{:S(2)}, u32[]{:S(2)}) collective-permute-start(bf16[3,6,16,128]{3,2,1,0:T(8,128)(2,1)S(1)} %get-tuple-element.41), channel_id=1, source_target_pairs={{0,14},{2,0},{4,2},{6,4},{8,6},{10,8},{12,10},{14,12},{1,15},{3,1}... | collective-permute-start | bytes 221192 | tf_op jit(solution)/shard_map/ppermute | solution.py:529
  54.7 2.7 %collective-permute-start.4 = (f32[8,128]{1,0:T(8,128)S(1)}, f32[8,128]{1,0:T(8,128)S(1)}, u32[]{:S(2)}, u32[]{:S(2)}) collective-permute-start(f32[8,128]{1,0:T(8,128)S(1)} %get-tuple-element.40.sums), channel_id=1, source_target_pairs={{0,2},{2,0},{1,3},{3,1},{4,6},{6,4},{5,7},{7,5},{8,10},{10,8},{9,1... | collective-permute-start | bytes 12296 | tf_op jit(solution)/shard_map/ppermute | solution.py:529
  59.7 2.0 %collective-permute-start.6 = (bf16[16,64,256]{2,1,0:T(8,128)(2,1)S(1)}, bf16[16,64,256]{2,1,0:T(8,128)(2,1)S(1)}, u32[]{:S(2)}, u32[]{:S(2)}) collective-permute-start(bf16[16,64,256]{2,1,0:T(8,128)(2,1)S(1)} %get-tuple-element.43), channel_id=1, source_target_pairs={{0,2},{2,0},{1,3},{3,1},{4,6},{6,4},{5,7},{7,5},{8,10},{10,8},{9,1... | collective-permute-start | bytes 1572872 | tf_op jit(solution)/shard_map/ppermute | solution.py:529
  76.6 13.1 %all-to-all-start.3 = ((bf16[8,64,256]{2,1,0:T(8,128)(2,1)}), bf16[8,64,256]{2,1,0:T(8,128)(2,1)S(1)}, u32[]{:S(2)}, u32[]{:S(2)}) async-start(bf16[8,64,256]{2,1,0:T(8,128)(2,1)} %shard_map.108), calls=%async_computation.3 | async-start | bytes 524288 | tf_op jit(solution)/shard_map/all_to_all | solution.py:543
  80.1 14.4 %collective-permute-start.7 = (bf16[3,6,16,128]{3,2,1,0:T(8,128)(2,1)S(1)}, bf16[3,6,16,128]{3,2,1,0:T(8,128)(2,1)S(1)}, u32[]{:S(2)}, u32[]{:S(2)}) collective-permute-start(bf16[3,6,16,128]{3,2,1,0:T(8,128)(2,1)S(1)} %get-tuple-element.46), channel_id=1, source_target_pairs={{0,1},{1,0},{2,3},{3,2},{4,5},{5,4},{6,7},{7,6},{8,9},{9,8},{10,11... | collective-permute-start | bytes 221192 | tf_op jit(solution)/shard_map/ppermute | solution.py:529
  90.8 10.7 %all-to-all-start.4 = ((bf16[16,56,128]{2,1,0:T(8,128)(2,1)}), bf16[16,56,128]{2,1,0:T(8,128)(2,1)S(1)}, u32[]{:S(2)}, u32[]{:S(2)}) async-start(bf16[16,56,128]{2,1,0:T(8,128)(2,1)} %get-tuple-element.44), calls=%async_computation.4 | async-start | bytes 458752 | tf_op jit(solution)/shard_map/all_to_all | solution.py:543
  101.5 5.4 %collective-permute-start.8 = (bf16[16,56,128]{2,1,0:T(8,128)(2,1)S(1)}, bf16[16,56,128]{2,1,0:T(8,128)(2,1)S(1)}, u32[]{:S(2)}, u32[]{:S(2)}) collective-permute-start(bf16[16,56,128]{2,1,0:T(8,128)(2,1)S(1)} %all-to-all-done.4), channel_id=1, source_target_pairs={{0,2},{2,0},{1,3},{3,1},{4,6},{6,4},{5,7},{7,5},{8,10},{10,8},{9,1... | collective-permute-start | bytes 688136 | tf_op jit(solution)/shard_map/ppermute | solution.py:529

commit v7 on v5

--- a/solution.py
+++ b/solution.py
@@ -95,9 +95,9 @@
         copy.start()
     keep = unless(ring_index(GX) == ring_size(GX) - 1)
     pick = row_picker(my, mz, mz - 1)
-    for copy in copies:
-        copy.wait()
+    copies[1].wait()
     m = mask_row(cells[...], mz, width)
+    copies[0].wait()
     value = row[...].reshape(m.shape) * m
     for py in range(2):
         held = (value[:, py].astype(F32) * keep).astype(BF)
@@ -173,9 +173,8 @@
     return cot * sig * (1.0 + normed * (1.0 - sig))
 
 
-def rim_parts(value, on, cot):
-    high, low = split(value, 2)
-    return [part.astype(BF) for part in (jnp.where(on > 0.0, high, OFF), low, cot)]
+def rim_parts(value, cot):
+    return [part.astype(BF) for part in split(value, 2) + [cot]]
 
 
 def merge_kernel(parts, xd, yface, zface, out, yplane):
@@ -202,9 +201,22 @@
         yplane[i, mx + 1] = jnp.concatenate(rows, axis=0).astype(BF)
 
 
-def forward_kernel(
-    xin, act, xh, yh, zh, weight, cot, pre, stats, xface, yface, zface, wmat
-):
+def rim_kernel(pre, cot, xface, yface, zface):
+    mx, my, mz, cout = pre.shape
+    for m in range(mx):
+        planes = (pre[m], cot[m].astype(F32))
+        side = rim_parts(*[rows_at(part, 0) for part in planes])
+        line = rim_parts(*[part[0] for part in planes])
+        whole = rim_parts(*planes) if m == 0 else None
+        for i in range(3):
+            yface[i, m] = line[i]
+            zface[i, m] = side[i]
+            if m == 0:
+                xface[i, :my] = whole[i]
+                xface[i, my] = side[i]
+
+
+def forward_kernel(xin, act, xh, yh, zh, weight, pre, stats, wmat):
     mx, my, mz, cout = pre.shape
     width = xin.shape[4]
     build_matrix(weight, wmat)
@@ -223,16 +235,6 @@
         value = out[:, :cout].reshape(my, mz, cout) + prev
         on = act[m].astype(F32)
         pre[m] = jnp.where(on > 0.0, value, OFF)
-        planes = (value, on, cot[m].astype(F32))
-        side = rim_parts(*[rows_at(part, 0) for part in planes])
-        line = rim_parts(*[part[0] for part in planes])
-        whole = rim_parts(*planes) if m == 0 else None
-        for i in range(3):
-            yface[i, m] = line[i]
-            zface[i, m] = side[i]
-            if m == 0:
-                xface[i, :my] = whole[i]
-                xface[i, my] = side[i]
         total = total + jnp.sum((on * value).reshape(rows, cout), axis=0, keepdims=True)
         count = count + jnp.sum(on.reshape(rows, cout), axis=0, keepdims=True)
     mean = total / jnp.maximum(count, 1.0)
@@ -256,8 +258,7 @@
 
 
 def rounded(value):
-    high, low = split(value, 2)
-    return high + low
+    return value.astype(BF).astype(F32)
 
 
 def outer(column, rows):
@@ -266,21 +267,28 @@
     )
 
 
-def write_chunk(ref, i, body, column, common):
+def write_chunk(ref, i, body, columns, common):
     left, right = common
     line = lax.broadcasted_iota(jnp.int32, left.shape, 0)
-    for at, part in enumerate(split(column, 3)):
-        left = jnp.where(line == at, part, left)
+    for k, column in enumerate(columns):
+        for at, part in enumerate(split(column, 3)):
+            left = jnp.where(line == 3 * k + at, part, left)
     ref[i] = jnp.concatenate([body, jnp.concatenate([left, right], axis=1)], axis=0).astype(BF)
 
 
-def common_rows(first, second, alpha, beta, high):
-    zero = jnp.zeros_like(first)
-    rows = split(first, 3) + split(second, 3) + split(alpha, 3) + split(beta, 2) + split(high, 2)
+def common_rows(alphas, highs, beta, first, second):
+    zero = jnp.zeros_like(beta)
     return (
-        jnp.concatenate([zero] * 3 + rows[:5], axis=0),
-        jnp.concatenate(rows[5:], axis=0),
-    )
+        jnp.concatenate([zero] * 6 + alphas, axis=0),
+        jnp.concatenate(highs + [beta] + split(first, 3) + split(second, 2), axis=0),
+    )
+
+
+def total_of(rows, start, stop):
+    value = rows[start : start + 1]
+    for i in range(start + 1, stop):
+        value = value + rows[i : i + 1]
+    return value
 
 
 def read_chunks(ref):
@@ -288,19 +296,19 @@
     rows = depth - 8
     cout = ref.shape[2] // 2
     slopes = hats = None
-    firsts = seconds = None
-    columns, vectors, betas = ([], [], None)
+    firsts = seconds = betas = None
+    columns, vectors = ([], [])
     for j in range(devices):
         value = ref[j].astype(F32)
         left, right = (value[rows:, :cout], value[rows:, cout:])
         part = value[:rows, cout:]
-        beta = right[4:5] + right[5:6]
+        beta = right[2:3]
         term = value[:rows, :cout] + part * beta
-        first = left[3:4] + left[4:5] + left[5:6]
-        second = left[6:7] + left[7:8] + right[0:1]
-        alpha = right[1:2] + right[2:3] + right[3:4]
-        columns.append(left[0:1] + left[1:2] + left[2:3])
-        vectors.append(jnp.concatenate([alpha, right[6:7] + right[7:8]], axis=1))
+        first = total_of(right, 3, 6)
+        second = total_of(right, 6, 8)
+        for k in range(2):
+            columns.append(total_of(left, 3 * k, 3 * k + 3))
+            vectors.append(jnp.concatenate([left[6 + k : 7 + k], right[k : k + 1]], axis=1))
         if j == 0:
             slopes, hats, firsts, seconds, betas = (term, part, first, second, beta)
         else:
@@ -312,7 +320,7 @@
     slopes = slopes + both[:, :cout]
     hats = hats + both[:, cout:]
     column = jnp.sum(columns, axis=0, keepdims=True)
-    middle = jnp.sum(vectors, axis=0, keepdims=True) / devices
+    middle = jnp.sum(vectors, axis=0, keepdims=True) / (2 * devices)
     return slopes, hats, column, firsts, seconds, middle[:, :cout], betas / devices, middle[:, cout:]
 
 
@@ -325,17 +333,17 @@
 
 
 def slope_kernel(
-    pre, cot, par, xin, xh, yh, zh, xd, yd, zface, out, big, zplane, slope, acc
+    pre, cot, par, xin, xh, yh, zh, xd, yd, zface, out, keep, send, zplane, slope, acc, big
 ):
     mx, my, mz, cout = pre.shape
     width = xin.shape[4]
     half = width // 2
     rows = my * mz
     mean, rstd, gain, bias = (par[i : i + 1] for i in range(4))
-    first, second, count, high, square = (jnp.zeros((1, cout), F32) for _ in range(5))
     zplane[:, :mx] = zface[...]
     zplane[:, mx] = xd[:, my]
     zplane[:, mx + 1] = yd[:, mx + 1]
+    first, second, count, high, square = (jnp.zeros((1, cout), F32) for _ in range(5))
     for m in range(mx):
         on, hat = standardized(pre[m].reshape(rows, cout), mean, rstd)
         normed = hat * gain + bias
@@ -346,10 +354,10 @@
         first = first + jnp.sum(tilt, axis=0, keepdims=True)
         second = second + jnp.sum(tilt * hat, axis=0, keepdims=True)
         count = count + jnp.sum(on, axis=0, keepdims=True)
-        high = high + jnp.sum(on * hat, axis=0, keepdims=True)
-        square = square + jnp.sum(on * hat * hat, axis=0, keepdims=True)
+        high = high + jnp.sum(hat, axis=0, keepdims=True)
+        square = square + jnp.sum(hat * hat, axis=0, keepdims=True)
     some = jnp.maximum(count, 1.0)
-    alpha = first / some
+    alpha = rounded(first / some)
     high = rounded(high / some)
     beta = (second - high * first) / jnp.maximum(square - count * high * high, 0.01 * some)
     beta = rounded(beta)
@@ -363,13 +371,13 @@
         here, after = ([], [])
         for i, part in enumerate((rest, hat, on)):
             held = part.astype(BF)
-            keep = 8 if i == 2 else cout
+            lines = 8 if i == 2 else cout
             wide = held.astype(F32)
             rims[i].append(rows_at(wide.reshape(my, mz, cout), 0))
             nxt = pltpu.roll(wide, rows - 1, 0).reshape(my, mz, cout)
             nxt = jnp.where(last, 0.0, nxt).reshape(rows, cout)
-            here.append(wide.T[:keep])
-            after.append(nxt.T[:keep])
+            here.append(wide.T[:lines])
+            after.append(nxt.T[:lines])
         right = jnp.concatenate(here + after, axis=0).astype(BF)
         left = jnp.concatenate(
             [tile_of(xin, xh, yh, 2 * m + a, b).reshape(rows, width) for a, b in TAPS], axis=1
@@ -396,11 +404,12 @@
         acc[to + half : to + 3 * half] = own[: 2 * cout, at : at + width].T
     if acc.shape[0] > half * taps:
         acc[half * taps :] = jnp.zeros((acc.shape[0] - half * taps, 2 * cout), F32)
-    common = common_rows(first, second, alpha, beta, high)
+    zero = jnp.zeros_like(beta)
+    common = common_rows([alpha, zero], [high, zero], beta, first, second)
     lane = lax.broadcasted_iota(jnp.int32, (8, width), 1)
-    near, depth, _ = big.shape
+    _, plane, depth, _ = big.shape
     depth = depth - 8
-    for n in range(near):
+    for n in range(2 * plane):
         column = jnp.zeros((8, width), F32)
         for tap in range(taps):
             start = half * tap - depth * n
@@ -412,21 +421,47 @@
                 if shift:
                     row = pltpu.roll(row, shift, 1)
                 column = jnp.where((lane >= lo) & (lane < hi), row, column)
-        write_chunk(big, n, acc[depth * n : depth * (n + 1)], column, common)
+        write_chunk(big.at[n // plane], n % plane, acc[depth * n : depth * (n + 1)], [column], common)
+    core = lax.axis_index("c")
+    keep[...] = big[core]
+    send[...] = big[1 - core]
+
+
+def pair_kernel(mine, other, out):
+    _, depth, width = mine.shape
+    rows = depth - 8
+    cout = width // 2
+    for i in range(mine.shape[0]):
+        pair = [ref[i].astype(F32) for ref in (mine, other)]
+        left = [value[rows:, :cout] for value in pair]
+        right = [value[rows:, cout:] for value in pair]
+        beta = rounded(0.5 * (right[0][2:3] + right[1][2:3]))
+        first = total_of(right[0], 3, 6) + total_of(right[1], 3, 6)
+        second = total_of(right[0], 6, 8) + total_of(right[1], 6, 8)
+        slopes = pair[0][:rows, :cout] + pair[1][:rows, :cout]
+        hats = pair[0][:rows, cout:] + pair[1][:rows, cout:]
+        for value, vectors in zip(pair, right):
+            slopes = slopes + value[:rows, cout:] * (vectors[2:3] - beta)
+        common = common_rows(
+            [part[6:7] for part in left], [part[0:1] for part in right], beta, first, second
+        )
+        columns = [eight(total_of(part, 0, 3)) for part in left]
+        write_chunk(out, i, jnp.concatenate([slopes, hats], axis=1), columns, common)
 
 
 def near_kernel(parts, out):
     slopes, hats, column, first, second, alpha, beta, high = read_chunks(parts)
     rows = slopes.shape[0]
     cout = slopes.shape[1]
-    beta, high = (rounded(beta), rounded(high))
+    alpha, beta, high = (rounded(alpha), rounded(beta), rounded(high))
     both = outer(lone(column), lone(jnp.concatenate([alpha, high], axis=1)))[:rows]
     hats = hats - both[:, cout:]
     slopes = slopes - both[:, :cout] - hats * beta
-    common = common_rows(first, second, alpha, beta, high)
+    zero = jnp.zeros_like(beta)
+    common = common_rows([alpha, zero], [high, zero], beta, first, second)
     body = jnp.concatenate([slopes, hats], axis=1)
     for i in range(out.shape[0]):
-        write_chunk(out, i, body, eight(column), common)
+        write_chunk(out, i, body, [eight(column)], common)
 
 
 def far_kernel(parts, par, dw, shift_out, tilt_out, both):
@@ -565,18 +600,24 @@
     yh = beyond(jnp.concatenate([yface, slab(zfaces[:, 1, my - 1], mz)], axis=0), GY, 1)
     zfaces = jnp.concatenate([zfaces.reshape(2 * rows, my, width), yh[rows:]], axis=0)
     zh = beyond(zfaces, GZ, 1)
-    pre, stats, xface, yface, zface = call(
+    pre, stats = call(
         forward_kernel,
         [
             shape((mx, my, mz, cout), F32),
             shape((near, 3, cout), F32),
+        ],
+        [xin, act, xh, yh, zh, weight],
+        scratch=[pltpu.VMEM((9 * width, 2 * cout), BF)],
+        flops=1_200_000_000,
+    )
+    xface, yface, zface = call(
+        rim_kernel,
+        [
             shape((3, my + 1, mz, cout), BF),
             shape((3, mx, mz, cout), BF),
             shape((3, mx, my, cout), BF),
         ],
-        [xin, act, xh, yh, zh, weight, cotangent],
-        scratch=[pltpu.VMEM((9 * width, 2 * cout), BF)],
-        flops=1_200_000_000,
+        [pre, cotangent],
     )
     xd = moved(xface, GX, -1)
     stats, yplane = call(
@@ -592,21 +633,28 @@
     par = jnp.stack([mean, rstd, norm[0], norm[1], count])
     taps = 27 * cin
     rows = -(-taps // (8 * near)) * 8
-    section_out, big, zplane = call(
+    plane = lax.axis_size(PLANE)
+    chunks = (plane, rows + 8, 2 * cout)
+    section_out, big, send, zplane = call(
         slope_kernel,
         [
             shape((mx, my, mz, cout), BF),
-            shape((near, rows + 8, 2 * cout), BF),
+            shape(chunks, BF),
+            shape(chunks, BF),
             shape((3, mx + 2, my, cout), BF),
         ],
         [pre, cotangent, par, xin, xh, yh, zh, xd, yd, zface],
-        scratch=[pltpu.VMEM(pre.shape, F32), pltpu.VMEM((near * rows, 2 * cout), F32)],
+        scratch=[
+            pltpu.VMEM(pre.shape, F32),
+            pltpu.VMEM((near * rows, 2 * cout), F32),
+            pltpu.VMEM((2,) + chunks, BF),
+        ],
         flops=2_400_000_000,
     )
+    (big,) = call(pair_kernel, [shape(chunks, BF)], [big, moved(send, "c", 1)])
     zd = moved(zplane, GZ, -1)
     far = lax.axis_size(FAR)
-    (big,) = call(near_kernel, [shape((far, rows + 8, 2 * cout), BF)], [exchanged(big, NEAR)])
-    plane = lax.axis_size(PLANE)
+    (big,) = call(near_kernel, [shape((far, rows + 8, 2 * cout), BF)], [exchanged(big, PLANE)])
     dw, shift, tilt, grads = call(
         far_kernel,
         [

time: 113 us -> 107 us (0.947)
  blocking collectives: 38.6 us -> 29.7 us
  starting transfers between devices: 22.8 us -> 28 us
  waiting for transfers between devices: 33.8 us -> 31.9 us
    all_to_all x2, blocking collectives: 38.6 us -> 29.7 us  [exchanged(): return lax.all_to_all(value, axes, 0, 0)]
    ppermute x7 -> x8, starting transfers between devices: 12.1 us -> 17.2 us  [moved(): lax.ppermute(value, axes, [(i, (i + by) % count) for i in range(count)])]
    all_to_all x3, waiting for transfers between devices: 22.4 us -> 19 us  [exchanged(): return lax.all_to_all(value, axes, 0, 0)]
    ppermute x7 -> x8, waiting for transfers between devices: 11.4 us -> 12.9 us  [moved(): lax.ppermute(value, axes, [(i, (i + by) % count) for i in range(count)])]
    pallas_call x7 -> x9, Pallas kernels: 12.3 us -> 12.4 us  [call(): pl.pallas_call(kernel, out_shape=outs, in_specs=[pl.BlockSpec(memory_spac...]
  transfers between devices with their start and end apart: 10 -> 11, of which waited for: 7 -> 8; matrix products, arithmetic and copies ran while one was open for 0% -> 0% of each run, Pallas kernels for 5% -> 5%
where the time goes in v7:
time: 107 us
  waiting for transfers between devices  31.9 us (30%)
  blocking collectives  29.7 us (28%)
  starting transfers between devices  28 us (26%)
  Pallas kernels  14.3 us (13%)
  other arithmetic  1.26 us (1%)
    all_to_all x2, blocking collectives, exchanged(): return lax.all_to_all(value, axes, 0, 0)  29.7 us
    all_to_all x3, waiting for transfers between devices, exchanged(): return lax.all_to_all(value, axes, 0, 0)  19 us
    ppermute x8, starting transfers between devices, moved(): lax.ppermute(value, axes, [(i, (i + by) % count) for i in range(count)])  17.2 us
    ppermute x8, waiting for transfers between devices, moved(): lax.ppermute(value, axes, [(i, (i + by) % count) for i in range(count)])  12.9 us
    pallas_call x9, Pallas kernels, call(): pl.pallas_call(kernel, out_shape=outs, in_specs=[pl.BlockSpec(memory_spac...  12.4 us
    all_to_all x3, starting transfers between devices, exchanged(): return lax.all_to_all(value, axes, 0, 0)  10.8 us
  transfers between devices with their start and end apart: 11, of which 8 were waited for; matrix products, arithmetic and copies ran while one was open for 0% of the time, Pallas kernels for 5%

profile of v7, /device:TPU:1, one launch (start us, length us, event | category | flops | bytes accessed | tf_op | source)
XLA Modules:
  0.0 106.8 jit_solution(9081887885778778116)
XLA Ops:
  0.7 1.9 %shard_map.102 = bf16[2,17,16,128]{3,2,1,0:T(8,128)(2,1)} custom-call(bf16[8,32,16,128]{3,2,1,0:T(8,128)(2,1)} %feat.3, s32[8,32,32]{2,1,0:T(8,128)} %active.5), custom_call_target="tpu_custom_call" | custom-call | flops 10000000 | bytes 400000 | tf_op jit(solution)/shard_map/pallas_call | solution.py:573
  2.5 3.8 %collective-permute-start = (bf16[2,17,16,128]{3,2,1,0:T(8,128)(2,1)}, bf16[2,17,16,128]{3,2,1,0:T(8,128)(2,1)S(1)}, u32[]{:S(2)}, u32[]{:S(2)}) collective-permute-start(bf16[2,17,16,128]{3,2,1,0:T(8,128)(2,1)} %shard_map.102), channel_id=1, source_target_pairs={{0,16},{16,32},{32,48},{48,64},{64,80},{80,96},{96,112},{112,128},... | collective-permute-start | bytes 417800 | tf_op jit(solution)/shard_map/ppermute | solution.py:541
  7.0 1.8 %shard_map.101 = (bf16[8,2,16,16,128]{4,3,2,1,0:T(8,128)(2,1)S(1)}, bf16[4,16,16,128]{3,2,1,0:T(8,128)(2,1)S(1)}, bf16[8,2,16,128]{3,2,1,0:T(8,128)(2,1)S(1)}, f32[2,128]{1,0:T(2,128)S(1)}) custom-call(bf16[8,32,16,128]{3,2,1,0:T(8,128)(2,1)S(1)} %copy-done, s32[8,32,32]{2,1,0:T(8,128)S(1)} %copy-done.1, f32[1,128]{1,0:T(1,128)S(1)} %bitcast.39, ...), custom_call_target="tpu_custom_call" | custom-call | flops 100000000 | bytes 2459648 | tf_op jit(solution)/shard_map/pallas_call | solution.py:21
  8.9 6.4 %collective-permute-done.xh = bf16[2,17,16,128]{3,2,1,0:T(8,128)(2,1)S(1)} collective-permute-done((bf16[2,17,16,128]{3,2,1,0:T(8,128)(2,1)}, bf16[2,17,16,128]{3,2,1,0:T(8,128)(2,1)S(1)}, u32[]{:S(2)}, u32[]{:S(2)}) %collective-permute-start) | collective-permute-done | bytes 139296 | tf_op jit(solution)/shard_map/ppermute | solution.py:541
  15.4 2.3 %collective-permute-start.1 = (bf16[10,16,128]{2,1,0:T(8,128)(2,1)S(1)}, bf16[10,16,128]{2,1,0:T(8,128)(2,1)S(1)}, u32[]{:S(2)}, u32[]{:S(2)}) collective-permute-start(bf16[10,16,128]{2,1,0:T(8,128)(2,1)S(1)} %maximum_multiply_fusion.1), channel_id=1, source_target_pairs={{0,2},{2,4},{4,6},{6,8},{8,10},{10,12},{12,14},{14,0},{1,3},{3,5},... | collective-permute-start | bytes 122888 | tf_op jit(solution)/shard_map/ppermute | solution.py:541
  19.3 2.9 %collective-permute-done.2.zh = bf16[19,16,128]{2,1,0:T(8,128)(2,1)S(1)} collective-permute-done((bf16[19,16,128]{2,1,0:T(8,128)(2,1)S(1)}, bf16[19,16,128]{2,1,0:T(8,128)(2,1)S(1)}, u32[]{:S(2)}, u32[]{:S(2)}) %collective-permute-start.2) | collective-permute-done | bytes 77856 | tf_op jit(solution)/shard_map/ppermute | solution.py:541
  22.1 1.3 %shard_map.103 = (f32[4,16,16,128]{3,2,1,0:T(8,128)S(1)}, f32[32,3,128]{2,1,0:T(4,128)S(1)}) custom-call(bf16[8,2,16,16,128]{4,3,2,1,0:T(8,128)(2,1)S(1)} %get-tuple-element.26.xin, bf16[4,16,16,128]{3,2,1,0:T(8,128)(2,1)S(1)} %get-tuple-element.27.act, bf16[2,17,16,128]{3,2,1,0:T(8,128)(2,1)S(1)} %collective-permute-done.xh, ...), custom_call_target="tpu_custom_call" | custom-call | flops 1200000000 | bytes 2584576 | tf_op jit(solution)/shard_map/pallas_call | solution.py:21
  23.5 3.0 %collective-permute-start.3 = (bf16[3,17,16,128]{3,2,1,0:T(8,128)(2,1)S(1)}, bf16[3,17,16,128]{3,2,1,0:T(8,128)(2,1)S(1)}, u32[]{:S(2)}, u32[]{:S(2)}) collective-permute-start(bf16[3,17,16,128]{3,2,1,0:T(8,128)(2,1)S(1)} %get-tuple-element.31), channel_id=1, source_target_pairs={{0,240},{16,0},{32,16},{48,32},{64,48},{80,64},{96,80},{112,96},{1... | collective-permute-start | bytes 626696 | tf_op jit(solution)/shard_map/ppermute | solution.py:541
  26.6 16.1 %all_to_all.25.parts = f32[32,3,128]{2,1,0:T(4,128)S(1)} all-to-all(f32[32,3,128]{2,1,0:T(4,128)S(1)} %get-tuple-element.30), channel_id=1, replica_groups=mesh['z'=8,'yh'=2,'x'=4,'c'=2,'yl'=2] {'c','yh','x','yl'}, dimensions={0} | all-to-all | bytes 98304 | tf_op jit(solution)/shard_map/all_to_all | solution.py:555
  43.3 3.5 %all-to-all-start.1 = ((f32[8,3,128]{2,1,0:T(4,128)}), f32[8,3,128]{2,1,0:T(4,128)S(1)}, u32[]{:S(2)}, u32[]{:S(2)}) async-start(f32[8,3,128]{2,1,0:T(4,128)} %get-tuple-element.34), calls=%async_computation.1 | async-start | bytes 32768 | tf_op jit(solution)/shard_map/all_to_all | solution.py:555
  47.6 5.9 %all-to-all-done.1 = f32[8,3,128]{2,1,0:T(4,128)S(1)} async-done(((f32[8,3,128]{2,1,0:T(4,128)}), f32[8,3,128]{2,1,0:T(4,128)S(1)}, u32[]{:S(2)}, u32[]{:S(2)}) %all-to-all-start.1) | async-done | bytes 12320 | tf_op jit(solution)/shard_map/all_to_all | solution.py:555
  53.6 3.1 %shard_map.106 = (bf16[4,16,16,128]{3,2,1,0:T(8,128)(2,1)}, bf16[16,64,256]{2,1,0:T(8,128)(2,1)S(1)}, bf16[16,64,256]{2,1,0:T(8,128)(2,1)S(1)}, bf16[3,6,16,128]{3,2,1,0:T(8,128)(2,1)S(1)}) custom-call(f32[4,16,16,128]{3,2,1,0:T(8,128)S(1)} %get-tuple-element.29.pre, bf16[4,16,16,128]{3,2,1,0:T(8,128)(2,1)S(1)} %copy-done.2, ...), custom_call_target="tpu_custom_call" | custom-call | flops 2400000000 | bytes 3811840 | tf_op jit(solution)/shard_map/pallas_call | solution.py:21
  56.7 1.9 %collective-permute-start.5 = (bf16[16,64,256]{2,1,0:T(8,128)(2,1)S(1)}, bf16[16,64,256]{2,1,0:T(8,128)(2,1)S(1)}, u32[]{:S(2)}, u32[]{:S(2)}) collective-permute-start(bf16[16,64,256]{2,1,0:T(8,128)(2,1)S(1)} %get-tuple-element.39), channel_id=1, source_target_pairs={{0,2},{2,0},{1,3},{3,1},{4,6},{6,4},{5,7},{7,5},{8,10},{10,8},{9,1... | collective-permute-start | bytes 1572872 | tf_op jit(solution)/shard_map/ppermute | solution.py:541
  58.6 1.5 %collective-permute-done.5.other = bf16[16,64,256]{2,1,0:T(8,128)(2,1)S(1)} collective-permute-done((bf16[16,64,256]{2,1,0:T(8,128)(2,1)S(1)}, bf16[16,64,256]{2,1,0:T(8,128)(2,1)S(1)}, u32[]{:S(2)}, u32[]{:S(2)}) %collective-permute-start.5) | collective-permute-done | bytes 524320 | tf_op jit(solution)/shard_map/ppermute | solution.py:541
  60.5 13.6 %all_to_all.26.parts = bf16[16,64,256]{2,1,0:T(8,128)(2,1)S(1)} all-to-all(bf16[16,64,256]{2,1,0:T(8,128)(2,1)S(1)} %shard_map.107), channel_id=1, replica_groups=mesh['z'=8,'yh'=2,'x'=4,'c'=2,'yl'=2] {'yh','x','yl'}, dimensions={0} | all-to-all | bytes 1048576 | tf_op jit(solution)/shard_map/all_to_all | solution.py:555
  74.1 1.1 %shard_map.108 = bf16[8,64,256]{2,1,0:T(8,128)(2,1)} custom-call(bf16[16,64,256]{2,1,0:T(8,128)(2,1)S(1)} %all_to_all.26.parts), custom_call_target="tpu_custom_call" | custom-call | flops 100000000 | bytes 786432 | tf_op jit(solution)/shard_map/pallas_call | solution.py:21
  75.2 3.5 %all-to-all-start.3 = ((bf16[8,64,256]{2,1,0:T(8,128)(2,1)}), bf16[8,64,256]{2,1,0:T(8,128)(2,1)S(1)}, u32[]{:S(2)}, u32[]{:S(2)}) async-start(bf16[8,64,256]{2,1,0:T(8,128)(2,1)} %shard_map.108), calls=%async_computation.3 | async-start | bytes 524288 | tf_op jit(solution)/shard_map/all_to_all | solution.py:555
  79.0 9.0 %all-to-all-done.3.parts = bf16[8,64,256]{2,1,0:T(8,128)(2,1)S(1)} async-done(((bf16[8,64,256]{2,1,0:T(8,128)(2,1)}), bf16[8,64,256]{2,1,0:T(8,128)(2,1)S(1)}, u32[]{:S(2)}, u32[]{:S(2)}) %all-to-all-start.3) | async-done | bytes 262176 | tf_op jit(solution)/shard_map/all_to_all | solution.py:555
  88.0 1.1 %shard_map.109 = (bf16[16,56,128]{2,1,0:T(8,128)(2,1)}, f32[1,128]{1,0:T(1,128)}, f32[1,128]{1,0:T(1,128)}, f32[2,128]{1,0:T(2,128)S(1)}) custom-call(bf16[8,64,256]{2,1,0:T(8,128)(2,1)S(1)} %all-to-all-done.3.parts, f32[5,128]{1,0:T(8,128)S(1)} %pad_maximum_fusion.2.par), custom_call_target="tpu_custom_call" | custom-call | flops 100000000 | bytes 496128 | tf_op jit(solution)/shard_map/pallas_call | solution.py:21
  89.1 3.7 %all-to-all-start.4 = ((bf16[16,56,128]{2,1,0:T(8,128)(2,1)}), bf16[16,56,128]{2,1,0:T(8,128)(2,1)S(1)}, u32[]{:S(2)}, u32[]{:S(2)}) async-start(bf16[16,56,128]{2,1,0:T(8,128)(2,1)} %get-tuple-element.40), calls=%async_computation.4 | async-start | bytes 458752 | tf_op jit(solution)/shard_map/all_to_all | solution.py:555
  92.9 3.0 %shard_map.110 = bf16[8,16,2,16,128]{4,3,2,1,0:T(8,128)(2,1)} custom-call(f32[4,16,16,128]{3,2,1,0:T(8,128)S(1)} %get-tuple-element.29.pre, bf16[4,16,16,128]{3,2,1,0:T(8,128)(2,1)S(1)} %copy-done.2, f32[5,128]{1,0:T(8,128)S(1)} %pad_maximum_fusion.2.par, f32[2,128]{1,0:T(2,128)S(1)} %get-tuple-element.41.grads, ...), custom_call_target="tpu_custom_call" | custom-call | flops 2400000000 | bytes 2670080 | tf_op jit(solution)/shard_map/pallas_call | solution.py:21
  95.8 4.2 %all-to-all-done.4 = bf16[16,56,128]{2,1,0:T(8,128)(2,1)S(1)} async-done(((bf16[16,56,128]{2,1,0:T(8,128)(2,1)}), bf16[16,56,128]{2,1,0:T(8,128)(2,1)S(1)}, u32[]{:S(2)}, u32[]{:S(2)}) %all-to-all-start.4) | async-done | bytes 229408 | tf_op jit(solution)/shard_map/all_to_all | solution.py:555
  100.0 4.5 %collective-permute-start.7 = (bf16[16,56,128]{2,1,0:T(8,128)(2,1)S(1)}, bf16[16,56,128]{2,1,0:T(8,128)(2,1)S(1)}, u32[]{:S(2)}, u32[]{:S(2)}) collective-permute-start(bf16[16,56,128]{2,1,0:T(8,128)(2,1)S(1)} %all-to-all-done.4), channel_id=1, source_target_pairs={{0,2},{2,0},{1,3},{3,1},{4,6},{6,4},{5,7},{7,5},{8,10},{10,8},{9,1... | collective-permute-start | bytes 688136 | tf_op jit(solution)/shard_map/ppermute | solution.py:541
  104.5 1.1 %collective-permute-done.7 = bf16[16,56,128]{2,1,0:T(8,128)(2,1)S(1)} collective-permute-done((bf16[16,56,128]{2,1,0:T(8,128)(2,1)S(1)}, bf16[16,56,128]{2,1,0:T(8,128)(2,1)S(1)}, u32[]{:S(2)}, u32[]{:S(2)}) %collective-permute-start.7) | collective-permute-done | bytes 229408 | tf_op jit(solution)/shard_map/ppermute | solution.py:541
  (45 shorter events, 5.7 us)
Async XLA Ops:
  0.6 5.7 %copy-start.1 = (s32[8,32,32]{2,1,0:T(8,128)S(1)}, s32[8,32,32]{2,1,0:T(8,128)}, u32[]{:S(2)}) copy-start(s32[8,32,32]{2,1,0:T(8,128)} %active.5) | copy-start | bytes 98308
  0.6 5.7 %copy-start = (bf16[8,32,16,128]{3,2,1,0:T(8,128)(2,1)S(1)}, bf16[8,32,16,128]{3,2,1,0:T(8,128)(2,1)}, u32[]{:S(2)}) copy-start(bf16[8,32,16,128]{3,2,1,0:T(8,128)(2,1)} %feat.3) | copy-start | bytes 3145732
  2.5 12.7 %collective-permute-start = (bf16[2,17,16,128]{3,2,1,0:T(8,128)(2,1)}, bf16[2,17,16,128]{3,2,1,0:T(8,128)(2,1)S(1)}, u32[]{:S(2)}, u32[]{:S(2)}) collective-permute-start(bf16[2,17,16,128]{3,2,1,0:T(8,128)(2,1)} %shard_map.102), channel_id=1, source_target_pairs={{0,16},{16,32},{32,48},{48,64},{64,80},{80,96},{96,112},{112,128},... | collective-permute-start | bytes 417800 | tf_op jit(solution)/shard_map/ppermute | solution.py:541
  6.4 0.7 copy-start.3
  6.4 0.7 copy-start.4
  8.8 13.3 %copy-start.5 = (bf16[3,3,3,64,128]{4,3,2,1,0:T(8,128)(2,1)S(1)}, bf16[3,3,3,64,128]{4,3,2,1,0:T(8,128)(2,1)}, u32[]{:S(2)}) copy-start(bf16[3,3,3,64,128]{4,3,2,1,0:T(8,128)(2,1)} %weight.3) | copy-start | bytes 1327108
  15.4 3.4 %collective-permute-start.1 = (bf16[10,16,128]{2,1,0:T(8,128)(2,1)S(1)}, bf16[10,16,128]{2,1,0:T(8,128)(2,1)S(1)}, u32[]{:S(2)}, u32[]{:S(2)}) collective-permute-start(bf16[10,16,128]{2,1,0:T(8,128)(2,1)S(1)} %maximum_multiply_fusion.1), channel_id=1, source_target_pairs={{0,2},{2,4},{4,6},{6,8},{8,10},{10,12},{12,14},{14,0},{1,3},{3,5},... | collective-permute-start | bytes 122888 | tf_op jit(solution)/shard_map/ppermute | solution.py:541
  18.8 3.3 %collective-permute-start.2 = (bf16[19,16,128]{2,1,0:T(8,128)(2,1)S(1)}, bf16[19,16,128]{2,1,0:T(8,128)(2,1)S(1)}, u32[]{:S(2)}, u32[]{:S(2)}) collective-permute-start(bf16[19,16,128]{2,1,0:T(8,128)(2,1)S(1)} %maximum_multiply_fusion), channel_id=1, source_target_pairs={{0,1},{1,0},{2,3},{3,2},{4,5},{5,4},{6,7},{7,6},{8,9},{9,8},{10,11... | collective-permute-start | bytes 233480 | tf_op jit(solution)/shard_map/ppermute | solution.py:541
  22.1 1.3 %copy-start.2 = (bf16[4,16,16,128]{3,2,1,0:T(8,128)(2,1)S(1)}, bf16[4,16,16,128]{3,2,1,0:T(8,128)(2,1)}, u32[]{:S(2)}) copy-start(bf16[4,16,16,128]{3,2,1,0:T(8,128)(2,1)} %cot.5) | copy-start | bytes 786436
  23.5 19.1 %collective-permute-start.3 = (bf16[3,17,16,128]{3,2,1,0:T(8,128)(2,1)S(1)}, bf16[3,17,16,128]{3,2,1,0:T(8,128)(2,1)S(1)}, u32[]{:S(2)}, u32[]{:S(2)}) collective-permute-start(bf16[3,17,16,128]{3,2,1,0:T(8,128)(2,1)S(1)} %get-tuple-element.31), channel_id=1, source_target_pairs={{0,240},{16,0},{32,16},{48,32},{64,48},{80,64},{96,80},{112,96},{1... | collective-permute-start | bytes 626696 | tf_op jit(solution)/shard_map/ppermute | solution.py:541
  43.3 10.2 %all-to-all-start.1 = ((f32[8,3,128]{2,1,0:T(4,128)}), f32[8,3,128]{2,1,0:T(4,128)S(1)}, u32[]{:S(2)}, u32[]{:S(2)}) async-start(f32[8,3,128]{2,1,0:T(4,128)} %get-tuple-element.34), calls=%async_computation.1 | async-start | bytes 32768 | tf_op jit(solution)/shard_map/all_to_all | solution.py:555
  46.9 6.7 %collective-permute-start.4 = (bf16[3,6,16,128]{3,2,1,0:T(8,128)(2,1)S(1)}, bf16[3,6,16,128]{3,2,1,0:T(8,128)(2,1)S(1)}, u32[]{:S(2)}, u32[]{:S(2)}) collective-permute-start(bf16[3,6,16,128]{3,2,1,0:T(8,128)(2,1)S(1)} %get-tuple-element.36), channel_id=1, source_target_pairs={{0,14},{2,0},{4,2},{6,4},{8,6},{10,8},{12,10},{14,12},{1,15},{3,1}... | collective-permute-start | bytes 221192 | tf_op jit(solution)/shard_map/ppermute | solution.py:541
  56.7 3.5 %collective-permute-start.5 = (bf16[16,64,256]{2,1,0:T(8,128)(2,1)S(1)}, bf16[16,64,256]{2,1,0:T(8,128)(2,1)S(1)}, u32[]{:S(2)}, u32[]{:S(2)}) collective-permute-start(bf16[16,64,256]{2,1,0:T(8,128)(2,1)S(1)} %get-tuple-element.39), channel_id=1, source_target_pairs={{0,2},{2,0},{1,3},{3,1},{4,6},{6,4},{5,7},{7,5},{8,10},{10,8},{9,1... | collective-permute-start | bytes 1572872 | tf_op jit(solution)/shard_map/ppermute | solution.py:541
  75.2 12.8 %all-to-all-start.3 = ((bf16[8,64,256]{2,1,0:T(8,128)(2,1)}), bf16[8,64,256]{2,1,0:T(8,128)(2,1)S(1)}, u32[]{:S(2)}, u32[]{:S(2)}) async-start(bf16[8,64,256]{2,1,0:T(8,128)(2,1)} %shard_map.108), calls=%async_computation.3 | async-start | bytes 524288 | tf_op jit(solution)/shard_map/all_to_all | solution.py:555
  78.7 14.1 %collective-permute-start.6 = (bf16[3,6,16,128]{3,2,1,0:T(8,128)(2,1)S(1)}, bf16[3,6,16,128]{3,2,1,0:T(8,128)(2,1)S(1)}, u32[]{:S(2)}, u32[]{:S(2)}) collective-permute-start(bf16[3,6,16,128]{3,2,1,0:T(8,128)(2,1)S(1)} %get-tuple-element.42), channel_id=1, source_target_pairs={{0,1},{1,0},{2,3},{3,2},{4,5},{5,4},{6,7},{7,6},{8,9},{9,8},{10,11... | collective-permute-start | bytes 221192 | tf_op jit(solution)/shard_map/ppermute | solution.py:541
  89.1 10.9 %all-to-all-start.4 = ((bf16[16,56,128]{2,1,0:T(8,128)(2,1)}), bf16[16,56,128]{2,1,0:T(8,128)(2,1)S(1)}, u32[]{:S(2)}, u32[]{:S(2)}) async-start(bf16[16,56,128]{2,1,0:T(8,128)(2,1)} %get-tuple-element.40), calls=%async_computation.4 | async-start | bytes 458752 | tf_op jit(solution)/shard_map/all_to_all | solution.py:555
  100.0 5.6 %collective-permute-start.7 = (bf16[16,56,128]{2,1,0:T(8,128)(2,1)S(1)}, bf16[16,56,128]{2,1,0:T(8,128)(2,1)S(1)}, u32[]{:S(2)}, u32[]{:S(2)}) collective-permute-start(bf16[16,56,128]{2,1,0:T(8,128)(2,1)S(1)} %all-to-all-done.4), channel_id=1, source_target_pairs={{0,2},{2,0},{1,3},{3,1},{4,6},{6,4},{5,7},{7,5},{8,10},{10,8},{9,1... | collective-permute-start | bytes 688136 | tf_op jit(solution)/shard_map/ppermute | solution.py:541

commit v8 on v7

--- a/solution.py
+++ b/solution.py
@@ -177,9 +177,7 @@
     return [part.astype(BF) for part in split(value, 2) + [cot]]
 
 
-def merge_kernel(parts, xd, yface, zface, out, yplane):
-    mx = yface.shape[1]
-    my = zface.shape[2]
+def merge_kernel(parts, out):
     counts, sums, squares = (
         jnp.concatenate([parts[j, i : i + 1] for j in range(parts.shape[0])], axis=0) for i in range(3)
     )
@@ -188,10 +186,14 @@
     mean = total / jnp.maximum(count, 1.0)
     apart = sums / jnp.maximum(counts, 1.0) - mean
     square = jnp.sum(squares + counts * apart * apart, axis=0, keepdims=True)
+    out[...] = jnp.concatenate([count, total, square] + [jnp.zeros_like(count)] * 5, axis=0)
+
+
+def pack_kernel(stats, xd, yface, zface, out, yplane):
+    mx = yface.shape[1]
+    my = zface.shape[2]
     for i in range(out.shape[0]):
-        out[i, 0:1] = count
-        out[i, 1:2] = total
-        out[i, 2:3] = square
+        out[i] = stats[:3]
     depth = yplane.shape[2]
     yplane[:, :mx] = yface[...]
     yplane[:, mx] = xd[:, 0]
@@ -333,16 +335,13 @@
 
 
 def slope_kernel(
-    pre, cot, par, xin, xh, yh, zh, xd, yd, zface, out, keep, send, zplane, slope, acc, big
+    pre, cot, par, xin, xh, yh, zh, _, out, keep, send, slope, acc, big
 ):
     mx, my, mz, cout = pre.shape
     width = xin.shape[4]
     half = width // 2
     rows = my * mz
     mean, rstd, gain, bias = (par[i : i + 1] for i in range(4))
-    zplane[:, :mx] = zface[...]
-    zplane[:, mx] = xd[:, my]
-    zplane[:, mx + 1] = yd[:, mx + 1]
     first, second, count, high, square = (jnp.zeros((1, cout), F32) for _ in range(5))
     for m in range(mx):
         on, hat = standardized(pre[m].reshape(rows, cout), mean, rstd)
@@ -460,11 +459,17 @@
     zero = jnp.zeros_like(beta)
     common = common_rows([alpha, zero], [high, zero], beta, first, second)
     body = jnp.concatenate([slopes, hats], axis=1)
-    for i in range(out.shape[0]):
-        write_chunk(out, i, body, [eight(column)], common)
-
-
-def far_kernel(parts, par, dw, shift_out, tilt_out, both):
+    write_chunk(out, 0, body, [eight(column)], common)
+    message = out[0]
+    for i in range(1, out.shape[0]):
+        out[i] = message
+
+
+def far_kernel(parts, par, xd, yd, zface, dw, shift_out, tilt_out, both, zplane):
+    mx, my = zface.shape[1:3]
+    zplane[:, :mx] = zface[...]
+    zplane[:, mx] = xd[:, my]
+    zplane[:, mx + 1] = yd[:, mx + 1]
     _, rstd, gain, _, count = (par[i : i + 1] for i in range(5))
     slopes, hats, column, first, second, _, _, _ = read_chunks(parts)
     shift, tilt = (first / count, second / count)
@@ -620,10 +625,11 @@
         [pre, cotangent],
     )
     xd = moved(xface, GX, -1)
+    (stats,) = call(merge_kernel, [shape((8, cout), F32)], [exchanged(stats, NEAR)])
     stats, yplane = call(
-        merge_kernel,
+        pack_kernel,
         [shape((lax.axis_size(FAR), 3, cout), F32), shape((3, mx + 2, mz, cout), BF)],
-        [exchanged(stats, NEAR), xd, yface, zface],
+        [stats, xd, yface, zface],
     )
     yd = moved(yplane, GY, -1)
     stats = merged(exchanged(stats, FAR))
@@ -635,15 +641,14 @@
     rows = -(-taps // (8 * near)) * 8
     plane = lax.axis_size(PLANE)
     chunks = (plane, rows + 8, 2 * cout)
-    section_out, big, send, zplane = call(
+    section_out, big, send = call(
         slope_kernel,
         [
             shape((mx, my, mz, cout), BF),
             shape(chunks, BF),
             shape(chunks, BF),
-            shape((3, mx + 2, my, cout), BF),
-        ],
-        [pre, cotangent, par, xin, xh, yh, zh, xd, yd, zface],
+        ],
+        [pre, cotangent, par, xin, xh, yh, zh, yd],
         scratch=[
             pltpu.VMEM(pre.shape, F32),
             pltpu.VMEM((near * rows, 2 * cout), F32),
@@ -652,19 +657,20 @@
         flops=2_400_000_000,
     )
     (big,) = call(pair_kernel, [shape(chunks, BF)], [big, moved(send, "c", 1)])
-    zd = moved(zplane, GZ, -1)
     far = lax.axis_size(FAR)
     (big,) = call(near_kernel, [shape((far, rows + 8, 2 * cout), BF)], [exchanged(big, PLANE)])
-    dw, shift, tilt, grads = call(
+    dw, shift, tilt, grads, zplane = call(
         far_kernel,
         [
             shape((plane, rows, cout), BF),
             shape((1, cout), F32),
             shape((1, cout), F32),
             shape((2, cout), F32),
-        ],
-        [exchanged(big, FAR), par],
-    )
+            shape((3, mx + 2, my, cout), BF),
+        ],
+        [exchanged(big, FAR), par, xd, yd, zface],
+    )
+    zd = moved(zplane, GZ, -1)
     shift_gradient, gain_gradient = (shift.reshape(cout), tilt.reshape(cout))
     (grad_features,) = call(
         input_kernel,

time: 107 us -> 107 us (level)
  blocking collectives: 29.7 us -> 42.3 us
  waiting for transfers between devices: 31.9 us -> 23 us
  starting transfers between devices: 28 us -> 25.2 us
    all_to_all x2 -> x3, blocking collectives: 29.7 us -> 42.3 us  [exchanged(): return lax.all_to_all(value, axes, 0, 0)]
    all_to_all x3 -> x2, waiting for transfers between devices: 19 us -> 10.1 us  [exchanged(): return lax.all_to_all(value, axes, 0, 0)]
    all_to_all x3 -> x2, starting transfers between devices: 10.8 us -> 7.87 us  [exchanged(): return lax.all_to_all(value, axes, 0, 0)]
    pallas_call x9 -> x10, Pallas kernels: 12.4 us -> 11.7 us  [call(): pl.pallas_call(kernel, out_shape=outs, in_specs=[pl.BlockSpec(memory_spac...]
  transfers between devices with their start and end apart: 11 -> 10, of which waited for: 8 -> 7; matrix products, arithmetic and copies ran while one was open for 0% -> 0% of each run, Pallas kernels for 5% -> 4%
where the time goes in v8:
time: 107 us
  blocking collectives  42.3 us (40%)
  starting transfers between devices  25.2 us (24%)
  waiting for transfers between devices  23 us (21%)
  Pallas kernels  13.6 us (13%)
  other arithmetic  1.26 us (1%)
    all_to_all x3, blocking collectives, exchanged(): return lax.all_to_all(value, axes, 0, 0)  42.3 us
    ppermute x8, starting transfers between devices, moved(): lax.ppermute(value, axes, [(i, (i + by) % count) for i in range(count)])  17.3 us
    ppermute x8, waiting for transfers between devices, moved(): lax.ppermute(value, axes, [(i, (i + by) % count) for i in range(count)])  12.9 us
    pallas_call x10, Pallas kernels, call(): pl.pallas_call(kernel, out_shape=outs, in_specs=[pl.BlockSpec(memory_spac...  11.7 us
    all_to_all x2, waiting for transfers between devices, exchanged(): return lax.all_to_all(value, axes, 0, 0)  10.1 us
    all_to_all x2, starting transfers between devices, exchanged(): return lax.all_to_all(value, axes, 0, 0)  7.87 us
  transfers between devices with their start and end apart: 10, of which 7 were waited for; matrix products, arithmetic and copies ran while one was open for 0% of the time, Pallas kernels for 4%

profile of v8, /device:TPU:1, one launch (start us, length us, event | category | flops | bytes accessed | tf_op | source)
XLA Modules:
  0.0 107.0 jit_solution(15414947398515642817)
XLA Ops:
  0.7 1.9 %shard_map.102 = bf16[2,17,16,128]{3,2,1,0:T(8,128)(2,1)} custom-call(bf16[8,32,16,128]{3,2,1,0:T(8,128)(2,1)} %feat.3, s32[8,32,32]{2,1,0:T(8,128)} %active.5), custom_call_target="tpu_custom_call" | custom-call | flops 10000000 | bytes 400000 | tf_op jit(solution)/shard_map/pallas_call | solution.py:578
  2.5 3.8 %collective-permute-start = (bf16[2,17,16,128]{3,2,1,0:T(8,128)(2,1)}, bf16[2,17,16,128]{3,2,1,0:T(8,128)(2,1)S(1)}, u32[]{:S(2)}, u32[]{:S(2)}) collective-permute-start(bf16[2,17,16,128]{3,2,1,0:T(8,128)(2,1)} %shard_map.102), channel_id=1, source_target_pairs={{0,16},{16,32},{32,48},{48,64},{64,80},{80,96},{96,112},{112,128},... | collective-permute-start | bytes 417800 | tf_op jit(solution)/shard_map/ppermute | solution.py:546
  7.0 1.8 %shard_map.101 = (bf16[8,2,16,16,128]{4,3,2,1,0:T(8,128)(2,1)S(1)}, bf16[4,16,16,128]{3,2,1,0:T(8,128)(2,1)S(1)}, bf16[8,2,16,128]{3,2,1,0:T(8,128)(2,1)S(1)}, f32[2,128]{1,0:T(2,128)S(1)}) custom-call(bf16[8,32,16,128]{3,2,1,0:T(8,128)(2,1)S(1)} %copy-done, s32[8,32,32]{2,1,0:T(8,128)S(1)} %copy-done.1, f32[1,128]{1,0:T(1,128)S(1)} %bitcast.39, ...), custom_call_target="tpu_custom_call" | custom-call | flops 100000000 | bytes 2459648 | tf_op jit(solution)/shard_map/pallas_call | solution.py:21
  8.9 6.4 %collective-permute-done.xh = bf16[2,17,16,128]{3,2,1,0:T(8,128)(2,1)S(1)} collective-permute-done((bf16[2,17,16,128]{3,2,1,0:T(8,128)(2,1)}, bf16[2,17,16,128]{3,2,1,0:T(8,128)(2,1)S(1)}, u32[]{:S(2)}, u32[]{:S(2)}) %collective-permute-start) | collective-permute-done | bytes 139296 | tf_op jit(solution)/shard_map/ppermute | solution.py:546
  15.4 2.3 %collective-permute-start.1 = (bf16[10,16,128]{2,1,0:T(8,128)(2,1)S(1)}, bf16[10,16,128]{2,1,0:T(8,128)(2,1)S(1)}, u32[]{:S(2)}, u32[]{:S(2)}) collective-permute-start(bf16[10,16,128]{2,1,0:T(8,128)(2,1)S(1)} %maximum_multiply_fusion.1), channel_id=1, source_target_pairs={{0,2},{2,4},{4,6},{6,8},{8,10},{10,12},{12,14},{14,0},{1,3},{3,5},... | collective-permute-start | bytes 122888 | tf_op jit(solution)/shard_map/ppermute | solution.py:546
  17.8 1.0 collective-permute-done.1.yh
  19.3 2.9 %collective-permute-done.2.zh = bf16[19,16,128]{2,1,0:T(8,128)(2,1)S(1)} collective-permute-done((bf16[19,16,128]{2,1,0:T(8,128)(2,1)S(1)}, bf16[19,16,128]{2,1,0:T(8,128)(2,1)S(1)}, u32[]{:S(2)}, u32[]{:S(2)}) %collective-permute-start.2) | collective-permute-done | bytes 77856 | tf_op jit(solution)/shard_map/ppermute | solution.py:546
  22.1 1.3 %shard_map.103 = (f32[4,16,16,128]{3,2,1,0:T(8,128)S(1)}, f32[32,3,128]{2,1,0:T(4,128)S(1)}) custom-call(bf16[8,2,16,16,128]{4,3,2,1,0:T(8,128)(2,1)S(1)} %get-tuple-element.26.xin, bf16[4,16,16,128]{3,2,1,0:T(8,128)(2,1)S(1)} %get-tuple-element.27.act, bf16[2,17,16,128]{3,2,1,0:T(8,128)(2,1)S(1)} %collective-permute-done.xh, ...), custom_call_target="tpu_custom_call" | custom-call | flops 1200000000 | bytes 2584576 | tf_op jit(solution)/shard_map/pallas_call | solution.py:21
  23.5 3.0 %collective-permute-start.3 = (bf16[3,17,16,128]{3,2,1,0:T(8,128)(2,1)S(1)}, bf16[3,17,16,128]{3,2,1,0:T(8,128)(2,1)S(1)}, u32[]{:S(2)}, u32[]{:S(2)}) collective-permute-start(bf16[3,17,16,128]{3,2,1,0:T(8,128)(2,1)S(1)} %get-tuple-element.31), channel_id=1, source_target_pairs={{0,240},{16,0},{32,16},{48,32},{64,48},{80,64},{96,80},{112,96},{1... | collective-permute-start | bytes 626696 | tf_op jit(solution)/shard_map/ppermute | solution.py:546
  26.6 16.1 %all_to_all.25.parts = f32[32,3,128]{2,1,0:T(4,128)S(1)} all-to-all(f32[32,3,128]{2,1,0:T(4,128)S(1)} %get-tuple-element.30), channel_id=1, replica_groups=mesh['z'=8,'yh'=2,'x'=4,'c'=2,'yl'=2] {'c','yh','x','yl'}, dimensions={0} | all-to-all | bytes 98304 | tf_op jit(solution)/shard_map/all_to_all | solution.py:560
  43.3 3.5 %all-to-all-start.1 = ((f32[8,3,128]{2,1,0:T(4,128)}), f32[8,3,128]{2,1,0:T(4,128)S(1)}, u32[]{:S(2)}, u32[]{:S(2)}) async-start(f32[8,3,128]{2,1,0:T(4,128)} %get-tuple-element.34), calls=%async_computation.1 | async-start | bytes 32768 | tf_op jit(solution)/shard_map/all_to_all | solution.py:560
  47.6 5.9 %all-to-all-done.1 = f32[8,3,128]{2,1,0:T(4,128)S(1)} async-done(((f32[8,3,128]{2,1,0:T(4,128)}), f32[8,3,128]{2,1,0:T(4,128)S(1)}, u32[]{:S(2)}, u32[]{:S(2)}) %all-to-all-start.1) | async-done | bytes 12320 | tf_op jit(solution)/shard_map/all_to_all | solution.py:560
  53.6 3.1 %shard_map.107 = (bf16[4,16,16,128]{3,2,1,0:T(8,128)(2,1)}, bf16[16,64,256]{2,1,0:T(8,128)(2,1)S(1)}, bf16[16,64,256]{2,1,0:T(8,128)(2,1)S(1)}) custom-call(f32[4,16,16,128]{3,2,1,0:T(8,128)S(1)} %get-tuple-element.29.pre, bf16[4,16,16,128]{3,2,1,0:T(8,128)(2,1)S(1)} %copy-done.2, f32[5,128]{1,0:T(8,128)S(1)} %pad_maximum_fusion.2.par, ...), custom_call_target="tpu_custom_call" | custom-call | flops 2400000000 | bytes 3480064 | tf_op jit(solution)/shard_map/pallas_call | solution.py:21
  56.7 1.9 %collective-permute-start.5 = (bf16[16,64,256]{2,1,0:T(8,128)(2,1)S(1)}, bf16[16,64,256]{2,1,0:T(8,128)(2,1)S(1)}, u32[]{:S(2)}, u32[]{:S(2)}) collective-permute-start(bf16[16,64,256]{2,1,0:T(8,128)(2,1)S(1)} %get-tuple-element.39), channel_id=1, source_target_pairs={{0,2},{2,0},{1,3},{3,1},{4,6},{6,4},{5,7},{7,5},{8,10},{10,8},{9,1... | collective-permute-start | bytes 1572872 | tf_op jit(solution)/shard_map/ppermute | solution.py:546
  58.6 1.5 %collective-permute-done.5.other = bf16[16,64,256]{2,1,0:T(8,128)(2,1)S(1)} collective-permute-done((bf16[16,64,256]{2,1,0:T(8,128)(2,1)S(1)}, bf16[16,64,256]{2,1,0:T(8,128)(2,1)S(1)}, u32[]{:S(2)}, u32[]{:S(2)}) %collective-permute-start.5) | collective-permute-done | bytes 524320 | tf_op jit(solution)/shard_map/ppermute | solution.py:546
  60.5 13.6 %all_to_all.26.parts = bf16[16,64,256]{2,1,0:T(8,128)(2,1)S(1)} all-to-all(bf16[16,64,256]{2,1,0:T(8,128)(2,1)S(1)} %shard_map.108), channel_id=1, replica_groups=mesh['z'=8,'yh'=2,'x'=4,'c'=2,'yl'=2] {'yh','x','yl'}, dimensions={0} | all-to-all | bytes 1048576 | tf_op jit(solution)/shard_map/all_to_all | solution.py:560
  74.6 12.6 %all_to_all.27.parts = bf16[8,64,256]{2,1,0:T(8,128)(2,1)S(1)} all-to-all(bf16[8,64,256]{2,1,0:T(8,128)(2,1)S(1)} %shard_map.109), channel_id=1, replica_groups=mesh['z'=8,'yh'=2,'x'=4,'c'=2,'yl'=2] {'z'}, dimensions={0} | all-to-all | bytes 524288 | tf_op jit(solution)/shard_map/all_to_all | solution.py:560
  87.1 1.1 shard_map.110
  88.5 4.3 %all-to-all-start.4 = ((bf16[16,56,128]{2,1,0:T(8,128)(2,1)}), bf16[16,56,128]{2,1,0:T(8,128)(2,1)S(1)}, u32[]{:S(2)}, u32[]{:S(2)}) async-start(bf16[16,56,128]{2,1,0:T(8,128)(2,1)} %get-tuple-element.40), calls=%async_computation.4 | async-start | bytes 458752 | tf_op jit(solution)/shard_map/all_to_all | solution.py:560
  92.9 3.0 %shard_map.111 = bf16[8,16,2,16,128]{4,3,2,1,0:T(8,128)(2,1)} custom-call(f32[4,16,16,128]{3,2,1,0:T(8,128)S(1)} %get-tuple-element.29.pre, bf16[4,16,16,128]{3,2,1,0:T(8,128)(2,1)S(1)} %copy-done.2, f32[5,128]{1,0:T(8,128)S(1)} %pad_maximum_fusion.2.par, f32[2,128]{1,0:T(2,128)S(1)} %get-tuple-element.41.grads, ...), custom_call_target="tpu_custom_call" | custom-call | flops 2400000000 | bytes 2670080 | tf_op jit(solution)/shard_map/pallas_call | solution.py:21
  95.8 4.2 %all-to-all-done.4 = bf16[16,56,128]{2,1,0:T(8,128)(2,1)S(1)} async-done(((bf16[16,56,128]{2,1,0:T(8,128)(2,1)}), bf16[16,56,128]{2,1,0:T(8,128)(2,1)S(1)}, u32[]{:S(2)}, u32[]{:S(2)}) %all-to-all-start.4) | async-done | bytes 229408 | tf_op jit(solution)/shard_map/all_to_all | solution.py:560
  100.0 4.7 %collective-permute-start.7 = (bf16[16,56,128]{2,1,0:T(8,128)(2,1)S(1)}, bf16[16,56,128]{2,1,0:T(8,128)(2,1)S(1)}, u32[]{:S(2)}, u32[]{:S(2)}) collective-permute-start(bf16[16,56,128]{2,1,0:T(8,128)(2,1)S(1)} %all-to-all-done.4), channel_id=1, source_target_pairs={{0,2},{2,0},{1,3},{3,1},{4,6},{6,4},{5,7},{7,5},{8,10},{10,8},{9,1... | collective-permute-start | bytes 688136 | tf_op jit(solution)/shard_map/ppermute | solution.py:546
  104.7 1.1 %collective-permute-done.7 = bf16[16,56,128]{2,1,0:T(8,128)(2,1)S(1)} collective-permute-done((bf16[16,56,128]{2,1,0:T(8,128)(2,1)S(1)}, bf16[16,56,128]{2,1,0:T(8,128)(2,1)S(1)}, u32[]{:S(2)}, u32[]{:S(2)}) %collective-permute-start.7) | collective-permute-done | bytes 229408 | tf_op jit(solution)/shard_map/ppermute | solution.py:546
  106.0 1.0 convert.1
  (45 shorter events, 4.1 us)
Async XLA Ops:
  0.6 5.7 %copy-start.1 = (s32[8,32,32]{2,1,0:T(8,128)S(1)}, s32[8,32,32]{2,1,0:T(8,128)}, u32[]{:S(2)}) copy-start(s32[8,32,32]{2,1,0:T(8,128)} %active.5) | copy-start | bytes 98308
  0.6 5.7 %copy-start = (bf16[8,32,16,128]{3,2,1,0:T(8,128)(2,1)S(1)}, bf16[8,32,16,128]{3,2,1,0:T(8,128)(2,1)}, u32[]{:S(2)}) copy-start(bf16[8,32,16,128]{3,2,1,0:T(8,128)(2,1)} %feat.3) | copy-start | bytes 3145732
  2.5 12.7 %collective-permute-start = (bf16[2,17,16,128]{3,2,1,0:T(8,128)(2,1)}, bf16[2,17,16,128]{3,2,1,0:T(8,128)(2,1)S(1)}, u32[]{:S(2)}, u32[]{:S(2)}) collective-permute-start(bf16[2,17,16,128]{3,2,1,0:T(8,128)(2,1)} %shard_map.102), channel_id=1, source_target_pairs={{0,16},{16,32},{32,48},{48,64},{64,80},{80,96},{96,112},{112,128},... | collective-permute-start | bytes 417800 | tf_op jit(solution)/shard_map/ppermute | solution.py:546
  6.4 0.7 copy-start.3
  6.4 0.7 copy-start.4
  8.8 13.3 %copy-start.5 = (bf16[3,3,3,64,128]{4,3,2,1,0:T(8,128)(2,1)S(1)}, bf16[3,3,3,64,128]{4,3,2,1,0:T(8,128)(2,1)}, u32[]{:S(2)}) copy-start(bf16[3,3,3,64,128]{4,3,2,1,0:T(8,128)(2,1)} %weight.3) | copy-start | bytes 1327108
  15.4 3.4 %collective-permute-start.1 = (bf16[10,16,128]{2,1,0:T(8,128)(2,1)S(1)}, bf16[10,16,128]{2,1,0:T(8,128)(2,1)S(1)}, u32[]{:S(2)}, u32[]{:S(2)}) collective-permute-start(bf16[10,16,128]{2,1,0:T(8,128)(2,1)S(1)} %maximum_multiply_fusion.1), channel_id=1, source_target_pairs={{0,2},{2,4},{4,6},{6,8},{8,10},{10,12},{12,14},{14,0},{1,3},{3,5},... | collective-permute-start | bytes 122888 | tf_op jit(solution)/shard_map/ppermute | solution.py:546
  18.8 3.3 %collective-permute-start.2 = (bf16[19,16,128]{2,1,0:T(8,128)(2,1)S(1)}, bf16[19,16,128]{2,1,0:T(8,128)(2,1)S(1)}, u32[]{:S(2)}, u32[]{:S(2)}) collective-permute-start(bf16[19,16,128]{2,1,0:T(8,128)(2,1)S(1)} %maximum_multiply_fusion), channel_id=1, source_target_pairs={{0,1},{1,0},{2,3},{3,2},{4,5},{5,4},{6,7},{7,6},{8,9},{9,8},{10,11... | collective-permute-start | bytes 233480 | tf_op jit(solution)/shard_map/ppermute | solution.py:546
  22.1 1.3 %copy-start.2 = (bf16[4,16,16,128]{3,2,1,0:T(8,128)(2,1)S(1)}, bf16[4,16,16,128]{3,2,1,0:T(8,128)(2,1)}, u32[]{:S(2)}) copy-start(bf16[4,16,16,128]{3,2,1,0:T(8,128)(2,1)} %cot.5) | copy-start | bytes 786436
  23.5 19.2 %collective-permute-start.3 = (bf16[3,17,16,128]{3,2,1,0:T(8,128)(2,1)S(1)}, bf16[3,17,16,128]{3,2,1,0:T(8,128)(2,1)S(1)}, u32[]{:S(2)}, u32[]{:S(2)}) collective-permute-start(bf16[3,17,16,128]{3,2,1,0:T(8,128)(2,1)S(1)} %get-tuple-element.31), channel_id=1, source_target_pairs={{0,240},{16,0},{32,16},{48,32},{64,48},{80,64},{96,80},{112,96},{1... | collective-permute-start | bytes 626696 | tf_op jit(solution)/shard_map/ppermute | solution.py:546
  43.3 10.2 %all-to-all-start.1 = ((f32[8,3,128]{2,1,0:T(4,128)}), f32[8,3,128]{2,1,0:T(4,128)S(1)}, u32[]{:S(2)}, u32[]{:S(2)}) async-start(f32[8,3,128]{2,1,0:T(4,128)} %get-tuple-element.34), calls=%async_computation.1 | async-start | bytes 32768 | tf_op jit(solution)/shard_map/all_to_all | solution.py:560
  46.9 6.7 %collective-permute-start.4 = (bf16[3,6,16,128]{3,2,1,0:T(8,128)(2,1)S(1)}, bf16[3,6,16,128]{3,2,1,0:T(8,128)(2,1)S(1)}, u32[]{:S(2)}, u32[]{:S(2)}) collective-permute-start(bf16[3,6,16,128]{3,2,1,0:T(8,128)(2,1)S(1)} %get-tuple-element.36), channel_id=1, source_target_pairs={{0,14},{2,0},{4,2},{6,4},{8,6},{10,8},{12,10},{14,12},{1,15},{3,1}... | collective-permute-start | bytes 221192 | tf_op jit(solution)/shard_map/ppermute | solution.py:546
  56.7 3.5 %collective-permute-start.5 = (bf16[16,64,256]{2,1,0:T(8,128)(2,1)S(1)}, bf16[16,64,256]{2,1,0:T(8,128)(2,1)S(1)}, u32[]{:S(2)}, u32[]{:S(2)}) collective-permute-start(bf16[16,64,256]{2,1,0:T(8,128)(2,1)S(1)} %get-tuple-element.39), channel_id=1, source_target_pairs={{0,2},{2,0},{1,3},{3,1},{4,6},{6,4},{5,7},{7,5},{8,10},{10,8},{9,1... | collective-permute-start | bytes 1572872 | tf_op jit(solution)/shard_map/ppermute | solution.py:546
  88.2 4.6 %collective-permute-start.6 = (bf16[3,6,16,128]{3,2,1,0:T(8,128)(2,1)S(1)}, bf16[3,6,16,128]{3,2,1,0:T(8,128)(2,1)S(1)}, u32[]{:S(2)}, u32[]{:S(2)}) collective-permute-start(bf16[3,6,16,128]{3,2,1,0:T(8,128)(2,1)S(1)} %get-tuple-element.42), channel_id=1, source_target_pairs={{0,1},{1,0},{2,3},{3,2},{4,5},{5,4},{6,7},{7,6},{8,9},{9,8},{10,11... | collective-permute-start | bytes 221192 | tf_op jit(solution)/shard_map/ppermute | solution.py:546
  88.5 11.6 %all-to-all-start.4 = ((bf16[16,56,128]{2,1,0:T(8,128)(2,1)}), bf16[16,56,128]{2,1,0:T(8,128)(2,1)S(1)}, u32[]{:S(2)}, u32[]{:S(2)}) async-start(bf16[16,56,128]{2,1,0:T(8,128)(2,1)} %get-tuple-element.40), calls=%async_computation.4 | async-start | bytes 458752 | tf_op jit(solution)/shard_map/all_to_all | solution.py:560
  100.0 5.8 %collective-permute-start.7 = (bf16[16,56,128]{2,1,0:T(8,128)(2,1)S(1)}, bf16[16,56,128]{2,1,0:T(8,128)(2,1)S(1)}, u32[]{:S(2)}, u32[]{:S(2)}) collective-permute-start(bf16[16,56,128]{2,1,0:T(8,128)(2,1)S(1)} %all-to-all-done.4), channel_id=1, source_target_pairs={{0,2},{2,0},{1,3},{3,1},{4,6},{6,4},{5,7},{7,5},{8,10},{10,8},{9,1... | collective-permute-start | bytes 688136 | tf_op jit(solution)/shard_map/ppermute | solution.py:546

commit v9 on v8

--- a/solution.py
+++ b/solution.py
@@ -189,11 +189,14 @@
     out[...] = jnp.concatenate([count, total, square] + [jnp.zeros_like(count)] * 5, axis=0)
 
 
-def pack_kernel(stats, xd, yface, zface, out, yplane):
+def spread_kernel(stats, _, out):
+    for i in range(out.shape[0]):
+        out[i] = stats[:3]
+
+
+def pack_y(xd, yface, zface, yplane):
     mx = yface.shape[1]
     my = zface.shape[2]
-    for i in range(out.shape[0]):
-        out[i] = stats[:3]
     depth = yplane.shape[2]
     yplane[:, :mx] = yface[...]
     yplane[:, mx] = xd[:, 0]
@@ -335,7 +338,7 @@
 
 
 def slope_kernel(
-    pre, cot, par, xin, xh, yh, zh, _, out, keep, send, slope, acc, big
+    pre, cot, par, xin, xh, yh, zh, out, keep, send, slope, acc, big
 ):
     mx, my, mz, cout = pre.shape
     width = xin.shape[4]
@@ -448,7 +451,8 @@
         write_chunk(out, i, jnp.concatenate([slopes, hats], axis=1), columns, common)
 
 
-def near_kernel(parts, out):
+def near_kernel(parts, xd, yface, zface, out, yplane):
+    pack_y(xd, yface, zface, yplane)
     slopes, hats, column, first, second, alpha, beta, high = read_chunks(parts)
     rows = slopes.shape[0]
     cout = slopes.shape[1]
@@ -626,12 +630,7 @@
     )
     xd = moved(xface, GX, -1)
     (stats,) = call(merge_kernel, [shape((8, cout), F32)], [exchanged(stats, NEAR)])
-    stats, yplane = call(
-        pack_kernel,
-        [shape((lax.axis_size(FAR), 3, cout), F32), shape((3, mx + 2, mz, cout), BF)],
-        [stats, xd, yface, zface],
-    )
-    yd = moved(yplane, GY, -1)
+    (stats,) = call(spread_kernel, [shape((lax.axis_size(FAR), 3, cout), F32)], [stats, xd])
     stats = merged(exchanged(stats, FAR))
     count = stats[0]
     mean = stats[1] / count
@@ -648,7 +647,7 @@
             shape(chunks, BF),
             shape(chunks, BF),
         ],
-        [pre, cotangent, par, xin, xh, yh, zh, yd],
+        [pre, cotangent, par, xin, xh, yh, zh],
         scratch=[
             pltpu.VMEM(pre.shape, F32),
             pltpu.VMEM((near * rows, 2 * cout), F32),
@@ -658,7 +657,12 @@
     )
     (big,) = call(pair_kernel, [shape(chunks, BF)], [big, moved(send, "c", 1)])
     far = lax.axis_size(FAR)
-    (big,) = call(near_kernel, [shape((far, rows + 8, 2 * cout), BF)], [exchanged(big, PLANE)])
+    big, yplane = call(
+        near_kernel,
+        [shape((far, rows + 8, 2 * cout), BF), shape((3, mx + 2, mz, cout), BF)],
+        [exchanged(big, PLANE), xd, yface, zface],
+    )
+    yd = moved(yplane, GY, -1)
     dw, shift, tilt, grads, zplane = call(
         far_kernel,
         [

time: 107 us -> 107 us (level)
  blocking collectives: 42.3 us -> 39.6 us
  waiting for transfers between devices: 23 us -> 25 us
    all_to_all x3, blocking collectives: 42.3 us -> 39.6 us  [exchanged(): return lax.all_to_all(value, axes, 0, 0)]
    ppermute x8, waiting for transfers between devices: 12.9 us -> 15 us  [moved(): lax.ppermute(value, axes, [(i, (i + by) % count) for i in range(count)])]
  transfers between devices with their start and end apart: 10 -> 10, of which waited for: 7 -> 8; matrix products, arithmetic and copies ran while one was open for 0% -> 0% of each run, Pallas kernels for 4% -> 4%
where the time goes in v9:
time: 107 us
  blocking collectives  39.6 us (37%)
  starting transfers between devices  25.6 us (24%)
  waiting for transfers between devices  25 us (23%)
  Pallas kernels  13.7 us (13%)
  other arithmetic  1.26 us (1%)
    all_to_all x3, blocking collectives, exchanged(): return lax.all_to_all(value, axes, 0, 0)  39.6 us
    ppermute x8, starting transfers between devices, moved(): lax.ppermute(value, axes, [(i, (i + by) % count) for i in range(count)])  18.1 us
    ppermute x8, waiting for transfers between devices, moved(): lax.ppermute(value, axes, [(i, (i + by) % count) for i in range(count)])  15 us
    pallas_call x10, Pallas kernels, call(): pl.pallas_call(kernel, out_shape=outs, in_specs=[pl.BlockSpec(memory_spac...  11.8 us
    all_to_all x2, waiting for transfers between devices, exchanged(): return lax.all_to_all(value, axes, 0, 0)  10 us
    all_to_all x2, starting transfers between devices, exchanged(): return lax.all_to_all(value, axes, 0, 0)  7.44 us
  transfers between devices with their start and end apart: 10, of which 8 were waited for; matrix products, arithmetic and copies ran while one was open for 0% of the time, Pallas kernels for 4%

profile of v9, /device:TPU:1, one launch (start us, length us, event | category | flops | bytes accessed | tf_op | source)
XLA Modules:
  0.0 106.8 jit_solution(16106889949846868825)
XLA Ops:
  0.7 1.9 %shard_map.102 = bf16[2,17,16,128]{3,2,1,0:T(8,128)(2,1)} custom-call(bf16[8,32,16,128]{3,2,1,0:T(8,128)(2,1)} %feat.3, s32[8,32,32]{2,1,0:T(8,128)} %active.5), custom_call_target="tpu_custom_call" | custom-call | flops 10000000 | bytes 400000 | tf_op jit(solution)/shard_map/pallas_call | solution.py:582
  2.5 3.8 %collective-permute-start = (bf16[2,17,16,128]{3,2,1,0:T(8,128)(2,1)}, bf16[2,17,16,128]{3,2,1,0:T(8,128)(2,1)S(1)}, u32[]{:S(2)}, u32[]{:S(2)}) collective-permute-start(bf16[2,17,16,128]{3,2,1,0:T(8,128)(2,1)} %shard_map.102), channel_id=1, source_target_pairs={{0,16},{16,32},{32,48},{48,64},{64,80},{80,96},{96,112},{112,128},... | collective-permute-start | bytes 417800 | tf_op jit(solution)/shard_map/ppermute | solution.py:550
  7.0 1.8 %shard_map.101 = (bf16[8,2,16,16,128]{4,3,2,1,0:T(8,128)(2,1)S(1)}, bf16[4,16,16,128]{3,2,1,0:T(8,128)(2,1)S(1)}, bf16[8,2,16,128]{3,2,1,0:T(8,128)(2,1)S(1)}, f32[2,128]{1,0:T(2,128)S(1)}) custom-call(bf16[8,32,16,128]{3,2,1,0:T(8,128)(2,1)S(1)} %copy-done, s32[8,32,32]{2,1,0:T(8,128)S(1)} %copy-done.1, f32[1,128]{1,0:T(1,128)S(1)} %bitcast.39, ...), custom_call_target="tpu_custom_call" | custom-call | flops 100000000 | bytes 2459648 | tf_op jit(solution)/shard_map/pallas_call | solution.py:21
  8.9 6.4 %collective-permute-done.xh = bf16[2,17,16,128]{3,2,1,0:T(8,128)(2,1)S(1)} collective-permute-done((bf16[2,17,16,128]{3,2,1,0:T(8,128)(2,1)}, bf16[2,17,16,128]{3,2,1,0:T(8,128)(2,1)S(1)}, u32[]{:S(2)}, u32[]{:S(2)}) %collective-permute-start) | collective-permute-done | bytes 139296 | tf_op jit(solution)/shard_map/ppermute | solution.py:550
  15.4 2.3 %collective-permute-start.1 = (bf16[10,16,128]{2,1,0:T(8,128)(2,1)S(1)}, bf16[10,16,128]{2,1,0:T(8,128)(2,1)S(1)}, u32[]{:S(2)}, u32[]{:S(2)}) collective-permute-start(bf16[10,16,128]{2,1,0:T(8,128)(2,1)S(1)} %maximum_multiply_fusion.1), channel_id=1, source_target_pairs={{0,2},{2,4},{4,6},{6,8},{8,10},{10,12},{12,14},{14,0},{1,3},{3,5},... | collective-permute-start | bytes 122888 | tf_op jit(solution)/shard_map/ppermute | solution.py:550
  19.3 2.9 %collective-permute-done.2.zh = bf16[19,16,128]{2,1,0:T(8,128)(2,1)S(1)} collective-permute-done((bf16[19,16,128]{2,1,0:T(8,128)(2,1)S(1)}, bf16[19,16,128]{2,1,0:T(8,128)(2,1)S(1)}, u32[]{:S(2)}, u32[]{:S(2)}) %collective-permute-start.2) | collective-permute-done | bytes 77856 | tf_op jit(solution)/shard_map/ppermute | solution.py:550
  22.1 1.3 %shard_map.103 = (f32[4,16,16,128]{3,2,1,0:T(8,128)S(1)}, f32[32,3,128]{2,1,0:T(4,128)S(1)}) custom-call(bf16[8,2,16,16,128]{4,3,2,1,0:T(8,128)(2,1)S(1)} %get-tuple-element.26.xin, bf16[4,16,16,128]{3,2,1,0:T(8,128)(2,1)S(1)} %get-tuple-element.27.act, bf16[2,17,16,128]{3,2,1,0:T(8,128)(2,1)S(1)} %collective-permute-done.xh, ...), custom_call_target="tpu_custom_call" | custom-call | flops 1200000000 | bytes 2584576 | tf_op jit(solution)/shard_map/pallas_call | solution.py:21
  23.5 3.0 %collective-permute-start.3 = (bf16[3,17,16,128]{3,2,1,0:T(8,128)(2,1)S(1)}, bf16[3,17,16,128]{3,2,1,0:T(8,128)(2,1)S(1)}, u32[]{:S(2)}, u32[]{:S(2)}) collective-permute-start(bf16[3,17,16,128]{3,2,1,0:T(8,128)(2,1)S(1)} %get-tuple-element.31), channel_id=1, source_target_pairs={{0,240},{16,0},{32,16},{48,32},{64,48},{80,64},{96,80},{112,96},{1... | collective-permute-start | bytes 626696 | tf_op jit(solution)/shard_map/ppermute | solution.py:550
  26.6 16.1 %all_to_all.25.parts = f32[32,3,128]{2,1,0:T(4,128)S(1)} all-to-all(f32[32,3,128]{2,1,0:T(4,128)S(1)} %get-tuple-element.30), channel_id=1, replica_groups=mesh['z'=8,'yh'=2,'x'=4,'c'=2,'yl'=2] {'c','yh','x','yl'}, dimensions={0} | all-to-all | bytes 98304 | tf_op jit(solution)/shard_map/all_to_all | solution.py:564
  42.7 10.0 %all_to_all.26 = f32[8,3,128]{2,1,0:T(4,128)S(1)} all-to-all(f32[8,3,128]{2,1,0:T(4,128)S(1)} %shard_map.106), channel_id=1, replica_groups=mesh['z'=8,'yh'=2,'x'=4,'c'=2,'yl'=2] {'z'}, dimensions={0} | all-to-all | bytes 24576 | tf_op jit(solution)/shard_map/all_to_all | solution.py:564
  52.8 3.1 %shard_map.107 = (bf16[4,16,16,128]{3,2,1,0:T(8,128)(2,1)}, bf16[16,64,256]{2,1,0:T(8,128)(2,1)S(1)}, bf16[16,64,256]{2,1,0:T(8,128)(2,1)S(1)}) custom-call(f32[4,16,16,128]{3,2,1,0:T(8,128)S(1)} %get-tuple-element.29.pre, bf16[4,16,16,128]{3,2,1,0:T(8,128)(2,1)S(1)} %copy-done.2, f32[5,128]{1,0:T(8,128)S(1)} %pad_maximum_fusion.2.par, ...), custom_call_target="tpu_custom_call" | custom-call | flops 2400000000 | bytes 3406336 | tf_op jit(solution)/shard_map/pallas_call | solution.py:21
  55.9 1.9 %collective-permute-start.4 = (bf16[16,64,256]{2,1,0:T(8,128)(2,1)S(1)}, bf16[16,64,256]{2,1,0:T(8,128)(2,1)S(1)}, u32[]{:S(2)}, u32[]{:S(2)}) collective-permute-start(bf16[16,64,256]{2,1,0:T(8,128)(2,1)S(1)} %get-tuple-element.35), channel_id=1, source_target_pairs={{0,2},{2,0},{1,3},{3,1},{4,6},{6,4},{5,7},{7,5},{8,10},{10,8},{9,1... | collective-permute-start | bytes 1572872 | tf_op jit(solution)/shard_map/ppermute | solution.py:550
  57.8 1.5 %collective-permute-done.4.other = bf16[16,64,256]{2,1,0:T(8,128)(2,1)S(1)} collective-permute-done((bf16[16,64,256]{2,1,0:T(8,128)(2,1)S(1)}, bf16[16,64,256]{2,1,0:T(8,128)(2,1)S(1)}, u32[]{:S(2)}, u32[]{:S(2)}) %collective-permute-start.4) | collective-permute-done | bytes 524320 | tf_op jit(solution)/shard_map/ppermute | solution.py:550
  59.7 13.6 %all_to_all.27.parts = bf16[16,64,256]{2,1,0:T(8,128)(2,1)S(1)} all-to-all(bf16[16,64,256]{2,1,0:T(8,128)(2,1)S(1)} %shard_map.108), channel_id=1, replica_groups=mesh['z'=8,'yh'=2,'x'=4,'c'=2,'yl'=2] {'yh','x','yl'}, dimensions={0} | all-to-all | bytes 1048576 | tf_op jit(solution)/shard_map/all_to_all | solution.py:564
  73.3 1.1 %shard_map.109 = (bf16[8,64,256]{2,1,0:T(8,128)(2,1)}, bf16[3,6,16,128]{3,2,1,0:T(8,128)(2,1)S(1)}) custom-call(bf16[16,64,256]{2,1,0:T(8,128)(2,1)S(1)} %all_to_all.27.parts, bf16[3,17,16,128]{3,2,1,0:T(8,128)(2,1)S(1)} %collective-permute-done.3._.xd, bf16[3,4,16,128]{3,2,1,0:T(8,128)(2,1)S(1)} %get-tuple-element.36.yface, ...), custom_call_target="tpu_custom_call" | custom-call | flops 100000000 | bytes 1167360 | tf_op jit(solution)/shard_map/pallas_call | solution.py:21
  74.4 3.4 %all-to-all-start.3 = ((bf16[8,64,256]{2,1,0:T(8,128)(2,1)}), bf16[8,64,256]{2,1,0:T(8,128)(2,1)S(1)}, u32[]{:S(2)}, u32[]{:S(2)}) async-start(bf16[8,64,256]{2,1,0:T(8,128)(2,1)} %get-tuple-element.38), calls=%async_computation.3 | async-start | bytes 524288 | tf_op jit(solution)/shard_map/all_to_all | solution.py:564
  77.9 1.7 %collective-permute-start.5 = (bf16[3,6,16,128]{3,2,1,0:T(8,128)(2,1)S(1)}, bf16[3,6,16,128]{3,2,1,0:T(8,128)(2,1)S(1)}, u32[]{:S(2)}, u32[]{:S(2)}) collective-permute-start(bf16[3,6,16,128]{3,2,1,0:T(8,128)(2,1)S(1)} %get-tuple-element.39), channel_id=1, source_target_pairs={{0,14},{2,0},{4,2},{6,4},{8,6},{10,8},{12,10},{14,12},{1,15},{3,1}... | collective-permute-start | bytes 221192 | tf_op jit(solution)/shard_map/ppermute | solution.py:550
  79.6 2.0 %collective-permute-done.5.yd = bf16[3,6,16,128]{3,2,1,0:T(8,128)(2,1)S(1)} collective-permute-done((bf16[3,6,16,128]{3,2,1,0:T(8,128)(2,1)S(1)}, bf16[3,6,16,128]{3,2,1,0:T(8,128)(2,1)S(1)}, u32[]{:S(2)}, u32[]{:S(2)}) %collective-permute-start.5) | collective-permute-done | bytes 73760 | tf_op jit(solution)/shard_map/ppermute | solution.py:550
  81.6 5.8 %all-to-all-done.3.parts = bf16[8,64,256]{2,1,0:T(8,128)(2,1)S(1)} async-done(((bf16[8,64,256]{2,1,0:T(8,128)(2,1)}), bf16[8,64,256]{2,1,0:T(8,128)(2,1)S(1)}, u32[]{:S(2)}, u32[]{:S(2)}) %all-to-all-start.3) | async-done | bytes 262176 | tf_op jit(solution)/shard_map/all_to_all | solution.py:564
  88.7 4.0 %all-to-all-start.4 = ((bf16[16,56,128]{2,1,0:T(8,128)(2,1)}), bf16[16,56,128]{2,1,0:T(8,128)(2,1)S(1)}, u32[]{:S(2)}, u32[]{:S(2)}) async-start(bf16[16,56,128]{2,1,0:T(8,128)(2,1)} %get-tuple-element.40), calls=%async_computation.4 | async-start | bytes 458752 | tf_op jit(solution)/shard_map/all_to_all | solution.py:564
  92.7 3.0 %shard_map.111 = bf16[8,16,2,16,128]{4,3,2,1,0:T(8,128)(2,1)} custom-call(f32[4,16,16,128]{3,2,1,0:T(8,128)S(1)} %get-tuple-element.29.pre, bf16[4,16,16,128]{3,2,1,0:T(8,128)(2,1)S(1)} %copy-done.2, f32[5,128]{1,0:T(8,128)S(1)} %pad_maximum_fusion.2.par, f32[2,128]{1,0:T(2,128)S(1)} %get-tuple-element.41.grads, ...), custom_call_target="tpu_custom_call" | custom-call | flops 2400000000 | bytes 2670080 | tf_op jit(solution)/shard_map/pallas_call | solution.py:21
  95.7 4.2 %all-to-all-done.4 = bf16[16,56,128]{2,1,0:T(8,128)(2,1)S(1)} async-done(((bf16[16,56,128]{2,1,0:T(8,128)(2,1)}), bf16[16,56,128]{2,1,0:T(8,128)(2,1)S(1)}, u32[]{:S(2)}, u32[]{:S(2)}) %all-to-all-start.4) | async-done | bytes 229408 | tf_op jit(solution)/shard_map/all_to_all | solution.py:564
  99.9 4.6 %collective-permute-start.7 = (bf16[16,56,128]{2,1,0:T(8,128)(2,1)S(1)}, bf16[16,56,128]{2,1,0:T(8,128)(2,1)S(1)}, u32[]{:S(2)}, u32[]{:S(2)}) collective-permute-start(bf16[16,56,128]{2,1,0:T(8,128)(2,1)S(1)} %all-to-all-done.4), channel_id=1, source_target_pairs={{0,2},{2,0},{1,3},{3,1},{4,6},{6,4},{5,7},{7,5},{8,10},{10,8},{9,1... | collective-permute-start | bytes 688136 | tf_op jit(solution)/shard_map/ppermute | solution.py:550
  104.6 1.1 %collective-permute-done.7 = bf16[16,56,128]{2,1,0:T(8,128)(2,1)S(1)} collective-permute-done((bf16[16,56,128]{2,1,0:T(8,128)(2,1)S(1)}, bf16[16,56,128]{2,1,0:T(8,128)(2,1)S(1)}, u32[]{:S(2)}, u32[]{:S(2)}) %collective-permute-start.7) | collective-permute-done | bytes 229408 | tf_op jit(solution)/shard_map/ppermute | solution.py:550
  (45 shorter events, 5.3 us)
Async XLA Ops:
  0.6 5.7 %copy-start.1 = (s32[8,32,32]{2,1,0:T(8,128)S(1)}, s32[8,32,32]{2,1,0:T(8,128)}, u32[]{:S(2)}) copy-start(s32[8,32,32]{2,1,0:T(8,128)} %active.5) | copy-start | bytes 98308
  0.6 5.7 %copy-start = (bf16[8,32,16,128]{3,2,1,0:T(8,128)(2,1)S(1)}, bf16[8,32,16,128]{3,2,1,0:T(8,128)(2,1)}, u32[]{:S(2)}) copy-start(bf16[8,32,16,128]{3,2,1,0:T(8,128)(2,1)} %feat.3) | copy-start | bytes 3145732
  2.5 12.7 %collective-permute-start = (bf16[2,17,16,128]{3,2,1,0:T(8,128)(2,1)}, bf16[2,17,16,128]{3,2,1,0:T(8,128)(2,1)S(1)}, u32[]{:S(2)}, u32[]{:S(2)}) collective-permute-start(bf16[2,17,16,128]{3,2,1,0:T(8,128)(2,1)} %shard_map.102), channel_id=1, source_target_pairs={{0,16},{16,32},{32,48},{48,64},{64,80},{80,96},{96,112},{112,128},... | collective-permute-start | bytes 417800 | tf_op jit(solution)/shard_map/ppermute | solution.py:550
  6.4 0.7 copy-start.3
  6.4 0.7 copy-start.4
  8.8 13.3 %copy-start.5 = (bf16[3,3,3,64,128]{4,3,2,1,0:T(8,128)(2,1)S(1)}, bf16[3,3,3,64,128]{4,3,2,1,0:T(8,128)(2,1)}, u32[]{:S(2)}) copy-start(bf16[3,3,3,64,128]{4,3,2,1,0:T(8,128)(2,1)} %weight.3) | copy-start | bytes 1327108
  15.4 3.4 %collective-permute-start.1 = (bf16[10,16,128]{2,1,0:T(8,128)(2,1)S(1)}, bf16[10,16,128]{2,1,0:T(8,128)(2,1)S(1)}, u32[]{:S(2)}, u32[]{:S(2)}) collective-permute-start(bf16[10,16,128]{2,1,0:T(8,128)(2,1)S(1)} %maximum_multiply_fusion.1), channel_id=1, source_target_pairs={{0,2},{2,4},{4,6},{6,8},{8,10},{10,12},{12,14},{14,0},{1,3},{3,5},... | collective-permute-start | bytes 122888 | tf_op jit(solution)/shard_map/ppermute | solution.py:550
  18.8 3.3 %collective-permute-start.2 = (bf16[19,16,128]{2,1,0:T(8,128)(2,1)S(1)}, bf16[19,16,128]{2,1,0:T(8,128)(2,1)S(1)}, u32[]{:S(2)}, u32[]{:S(2)}) collective-permute-start(bf16[19,16,128]{2,1,0:T(8,128)(2,1)S(1)} %maximum_multiply_fusion), channel_id=1, source_target_pairs={{0,1},{1,0},{2,3},{3,2},{4,5},{5,4},{6,7},{7,6},{8,9},{9,8},{10,11... | collective-permute-start | bytes 233480 | tf_op jit(solution)/shard_map/ppermute | solution.py:550
  22.1 1.3 %copy-start.2 = (bf16[4,16,16,128]{3,2,1,0:T(8,128)(2,1)S(1)}, bf16[4,16,16,128]{3,2,1,0:T(8,128)(2,1)}, u32[]{:S(2)}) copy-start(bf16[4,16,16,128]{3,2,1,0:T(8,128)(2,1)} %cot.5) | copy-start | bytes 786436
  23.5 19.2 %collective-permute-start.3 = (bf16[3,17,16,128]{3,2,1,0:T(8,128)(2,1)S(1)}, bf16[3,17,16,128]{3,2,1,0:T(8,128)(2,1)S(1)}, u32[]{:S(2)}, u32[]{:S(2)}) collective-permute-start(bf16[3,17,16,128]{3,2,1,0:T(8,128)(2,1)S(1)} %get-tuple-element.31), channel_id=1, source_target_pairs={{0,240},{16,0},{32,16},{48,32},{64,48},{80,64},{96,80},{112,96},{1... | collective-permute-start | bytes 626696 | tf_op jit(solution)/shard_map/ppermute | solution.py:550
  55.9 3.5 %collective-permute-start.4 = (bf16[16,64,256]{2,1,0:T(8,128)(2,1)S(1)}, bf16[16,64,256]{2,1,0:T(8,128)(2,1)S(1)}, u32[]{:S(2)}, u32[]{:S(2)}) collective-permute-start(bf16[16,64,256]{2,1,0:T(8,128)(2,1)S(1)} %get-tuple-element.35), channel_id=1, source_target_pairs={{0,2},{2,0},{1,3},{3,1},{4,6},{6,4},{5,7},{7,5},{8,10},{10,8},{9,1... | collective-permute-start | bytes 1572872 | tf_op jit(solution)/shard_map/ppermute | solution.py:550
  74.4 13.0 %all-to-all-start.3 = ((bf16[8,64,256]{2,1,0:T(8,128)(2,1)}), bf16[8,64,256]{2,1,0:T(8,128)(2,1)S(1)}, u32[]{:S(2)}, u32[]{:S(2)}) async-start(bf16[8,64,256]{2,1,0:T(8,128)(2,1)} %get-tuple-element.38), calls=%async_computation.3 | async-start | bytes 524288 | tf_op jit(solution)/shard_map/all_to_all | solution.py:564
  77.9 3.8 %collective-permute-start.5 = (bf16[3,6,16,128]{3,2,1,0:T(8,128)(2,1)S(1)}, bf16[3,6,16,128]{3,2,1,0:T(8,128)(2,1)S(1)}, u32[]{:S(2)}, u32[]{:S(2)}) collective-permute-start(bf16[3,6,16,128]{3,2,1,0:T(8,128)(2,1)S(1)} %get-tuple-element.39), channel_id=1, source_target_pairs={{0,14},{2,0},{4,2},{6,4},{8,6},{10,8},{12,10},{14,12},{1,15},{3,1}... | collective-permute-start | bytes 221192 | tf_op jit(solution)/shard_map/ppermute | solution.py:550
  88.5 4.2 %collective-permute-start.6 = (bf16[3,6,16,128]{3,2,1,0:T(8,128)(2,1)S(1)}, bf16[3,6,16,128]{3,2,1,0:T(8,128)(2,1)S(1)}, u32[]{:S(2)}, u32[]{:S(2)}) collective-permute-start(bf16[3,6,16,128]{3,2,1,0:T(8,128)(2,1)S(1)} %get-tuple-element.42), channel_id=1, source_target_pairs={{0,1},{1,0},{2,3},{3,2},{4,5},{5,4},{6,7},{7,6},{8,9},{9,8},{10,11... | collective-permute-start | bytes 221192 | tf_op jit(solution)/shard_map/ppermute | solution.py:550
  88.7 11.2 %all-to-all-start.4 = ((bf16[16,56,128]{2,1,0:T(8,128)(2,1)}), bf16[16,56,128]{2,1,0:T(8,128)(2,1)S(1)}, u32[]{:S(2)}, u32[]{:S(2)}) async-start(bf16[16,56,128]{2,1,0:T(8,128)(2,1)} %get-tuple-element.40), calls=%async_computation.4 | async-start | bytes 458752 | tf_op jit(solution)/shard_map/all_to_all | solution.py:564
  99.9 5.7 %collective-permute-start.7 = (bf16[16,56,128]{2,1,0:T(8,128)(2,1)S(1)}, bf16[16,56,128]{2,1,0:T(8,128)(2,1)S(1)}, u32[]{:S(2)}, u32[]{:S(2)}) collective-permute-start(bf16[16,56,128]{2,1,0:T(8,128)(2,1)S(1)} %all-to-all-done.4), channel_id=1, source_target_pairs={{0,2},{2,0},{1,3},{3,1},{4,6},{6,4},{5,7},{7,5},{8,10},{10,8},{9,1... | collective-permute-start | bytes 688136 | tf_op jit(solution)/shard_map/ppermute | solution.py:550
